TPU v7x, 32 devices: a whole 2x2x4 slice. The times are simulated.
32 devices in a mesh: groups: 1, row: 16 (over z, y, core), col: 2 (over x).
Axes of the slice: x: 2, y: 2, z: 4, core: 2. Of those that a mesh axis runs over, the one named last changes fastest.
Arguments:
- alignment_embedding: bfloat16 [32, 768, 256], P('groups', ('row', 'col')), may hold values from -6 to 6
- normalizer_factor: float32 [256], replicated, may hold values from 0.1 to 1.9
- normalizer_shift: float32 [256], replicated, may hold values from -3 to 3
- first_factor_matrix: bfloat16 [256, 32], replicated, may hold values from -0.375 to 0.375
- first_factor_shift: float32 [32], replicated, may hold values from -3 to 3
- second_factor_matrix: bfloat16 [256, 32], replicated, may hold values from -0.375 to 0.375
- second_factor_shift: float32 [32], replicated, may hold values from -3 to 3
- final_matrix: bfloat16 [1024, 128], replicated, may hold values from -1 to 1
- final_shift: float32 [128], replicated, may hold values from -3 to 3
Outputs:
- pair_update: bfloat16 [768, 768, 128], P(('groups', 'row'), 'col')
All inputs are finite; a program needn't handle non-finite values.
Results may differ from a plain program's by a relative error of at most 0.0056.
Values may be sent and summed in bfloat16 or wider, within the bound.
No kernel may reach another device: no remote copies, remote signals or barrier semaphores. Data moves between devices by JAX's collectives and lax.ppermute only.
A program may use at most 64 MiB of HBM per device.

v0:
```python
import math

import jax
import jax.numpy as jnp
from jax import lax
from jax.sharding import PartitionSpec as P


def per_device(
    alignment_embedding,
    normalizer_factor,
    normalizer_shift,
    first_factor_matrix,
    first_factor_shift,
    second_factor_matrix,
    second_factor_shift,
    final_matrix,
    final_shift,
):
    element_numbers = alignment_embedding.astype(jnp.float32)
    average = jnp.mean(element_numbers, axis=-1, keepdims=True)
    centered = element_numbers - average
    variance = jnp.mean(centered * centered, axis=-1, keepdims=True)
    normed = (centered * lax.rsqrt(variance + 1e-05) * normalizer_factor + normalizer_shift).astype(
        jnp.bfloat16
    )
    left_proj = (
        jnp.einsum("src,ck->srk", normed, first_factor_matrix, preferred_element_type=jnp.float32)
        + first_factor_shift
    ).astype(jnp.bfloat16)
    right_proj = (
        jnp.einsum("src,ck->srk", normed, second_factor_matrix, preferred_element_type=jnp.float32)
        + second_factor_shift
    ).astype(jnp.bfloat16)
    col_count = lax.axis_size("col")
    res_total = left_proj.shape[1] * col_count * lax.axis_size("row")
    span = res_total // col_count
    left_rows, right_rows = (
        lax.all_gather(left_proj, "col", axis=1, tiled=True),
        lax.all_gather(right_proj, "col", axis=1, tiled=True),
    )
    right_every = lax.all_gather(right_rows, "row", axis=1, tiled=True)
    right_cols = lax.dynamic_slice_in_dim(right_every, lax.axis_index("col") * span, span, 1)
    seq_count, row_count, width = left_rows.shape
    row_step = math.gcd(row_count, 8)
    right_flat = right_cols.transpose(0, 2, 1).reshape(seq_count, width * span)
    left_blocks = left_rows.reshape(seq_count, row_count // row_step, row_step, width).transpose(
        1, 3, 2, 0
    )
    final_trans = final_matrix.T
    shift_column = final_shift[:, None]

    def one_block(left_block):
        left_flat = left_block.reshape(width * row_step, seq_count)
        outer = jnp.dot(left_flat, right_flat, preferred_element_type=jnp.float32) / seq_count
        outer = outer.astype(jnp.bfloat16).reshape(width, row_step, width, span)
        outer = outer.transpose(0, 2, 1, 3).reshape(width * width, row_step * span)
        update = jnp.dot(final_trans, outer, preferred_element_type=jnp.float32) + shift_column
        return update.astype(jnp.bfloat16).T.reshape(row_step, span, -1)

    tiles = lax.map(one_block, left_blocks)
    return tiles.reshape(row_count, span, -1)


def solution(mesh):
    return jax.shard_map(
        per_device,
        mesh=mesh,
        in_specs=(P("groups", ("row", "col"), None), P(), P(), P(), P(), P(), P(), P(), P()),
        out_specs=P(("groups", "row"), "col", None),
        check_vma=False,
    )
```

profile of v0, /device:TPU:3, one launch (start us, length us, event | category | flops | bytes accessed | tf_op | source)
XLA Modules:
  0.0 133.0 jit_solution(11079793704884754490)
XLA Ops:
  10.6 6.6 %all_gather.10 = bf16[32,48,32]{2,1,0:T(8,128)(2,1)} all-gather(bf16[32,24,32]{2,1,0:T(8,128)(2,1)S(1)} %fusion.6), channel_id=1, replica_groups=mesh['groups'=1,'row'=16,'col'=2] {'col'}, dimensions={1}, use_global_device_ids=true | all-gather | bytes 147456 | tf_op jit(solution)/shard_map/all_gather | solution.py:40
  18.6 5.5 %all_gather.9 = bf16[32,48,32]{2,1,0:T(8,128)(2,1)S(1)} all-gather(bf16[32,24,32]{2,1,0:T(8,128)(2,1)S(1)} %fusion.5), channel_id=1, replica_groups=mesh['groups'=1,'row'=16,'col'=2] {'col'}, dimensions={1}, use_global_device_ids=true | all-gather | bytes 147456 | tf_op jit(solution)/shard_map/all_gather | solution.py:39
  24.8 56.8 %all-gather.2.cloned.1.call-done = bf16[32,768,32]{2,1,0:T(8,128)(2,1)} async-done(((bf16[32,48,32]{2,1,0:T(8,128)(2,1)}), bf16[32,768,32]{2,1,0:T(8,128)(2,1)}) %all-gather.2.cloned.1.call-update) | async-done | bytes 1572880 | tf_op jit(solution)/shard_map/all_gather | solution.py:42
  81.6 3.9 %dynamic-slice_bitcast_fusion = bf16[32,32,384]{1,2,0:T(8,128)(2,1)} fusion(bf16[32,768,32]{2,1,0:T(8,128)(2,1)} %all-gather.2.cloned.1.call-done, s32[]{:T(128)S(6)} %select_n.3), kind=kLoop, calls=%fused_computation.8 | loop fusion | bytes 1572868 | tf_op jit(solution)/shard_map/transpose | solution.py:46
  85.5 3.2 %copy.16 = bf16[4,8,32,384]{3,1,2,0:T(8,128)(2,1)S(1)} copy(bf16[4,8,32,384]{2,3,1,0:T(8,128)(2,1)} %bitcast.50) | data formatting | bytes 1572864
  88.8 37.4 %while.10 = (s32[]{:T(128)}, bf16[6,8,384,128]{3,2,1,0:T(8,128)(2,1)}, bf16[6,32,8,32]{3,2,1,0:T(8,128)(2,1)S(1)}, bf16[32,12288]{1,0:T(8,128)(2,1)S(1)}, bf16[1...) while((s32[]{:T(128)}, bf16[6,8,384,128]{3,2,1,0:T(8,128)(2,1)}, ...), condition=%wide.region_3.4_spmd, body=%wide.region_2.3_spmd.sunk | while | flops 1013710848 | bytes 28640336 | solution.py:61
  88.8 1.8 %fusion.30 = bf16[256,12288]{1,0:T(8,128)(2,1)S(1)} fusion(bf16[32,12288]{1,0:T(8,128)(2,1)S(1)} %get-tuple-element.104, bf16[6,32,8,32]{3,2,1,0:T(8,128)(2,1)S(1)} %get-tuple-element.103, s32[]{:T(128)} %get-tuple-element.94), kind=kOutput, calls=%fused_computation.1.clone.1 | convolution fusion | flops 207618048 | bytes 7143428 | tf_op jit(solution)/shard_map/while/body/eval_jaxpr/dot_general | solution.py:55
  90.5 1.6 %copy.19 = bf16[128,8,8,384]{3,1,2,0:T(8,128)(2,1)S(1)} copy(bf16[128,8,8,384]{3,2,1,0:T(8,128)(2,1)S(1)} %bitcast.46) | data formatting | bytes 12582912 | tf_op jit(solution)/shard_map/while
  92.2 1.9 %fusion.31 = bf16[3072,128]{1,0:T(8,128)(2,1)S(1)} fusion(bf16[1024,3072]{1,0:T(8,128)(2,1)S(1)} %bitcast.47, bf16[128,1024]{1,0:T(8,128)(2,1)S(1)} %get-tuple-element.105, f32[128]{0:T(128)S(1)} %bitcast.55), kind=kOutput, calls=%fused_computation.3.clone.1 | convolution fusion | flops 806092800 | bytes 7340544 | tf_op jit(solution)/shard_map/while/body/eval_jaxpr/dot_general | solution.py:58
  95.0 1.8 %fusion.30 = bf16[256,12288]{1,0:T(8,128)(2,1)S(1)} fusion(bf16[32,12288]{1,0:T(8,128)(2,1)S(1)} %get-tuple-element.104, bf16[6,32,8,32]{3,2,1,0:T(8,128)(2,1)S(1)} %get-tuple-element.103, s32[]{:T(128)} %get-tuple-element.94), kind=kOutput, calls=%fused_computation.1.clone.1 | convolution fusion | flops 207618048 | bytes 7143428 | tf_op jit(solution)/shard_map/while/body/eval_jaxpr/dot_general | solution.py:55
  96.8 1.6 %copy.19 = bf16[128,8,8,384]{3,1,2,0:T(8,128)(2,1)S(1)} copy(bf16[128,8,8,384]{3,2,1,0:T(8,128)(2,1)S(1)} %bitcast.46) | data formatting | bytes 12582912 | tf_op jit(solution)/shard_map/while
  98.4 1.9 %fusion.31 = bf16[3072,128]{1,0:T(8,128)(2,1)S(1)} fusion(bf16[1024,3072]{1,0:T(8,128)(2,1)S(1)} %bitcast.47, bf16[128,1024]{1,0:T(8,128)(2,1)S(1)} %get-tuple-element.105, f32[128]{0:T(128)S(1)} %bitcast.55), kind=kOutput, calls=%fused_computation.3.clone.1 | convolution fusion | flops 806092800 | bytes 7340544 | tf_op jit(solution)/shard_map/while/body/eval_jaxpr/dot_general | solution.py:58
  101.2 1.8 %fusion.30 = bf16[256,12288]{1,0:T(8,128)(2,1)S(1)} fusion(bf16[32,12288]{1,0:T(8,128)(2,1)S(1)} %get-tuple-element.104, bf16[6,32,8,32]{3,2,1,0:T(8,128)(2,1)S(1)} %get-tuple-element.103, s32[]{:T(128)} %get-tuple-element.94), kind=kOutput, calls=%fused_computation.1.clone.1 | convolution fusion | flops 207618048 | bytes 7143428 | tf_op jit(solution)/shard_map/while/body/eval_jaxpr/dot_general | solution.py:55
  103.0 1.6 %copy.19 = bf16[128,8,8,384]{3,1,2,0:T(8,128)(2,1)S(1)} copy(bf16[128,8,8,384]{3,2,1,0:T(8,128)(2,1)S(1)} %bitcast.46) | data formatting | bytes 12582912 | tf_op jit(solution)/shard_map/while
  104.7 1.9 %fusion.31 = bf16[3072,128]{1,0:T(8,128)(2,1)S(1)} fusion(bf16[1024,3072]{1,0:T(8,128)(2,1)S(1)} %bitcast.47, bf16[128,1024]{1,0:T(8,128)(2,1)S(1)} %get-tuple-element.105, f32[128]{0:T(128)S(1)} %bitcast.55), kind=kOutput, calls=%fused_computation.3.clone.1 | convolution fusion | flops 806092800 | bytes 7340544 | tf_op jit(solution)/shard_map/while/body/eval_jaxpr/dot_general | solution.py:58
  107.5 1.8 %fusion.30 = bf16[256,12288]{1,0:T(8,128)(2,1)S(1)} fusion(bf16[32,12288]{1,0:T(8,128)(2,1)S(1)} %get-tuple-element.104, bf16[6,32,8,32]{3,2,1,0:T(8,128)(2,1)S(1)} %get-tuple-element.103, s32[]{:T(128)} %get-tuple-element.94), kind=kOutput, calls=%fused_computation.1.clone.1 | convolution fusion | flops 207618048 | bytes 7143428 | tf_op jit(solution)/shard_map/while/body/eval_jaxpr/dot_general | solution.py:55
  109.3 1.6 %copy.19 = bf16[128,8,8,384]{3,1,2,0:T(8,128)(2,1)S(1)} copy(bf16[128,8,8,384]{3,2,1,0:T(8,128)(2,1)S(1)} %bitcast.46) | data formatting | bytes 12582912 | tf_op jit(solution)/shard_map/while
  110.9 1.9 %fusion.31 = bf16[3072,128]{1,0:T(8,128)(2,1)S(1)} fusion(bf16[1024,3072]{1,0:T(8,128)(2,1)S(1)} %bitcast.47, bf16[128,1024]{1,0:T(8,128)(2,1)S(1)} %get-tuple-element.105, f32[128]{0:T(128)S(1)} %bitcast.55), kind=kOutput, calls=%fused_computation.3.clone.1 | convolution fusion | flops 806092800 | bytes 7340544 | tf_op jit(solution)/shard_map/while/body/eval_jaxpr/dot_general | solution.py:58
  113.7 1.8 %fusion.30 = bf16[256,12288]{1,0:T(8,128)(2,1)S(1)} fusion(bf16[32,12288]{1,0:T(8,128)(2,1)S(1)} %get-tuple-element.104, bf16[6,32,8,32]{3,2,1,0:T(8,128)(2,1)S(1)} %get-tuple-element.103, s32[]{:T(128)} %get-tuple-element.94), kind=kOutput, calls=%fused_computation.1.clone.1 | convolution fusion | flops 207618048 | bytes 7143428 | tf_op jit(solution)/shard_map/while/body/eval_jaxpr/dot_general | solution.py:55
  115.5 1.6 %copy.19 = bf16[128,8,8,384]{3,1,2,0:T(8,128)(2,1)S(1)} copy(bf16[128,8,8,384]{3,2,1,0:T(8,128)(2,1)S(1)} %bitcast.46) | data formatting | bytes 12582912 | tf_op jit(solution)/shard_map/while
  117.1 1.9 %fusion.31 = bf16[3072,128]{1,0:T(8,128)(2,1)S(1)} fusion(bf16[1024,3072]{1,0:T(8,128)(2,1)S(1)} %bitcast.47, bf16[128,1024]{1,0:T(8,128)(2,1)S(1)} %get-tuple-element.105, f32[128]{0:T(128)S(1)} %bitcast.55), kind=kOutput, calls=%fused_computation.3.clone.1 | convolution fusion | flops 806092800 | bytes 7340544 | tf_op jit(solution)/shard_map/while/body/eval_jaxpr/dot_general | solution.py:58
  120.0 1.8 %fusion.30 = bf16[256,12288]{1,0:T(8,128)(2,1)S(1)} fusion(bf16[32,12288]{1,0:T(8,128)(2,1)S(1)} %get-tuple-element.104, bf16[6,32,8,32]{3,2,1,0:T(8,128)(2,1)S(1)} %get-tuple-element.103, s32[]{:T(128)} %get-tuple-element.94), kind=kOutput, calls=%fused_computation.1.clone.1 | convolution fusion | flops 207618048 | bytes 7143428 | tf_op jit(solution)/shard_map/while/body/eval_jaxpr/dot_general | solution.py:55
  121.7 1.6 %copy.19 = bf16[128,8,8,384]{3,1,2,0:T(8,128)(2,1)S(1)} copy(bf16[128,8,8,384]{3,2,1,0:T(8,128)(2,1)S(1)} %bitcast.46) | data formatting | bytes 12582912 | tf_op jit(solution)/shard_map/while
  123.4 1.9 %fusion.31 = bf16[3072,128]{1,0:T(8,128)(2,1)S(1)} fusion(bf16[1024,3072]{1,0:T(8,128)(2,1)S(1)} %bitcast.47, bf16[128,1024]{1,0:T(8,128)(2,1)S(1)} %get-tuple-element.105, f32[128]{0:T(128)S(1)} %bitcast.55), kind=kOutput, calls=%fused_computation.3.clone.1 | convolution fusion | flops 806092800 | bytes 7340544 | tf_op jit(solution)/shard_map/while/body/eval_jaxpr/dot_general | solution.py:58
  (23 shorter events, 11.7 us)
Async XLA Ops:
  6.5 2.6 %copy-start = (bf16[256,32]{0,1:T(8,128)(2,1)S(1)}, bf16[256,32]{0,1:T(8,128)(2,1)}, u32[]{:S(2)}) copy-start(bf16[256,32]{0,1:T(8,128)(2,1)} %param.16) | copy-start | bytes 49156
  6.5 18.0 %copy-start.1 = (bf16[1024,128]{1,0:T(8,128)(2,1)S(1)}, bf16[1024,128]{1,0:T(8,128)(2,1)}, u32[]{:S(2)}) copy-start(bf16[1024,128]{1,0:T(8,128)(2,1)} %param.18) | copy-start | bytes 786436
  6.5 75.0 %all-gather.2.cloned.1.call-start = ((), (), s32[]{:S(2)}) async-start(), calls=%async_computation | async-start | bytes 6684672 | tf_op jit(solution)/shard_map/all_gather | solution.py:42
  24.7 64.0 %copy-start.2 = (f32[128]{0:T(128)S(1)}, f32[128]{0:T(128)}, u32[]{:S(2)}) copy-start(f32[128]{0:T(128)} %param.19) | copy-start | bytes 1540
Sparse Core Ops, SparseCore 0:
  17.3 64.2 all-gather.1
where the time goes:
time: 134 us; the launch traced here: 133 us
  waiting for transfers between devices  56.9 us (42%)
  matrix products  24.8 us (19%)
  local copies, waits for them, and re-layouts  23.2 us (17%)
  between operations  13.5 us (10%)
  blocking collectives  12.1 us (9%)
  other arithmetic  2.54 us (2%)
    all_gather x1, waiting for transfers between devices, per_device(): right_every = lax.all_gather(right_rows, 'row', axis=1, tiled=True)  56.8 us
    dot_general x6, matrix products, one_block(): jnp.dot(final_trans, outer, preferred_element_type=jnp.float32)  11.2 us
    dot_general x6, matrix products, one_block(): jnp.dot(left_flat, right_flat, preferred_element_type=jnp.float32)  10.7 us
    while x6, local copies, waits for them, and re-layouts  9.81 us
    all_gather x1, blocking collectives, per_device(): lax.all_gather(right_proj, 'col', axis=1, tiled=True)  6.55 us
    dynamic_update_slice x6, local copies, waits for them, and re-layouts, per_device(): tiles = lax.map(one_block, left_blocks)  5.66 us
    all_gather x1, blocking collectives, per_device(): lax.all_gather(left_proj, 'col', axis=1, tiled=True)  5.53 us
    transpose x1, local copies, waits for them, and re-layouts, per_device(): right_flat = right_cols.transpose(0, 2, 1).reshape(seq_count, width * span)  3.92 us
  transfers between devices with their start and end apart: 1, of which 1 were waited for; matrix products, arithmetic and copies ran while one was open for 2% of the time, Pallas kernels for 0%

commit v1 on v0

v1 whole, which is shorter than its diff:
```python
import functools

import jax
import jax.numpy as jnp
from jax import lax
from jax.experimental import pallas as pl
from jax.experimental.pallas import tpu as pltpu
from jax.sharding import PartitionSpec as P

F32, BF16 = jnp.float32, jnp.bfloat16
LANES = 128
RUN = 8


def project_kernel(*refs):
    sources, (r_ref, l_ref, held), buffers, sems = refs[:7], refs[7:10], refs[10:17], refs[17]
    copies = [pltpu.make_async_copy(src, dst, sems.at[k]) for k, (src, dst) in enumerate(zip(sources, buffers))]
    for copy in copies:
        copy.start()
    for copy in copies:
        copy.wait()
    x_ref, gain_ref, shift_ref, left_ref, left_shift_ref, right_ref, right_shift_ref = buffers
    seqs, here, channels = x_ref.shape
    width = left_ref.shape[0]
    groups = LANES // width
    x = x_ref[...].astype(F32).reshape(seqs * here, channels)
    centered = x - jnp.mean(x, axis=-1, keepdims=True)
    variance = jnp.mean(centered * centered, axis=-1, keepdims=True)
    normed = (centered * lax.rsqrt(variance + 1e-05) * gain_ref[...] + shift_ref[...]).astype(BF16)
    matrices = jnp.concatenate([left_ref[...]] * groups + [right_ref[...]] * groups, axis=0)
    shifts = jnp.concatenate([left_shift_ref[...]] * groups + [right_shift_ref[...]] * groups, axis=1)
    both = lax.dot_general(normed, matrices, (((1,), (1,)), ((), ())), preferred_element_type=F32) + shifts
    held[0], held[1] = both[:, :LANES], both[:, LANES:]
    group = lax.broadcasted_iota(jnp.int32, (1, LANES), 1) // width
    per = here // groups
    for i in range(per):
        packed = held[0, pl.ds(i, seqs, stride=here), :]
        for g in range(1, groups):
            packed = jnp.where(group == g, held[0, pl.ds(g * per + i, seqs, stride=here), :], packed)
        l_ref[i * seqs : (i + 1) * seqs, :] = packed.astype(BF16)
    rows = []
    for q in range(seqs // RUN):
        tiles = []
        for t in range(RUN // groups):
            s = q * RUN + t * groups
            packed = held[1, s * here : (s + 1) * here, :]
            for g in range(1, groups):
                packed = jnp.where(group == g, held[1, (s + g) * here : (s + g + 1) * here, :], packed)
            tiles.append(packed)
        rows.append(jnp.concatenate(tiles, axis=1))
    packed = jnp.concatenate(rows, axis=0).astype(BF16)
    span = RUN * width
    a = lax.broadcasted_iota(jnp.int32, (span, span), 0)
    b = lax.broadcasted_iota(jnp.int32, (span, span), 1)
    order = jnp.where((a % width) * RUN + a // width == b, 1.0, 0.0).astype(BF16)
    ordered = jnp.dot(packed, order, preferred_element_type=F32).astype(BF16)
    for q in range(seqs // RUN):
        r_ref[:, q * span : (q + 1) * span] = ordered[q * here : (q + 1) * here, :]


def spread_left(seqs, width, l_ref, pairs, t_ref):
    groups = LANES // width
    residues = l_ref.shape[0] // seqs * groups
    left = jnp.concatenate([l_ref[:, g * width : (g + 1) * width] for g in range(groups)], axis=0)
    unroll = 4

    def step(n, carry):
        for u in range(unroll):
            m = n * unroll + u
            wide_out = jnp.dot(left, pairs[m], preferred_element_type=F32)
            for i in range(residues):
                for q in range(seqs // RUN):
                    s = i * seqs + q * RUN
                    block = jnp.concatenate([wide_out[s : s + RUN, :LANES], wide_out[s : s + RUN, LANES:]], axis=0)
                    start = pl.multiple_of(q * RUN * width + m * 2 * RUN, 2 * RUN)
                    t_ref[i // 2, pl.ds(start, 2 * RUN), (i % 2) * LANES : (i % 2 + 1) * LANES] = block.astype(BF16)
        return carry

    lax.fori_loop(0, width // 2 // unroll, step, 0)


def spread_first_kernel(seqs, width, l_ref, f_ref, t_ref, pairs, wide):
    wide[...] = f_ref[...].astype(F32)
    for d in range(width):
        pairs[d // 2, :, (d % 2) * LANES : (d % 2 + 1) * LANES] = wide[pl.ds(d, width, stride=width), :].astype(BF16)
    spread_left(seqs, width, l_ref, pairs, t_ref)


def spread_second_kernel(seqs, width, l_ref, pairs, t_ref):
    spread_left(seqs, width, l_ref, pairs, t_ref)


def arrange_kernel(own_ref, near_ref, far_ref, _, pair_ref):
    row, col = lax.axis_index("row"), lax.axis_index("col")
    inside = row // 8 == col
    here = own_ref.shape[0]
    own, near, far = own_ref[...], near_ref[...], far_ref[...]
    same, other = jnp.where(inside, own, near), jnp.where(inside, near, far)
    pair_ref[:here, :] = jnp.where(col == 0, same, other)
    pair_ref[here:, :] = jnp.where(col == 0, other, same)


def combine_kernel(seqs, masks, n_left, *refs):
    lefts, pieces = refs[:n_left], refs[n_left : n_left + len(masks)]
    shift_ref, out_ref, right, stage, sem = refs[n_left + len(masks) :]
    rows = pieces[0].shape[0]
    pairs = lefts[0].shape[0]
    for mask, piece in zip(masks, pieces):
        place = jnp.bitwise_xor(lax.rem(lax.axis_index("row"), len(masks)), mask) if len(masks) > 1 else 0
        right[pl.ds(pl.multiple_of(place * rows, rows), rows), :] = piece[...]
    shift = jnp.concatenate([shift_ref[...]] * 2, axis=1)
    unroll = next(u for u in (6, 4, 3, 2, 1) if pairs % u == 0)

    for h, left in enumerate(lefts):
        first = 2 * pairs * (jnp.bitwise_xor(lax.axis_index("col"), h) if n_left > 1 else 0)

        def step(n, carry, left=left, first=first, h=h):
            for u in range(unroll):
                p = n * unroll + u
                update = jnp.dot(right[...], left[p], preferred_element_type=F32) * (1.0 / seqs) + shift
                stage[h * pairs + p, 0] = update[:, :LANES].astype(BF16)
                stage[h * pairs + p, 1] = update[:, LANES:].astype(BF16)
                pltpu.make_async_copy(stage.at[h * pairs + p], out_ref.at[pl.ds(first + 2 * p, 2)], sem.at[h * pairs + p]).start()
            return carry

        lax.fori_loop(0, pairs // unroll, step, 0)

    def wait(p, carry):
        pltpu.make_async_copy(stage.at[p], out_ref.at[pl.ds(2 * p, 2)], sem.at[p]).wait()
        return carry

    lax.fori_loop(0, n_left * pairs, wait, 0)


VMEM = pl.BlockSpec(memory_space=pltpu.VMEM)
HBM = pl.BlockSpec(memory_space=pltpu.HBM)


def params():
    return pltpu.CompilerParams(vmem_limit_bytes=12 << 20)


def keep(value):
    return pltpu.with_memory_space_constraint(value, pltpu.VMEM)


def project(x, gain, shift, first, first_shift, second, second_shift):
    seqs, here, channels = x.shape
    width = first.shape[1]
    args = (x, gain[None], shift[None], first.T, first_shift[None], second.T, second_shift[None])
    args = [pltpu.with_memory_space_constraint(a, pltpu.HBM) for a in args]
    return pl.pallas_call(
        project_kernel,
        out_shape=(
            jax.ShapeDtypeStruct((here, seqs * width), BF16),
            jax.ShapeDtypeStruct((here * width // LANES * seqs, LANES), BF16),
        ),
        in_specs=[HBM] * len(args),
        out_specs=(VMEM, VMEM),
        scratch_shapes=[pltpu.VMEM((2, seqs * here, LANES), F32)]
        + [pltpu.VMEM(a.shape, a.dtype) for a in args]
        + [pltpu.SemaphoreType.DMA((len(args),))],
        compiler_params=params(),
        cost_estimate=pl.CostEstimate(flops=2 * x.size * 256, bytes_accessed=2 * x.size, transcendentals=0),
        name="project",
    )(*args)


def spread(left, final, seqs, width, pairs=None):
    residues = left.shape[0] // seqs * (LANES // width)
    wide = pltpu.VMEM((residues // 2, seqs * width, 2 * LANES), BF16)
    cost = pl.CostEstimate(
        flops=2 * residues * seqs * 256 * width * LANES, bytes_accessed=left.size * 2, transcendentals=0
    )
    if pairs is None:
        return pl.pallas_call(
            functools.partial(spread_first_kernel, seqs, width),
            out_shape=(wide, pltpu.VMEM((width // 2, width, 2 * LANES), BF16)),
            in_specs=[VMEM] * 2,
            out_specs=(VMEM, VMEM),
            scratch_shapes=[pltpu.VMEM(final.shape, F32)],
            compiler_params=params(),
            cost_estimate=cost,
            name="spread_first",
        )(left, final)
    return pl.pallas_call(
        functools.partial(spread_second_kernel, seqs, width),
        out_shape=wide,
        in_specs=[VMEM] * 2,
        out_specs=VMEM,
        compiler_params=params(),
        cost_estimate=cost,
        name="spread_second",
    )(left, keep(pairs))


def arrange(own, near, far, after):
    return pl.pallas_call(
        arrange_kernel,
        out_shape=jax.ShapeDtypeStruct((2 * own.shape[0], own.shape[1]), BF16),
        in_specs=[VMEM] * 4,
        out_specs=VMEM,
        compiler_params=params(),
        name="arrange",
    )(own, near, far, keep(after))


def combine(lefts, pieces, masks, final_shift, seqs):
    pairs, depth, _ = lefts[0].shape
    span = pieces[0].shape[0] * len(pieces)
    total = 2 * pairs * len(lefts)
    return pl.pallas_call(
        functools.partial(combine_kernel, seqs, masks, len(lefts)),
        out_shape=jax.ShapeDtypeStruct((total, span, LANES), BF16),
        in_specs=[VMEM] * (len(lefts) + len(pieces) + 1),
        out_specs=HBM,
        scratch_shapes=[
            pltpu.VMEM((span, depth), BF16),
            pltpu.VMEM((total // 2, 2, span, LANES), BF16),
            pltpu.SemaphoreType.DMA((total // 2,)),
        ],
        compiler_params=params(),
        cost_estimate=pl.CostEstimate(
            flops=2 * total * span * LANES * depth, bytes_accessed=total * span * LANES * 2, transcendentals=0
        ),
        name="combine",
    )(*[keep(left) for left in lefts], *pieces, final_shift[None])


def linear(target):
    moves = []
    for r in range(16):
        for c in range(2):
            t = target(r, c, r // 8 == c)
            if t is not None:
                moves.append((r * 2 + c, t[0] * 2 + t[1]))
    return moves


def flip(value, bits):
    return lax.ppermute(value, "row", [(r, r ^ bits) for r in range(16)])


def plain(x, gain, shift, first, first_shift, second, second_shift, final, final_shift):
    seqs, here, _ = x.shape
    width = first.shape[1]
    wide = x.astype(F32)
    centered = wide - jnp.mean(wide, axis=-1, keepdims=True)
    variance = jnp.mean(centered * centered, axis=-1, keepdims=True)
    normed = (centered * lax.rsqrt(variance + 1e-05) * gain + shift).astype(BF16)
    left = (jnp.einsum("src,ck->rsk", normed, first, preferred_element_type=F32) + first_shift).astype(BF16)
    right = (jnp.einsum("src,ck->rks", normed, second, preferred_element_type=F32) + second_shift).astype(BF16)
    right = right.reshape(here, width, seqs // RUN, RUN).transpose(0, 2, 1, 3).reshape(here, seqs * width)
    left = lax.all_gather(left.reshape(here, seqs * width), "col", axis=0, tiled=True)
    groups = LANES // width
    left = left.reshape(groups, -1, width).transpose(1, 0, 2).reshape(-1, LANES)
    every = lax.all_gather(right, ("row", "col"), axis=0, tiled=True)
    span = every.shape[0] // lax.axis_size("col")
    mine = lax.dynamic_slice_in_dim(every, lax.axis_index("col") * span, span, 0)
    spread_left, _ = spread(left, final, seqs, width)
    return combine([spread_left], [mine], (0,), final_shift, seqs)


def per_device(x, gain, shift, first, first_shift, second, second_shift, final, final_shift):
    seqs, here, _ = x.shape
    width = first.shape[1]
    if (lax.axis_size("row"), lax.axis_size("col"), here % 24) != (16, 2, 0):
        return plain(x, gain, shift, first, first_shift, second, second_shift, final, final_shift)
    right, left = project(x, gain, shift, first, first_shift, second, second_shift)
    both = ("row", "col")
    far = lax.ppermute(right, both, linear(lambda r, c, i: None if i else (r ^ 8, 1 - c)))
    beside = lax.ppermute(left, "col", [(0, 1), (1, 0)])
    near = lax.ppermute(right, both, linear(lambda r, c, i: (r ^ 8, c) if i else (r, 1 - c)))
    own, pairs = spread(left, final, seqs, width)
    pair = arrange(right, near, far, pairs)
    pieces = [pair] + [flip(pair, bits) for bits in (2, 4, 6)]
    pieces += [flip(piece, 1) for piece in pieces]
    lefts = [own, spread(beside, final, seqs, width, pairs)]
    return combine(lefts, pieces, (0, 2, 4, 6, 1, 3, 5, 7), final_shift, seqs)


def solution(mesh):
    return jax.shard_map(
        per_device,
        mesh=mesh,
        in_specs=(P("groups", ("row", "col"), None), P(), P(), P(), P(), P(), P(), P(), P()),
        out_specs=P(("groups", "row"), "col", None),
        check_vma=False,
    )
```

time: 134 us -> 30.2 us (0.23)
  the two profiles are of different devices: /device:TPU:3 before, /device:TPU:0 now
where the time goes in v1:
time: 30.2 us; the launch traced here: 30 us
  Pallas kernels  13.8 us (46%)
  starting transfers between devices  12.5 us (41%)
  waiting for transfers between devices  2.59 us (9%)
  local copies, waits for them, and re-layouts  0.95 us (3%)
    pallas_call x1, Pallas kernels, combine(): pl.pallas_call(functools.partial(combine_kernel, seqs, masks, len(lefts))...  6.76 us
    ppermute x1, starting transfers between devices, per_device(): lax.ppermute(right, both, linear(lambda r, c, i: (r ^ 8, c) if i else (r,...  6.6 us
    ppermute x7, starting transfers between devices, flip(): return lax.ppermute(value, 'row', [(r, r ^ bits) for r in range(16)])  3.76 us
    pallas_call x1, Pallas kernels, spread(): pl.pallas_call(functools.partial(spread_first_kernel, seqs, width), out_s...  2.79 us
    ppermute x7, waiting for transfers between devices, flip(): return lax.ppermute(value, 'row', [(r, r ^ bits) for r in range(16)])  2.58 us
    pallas_call x1, Pallas kernels, spread(): pl.pallas_call(functools.partial(spread_second_kernel, seqs, width), out_...  2.56 us
    pallas_call x1, Pallas kernels, project(): pl.pallas_call(project_kernel, out_shape=(jax.ShapeDtypeStruct((here, seq...  1.68 us
    ppermute x1, starting transfers between devices, per_device(): beside = lax.ppermute(left, 'col', [(0, 1), (1, 0)])  1.53 us
  transfers between devices with their start and end apart: 10, of which 3 were waited for; matrix products, arithmetic and copies ran while one was open for 0% of the time, Pallas kernels for 18%

profile of v1, /device:TPU:0, one launch (start us, length us, event | category | flops | bytes accessed | tf_op | source)
XLA Modules:
  0.0 30.0 jit_solution(6530329988063403973)
XLA Ops:
  0.0 1.7 %project.1 = (bf16[24,1024]{1,0:T(8,128)(2,1)S(1)}, bf16[192,128]{1,0:T(8,128)(2,1)S(1)}) custom-call(bf16[32,24,256]{2,1,0:T(8,128)(2,1)} %refs_0_.1, f32[1,256]{1,0:T(1,128)} %bitcast.10, f32[1,256]{1,0:T(1,128)} %bitcast.11, bf16[32,256]{1,0:T(8,128)(2,1)} %bitcast.8, f32[1,32]{1,0:T(1,128)} %bitcast.12, bf16[32,256]{1,0:T(8,128)(2,1)} %bitcast.9, ...), custom_call_target="tpu_custom_call" | custom-call | flops 100663296 | bytes 393216 | tf_op jit(solution)/shard_map/project/pallas_call | solution.py:152
  1.7 0.7 %collective-permute-start.2 = (bf16[24,1024]{1,0:T(8,128)(2,1)S(1)}, bf16[24,1024]{1,0:T(8,128)(2,1)S(1)}, u32[]{:S(2)}, u32[]{:S(2)}) collective-permute-start(bf16[24,1024]{1,0:T(8,128)(2,1)S(1)} %get-tuple-element.12.own_ref), channel_id=1, source_target_pairs={{1,16},{3,18},{5,20},{7,22},{9,24},{11,26},{13,28},{15,30},{16,1},... | collective-permute-start | bytes 147464 | tf_op jit(solution)/shard_map/ppermute | solution.py:271
  2.4 6.6 %collective-permute-start.1 = (bf16[24,1024]{1,0:T(8,128)(2,1)S(1)}, bf16[24,1024]{1,0:T(8,128)(2,1)S(1)}, u32[]{:S(2)}, u32[]{:S(2)}) collective-permute-start(bf16[24,1024]{1,0:T(8,128)(2,1)S(1)} %get-tuple-element.12.own_ref), channel_id=1, source_target_pairs={{0,16},{1,0},{2,18},{3,2},{4,20},{5,4},{6,22},{7,6},{8,24},{9,8},{... | collective-permute-start | bytes 147464 | tf_op jit(solution)/shard_map/ppermute | solution.py:273
  9.0 0.9 %copy-done.1 = bf16[1024,128]{1,0:T(8,128)(2,1)S(1)} copy-done((bf16[1024,128]{1,0:T(8,128)(2,1)S(1)}, bf16[1024,128]{1,0:T(8,128)(2,1)}, u32[]{:S(2)}) %copy-start.1) | copy-done | bytes 262168
  9.9 2.8 %spread_first.1 = (bf16[12,1024,256]{2,1,0:T(8,128)(2,1)S(1)}, bf16[16,32,256]{2,1,0:T(8,128)(2,1)S(1)}) custom-call(bf16[192,128]{1,0:T(8,128)(2,1)S(1)} %get-tuple-element.9.l_ref, bf16[1024,128]{1,0:T(8,128)(2,1)S(1)} %copy-done.1), custom_call_target="tpu_custom_call" | custom-call | flops 1610612736 | bytes 49152 | tf_op jit(solution)/shard_map/spread_first/pallas_call | solution.py:176
  12.7 0.0 collective-permute-done.2.far_ref
  12.7 0.0 collective-permute-done.1.near_ref
  12.8 2.6 %collective-permute-start.5 = (bf16[48,1024]{1,0:T(8,128)(2,1)S(1)}, bf16[48,1024]{1,0:T(8,128)(2,1)S(1)}, u32[]{:S(2)}, u32[]{:S(2)}) collective-permute-start(bf16[48,1024]{1,0:T(8,128)(2,1)S(1)} %arrange.1.refs_2_), channel_id=1, source_target_pairs={{0,12},{2,14},{4,8},{6,10},{8,4},{10,6},{12,0},{14,2},{16,28},{18,... | collective-permute-start | bytes 294920 | tf_op jit(solution)/shard_map/ppermute | solution.py:241
  15.4 0.4 %collective-permute-start.4 = (bf16[48,1024]{1,0:T(8,128)(2,1)S(1)}, bf16[48,1024]{1,0:T(8,128)(2,1)S(1)}, u32[]{:S(2)}, u32[]{:S(2)}) collective-permute-start(bf16[48,1024]{1,0:T(8,128)(2,1)S(1)} %arrange.1.refs_2_), channel_id=1, source_target_pairs={{0,8},{2,10},{4,12},{6,14},{8,0},{10,2},{12,4},{14,6},{16,24},{18,... | collective-permute-start | bytes 294920 | tf_op jit(solution)/shard_map/ppermute | solution.py:241
  15.8 0.5 %collective-permute-start.3 = (bf16[48,1024]{1,0:T(8,128)(2,1)S(1)}, bf16[48,1024]{1,0:T(8,128)(2,1)S(1)}, u32[]{:S(2)}, u32[]{:S(2)}) collective-permute-start(bf16[48,1024]{1,0:T(8,128)(2,1)S(1)} %arrange.1.refs_2_), channel_id=1, source_target_pairs={{0,4},{2,6},{4,0},{6,2},{8,12},{10,14},{12,8},{14,10},{16,20},{18,... | collective-permute-start | bytes 294920 | tf_op jit(solution)/shard_map/ppermute | solution.py:241
  16.3 1.5 %collective-permute-start = (bf16[192,128]{1,0:T(8,128)(2,1)S(1)}, bf16[192,128]{1,0:T(8,128)(2,1)S(1)}, u32[]{:S(2)}, u32[]{:S(2)}) collective-permute-start(bf16[192,128]{1,0:T(8,128)(2,1)S(1)} %get-tuple-element.9.l_ref), channel_id=1, source_target_pairs={{0,1},{1,0},{2,3},{3,2},{4,5},{5,4},{6,7},{7,6},{8,9},{9,8},{10,11... | collective-permute-start | bytes 147464 | tf_op jit(solution)/shard_map/ppermute | solution.py:272
  17.9 0.0 collective-permute-start.6
  17.9 1.2 %collective-permute-done.5.refs_5_ = bf16[48,1024]{1,0:T(8,128)(2,1)S(1)} collective-permute-done((bf16[48,1024]{1,0:T(8,128)(2,1)S(1)}, bf16[48,1024]{1,0:T(8,128)(2,1)S(1)}, u32[]{:S(2)}, u32[]{:S(2)}) %collective-permute-start.5) | collective-permute-done | bytes 98336 | tf_op jit(solution)/shard_map/ppermute | solution.py:241
  19.0 0.0 collective-permute-start.9
  19.0 1.1 %collective-permute-done.4.refs_4_ = bf16[48,1024]{1,0:T(8,128)(2,1)S(1)} collective-permute-done((bf16[48,1024]{1,0:T(8,128)(2,1)S(1)}, bf16[48,1024]{1,0:T(8,128)(2,1)S(1)}, u32[]{:S(2)}, u32[]{:S(2)}) %collective-permute-start.4) | collective-permute-done | bytes 98336 | tf_op jit(solution)/shard_map/ppermute | solution.py:241
  20.1 0.0 collective-permute-start.8
  20.1 0.3 %collective-permute-done.3.refs_3_ = bf16[48,1024]{1,0:T(8,128)(2,1)S(1)} collective-permute-done((bf16[48,1024]{1,0:T(8,128)(2,1)S(1)}, bf16[48,1024]{1,0:T(8,128)(2,1)S(1)}, u32[]{:S(2)}, u32[]{:S(2)}) %collective-permute-start.3) | collective-permute-done | bytes 98336 | tf_op jit(solution)/shard_map/ppermute | solution.py:241
  20.4 0.2 collective-permute-start.7
  20.6 0.0 collective-permute-done.l_ref
  20.6 2.6 %spread_second.1.refs_1_ = bf16[12,1024,256]{2,1,0:T(8,128)(2,1)S(1)} custom-call(bf16[192,128]{1,0:T(8,128)(2,1)S(1)} %collective-permute-done.l_ref, bf16[16,32,256]{2,1,0:T(8,128)(2,1)S(1)} %get-tuple-element.11.pairs._), custom_call_target="tpu_custom_call" | custom-call | flops 1610612736 | bytes 49152 | tf_op jit(solution)/shard_map/spread_second/pallas_call | solution.py:186
  23.2 0.0 collective-permute-done.6.refs_6_
  23.2 0.0 collective-permute-done.9.refs_9_
  23.2 0.0 collective-permute-done.7.refs_7_
  23.3 6.8 %combine.1 = bf16[48,384,128]{2,1,0:T(8,128)(2,1)} custom-call(bf16[12,1024,256]{2,1,0:T(8,128)(2,1)S(1)} %get-tuple-element.10.refs_0_, bf16[12,1024,256]{2,1,0:T(8,128)(2,1)S(1)} %spread_second.1.refs_1_, bf16[48,1024]{1,0:T(8,128)(2,1)S(1)} %arrange.1.refs_2_, bf16[48,1024]{1,0:T(8,128)(2,1)S(1)} %collective-permute-done.3.refs_3_, ...), custom_call_target="tpu_custom_call" | custom-call | flops 4831838208 | bytes 4718592 | tf_op jit(solution)/shard_map/combine/pallas_call | solution.py:212
  (5 shorter events, 0.0 us)
Async XLA Ops:
  1.7 11.0 %collective-permute-start.2 = (bf16[24,1024]{1,0:T(8,128)(2,1)S(1)}, bf16[24,1024]{1,0:T(8,128)(2,1)S(1)}, u32[]{:S(2)}, u32[]{:S(2)}) collective-permute-start(bf16[24,1024]{1,0:T(8,128)(2,1)S(1)} %get-tuple-element.12.own_ref), channel_id=1, source_target_pairs={{1,16},{3,18},{5,20},{7,22},{9,24},{11,26},{13,28},{15,30},{16,1},... | collective-permute-start | bytes 147464 | tf_op jit(solution)/shard_map/ppermute | solution.py:271
  2.4 10.4 %collective-permute-start.1 = (bf16[24,1024]{1,0:T(8,128)(2,1)S(1)}, bf16[24,1024]{1,0:T(8,128)(2,1)S(1)}, u32[]{:S(2)}, u32[]{:S(2)}) collective-permute-start(bf16[24,1024]{1,0:T(8,128)(2,1)S(1)} %get-tuple-element.12.own_ref), channel_id=1, source_target_pairs={{0,16},{1,0},{2,18},{3,2},{4,20},{5,4},{6,22},{7,6},{8,24},{9,8},{... | collective-permute-start | bytes 147464 | tf_op jit(solution)/shard_map/ppermute | solution.py:273
  9.0 0.9 %copy-start.1 = (bf16[1024,128]{1,0:T(8,128)(2,1)S(1)}, bf16[1024,128]{1,0:T(8,128)(2,1)}, u32[]{:S(2)}) copy-start(bf16[1024,128]{1,0:T(8,128)(2,1)} %f_ref.1) | copy-start | bytes 786436
  9.9 13.3 %copy-start = (f32[128]{0:T(128)S(1)}, f32[128]{0:T(128)}, u32[]{:S(2)}) copy-start(f32[128]{0:T(128)} %param.17) | copy-start | bytes 1540
  12.8 6.3 %collective-permute-start.5 = (bf16[48,1024]{1,0:T(8,128)(2,1)S(1)}, bf16[48,1024]{1,0:T(8,128)(2,1)S(1)}, u32[]{:S(2)}, u32[]{:S(2)}) collective-permute-start(bf16[48,1024]{1,0:T(8,128)(2,1)S(1)} %arrange.1.refs_2_), channel_id=1, source_target_pairs={{0,12},{2,14},{4,8},{6,10},{8,4},{10,6},{12,0},{14,2},{16,28},{18,... | collective-permute-start | bytes 294920 | tf_op jit(solution)/shard_map/ppermute | solution.py:241
  15.4 4.8 %collective-permute-start.4 = (bf16[48,1024]{1,0:T(8,128)(2,1)S(1)}, bf16[48,1024]{1,0:T(8,128)(2,1)S(1)}, u32[]{:S(2)}, u32[]{:S(2)}) collective-permute-start(bf16[48,1024]{1,0:T(8,128)(2,1)S(1)} %arrange.1.refs_2_), channel_id=1, source_target_pairs={{0,8},{2,10},{4,12},{6,14},{8,0},{10,2},{12,4},{14,6},{16,24},{18,... | collective-permute-start | bytes 294920 | tf_op jit(solution)/shard_map/ppermute | solution.py:241
  15.8 4.6 %collective-permute-start.3 = (bf16[48,1024]{1,0:T(8,128)(2,1)S(1)}, bf16[48,1024]{1,0:T(8,128)(2,1)S(1)}, u32[]{:S(2)}, u32[]{:S(2)}) collective-permute-start(bf16[48,1024]{1,0:T(8,128)(2,1)S(1)} %arrange.1.refs_2_), channel_id=1, source_target_pairs={{0,4},{2,6},{4,0},{6,2},{8,12},{10,14},{12,8},{14,10},{16,20},{18,... | collective-permute-start | bytes 294920 | tf_op jit(solution)/shard_map/ppermute | solution.py:241
  16.3 4.3 %collective-permute-start = (bf16[192,128]{1,0:T(8,128)(2,1)S(1)}, bf16[192,128]{1,0:T(8,128)(2,1)S(1)}, u32[]{:S(2)}, u32[]{:S(2)}) collective-permute-start(bf16[192,128]{1,0:T(8,128)(2,1)S(1)} %get-tuple-element.9.l_ref), channel_id=1, source_target_pairs={{0,1},{1,0},{2,3},{3,2},{4,5},{5,4},{6,7},{7,6},{8,9},{9,8},{10,11... | collective-permute-start | bytes 147464 | tf_op jit(solution)/shard_map/ppermute | solution.py:272
  17.9 5.3 %collective-permute-start.6 = (bf16[48,1024]{1,0:T(8,128)(2,1)S(1)}, bf16[48,1024]{1,0:T(8,128)(2,1)S(1)}, u32[]{:S(2)}, u32[]{:S(2)}) collective-permute-start(bf16[48,1024]{1,0:T(8,128)(2,1)S(1)} %arrange.1.refs_2_), channel_id=1, source_target_pairs={{0,2},{2,0},{4,6},{6,4},{8,10},{10,8},{12,14},{14,12},{16,18},{18,... | collective-permute-start | bytes 294920 | tf_op jit(solution)/shard_map/ppermute | solution.py:241
  19.0 4.2 %collective-permute-start.9 = (bf16[48,1024]{1,0:T(8,128)(2,1)S(1)}, bf16[48,1024]{1,0:T(8,128)(2,1)S(1)}, u32[]{:S(2)}, u32[]{:S(2)}) collective-permute-start(bf16[48,1024]{1,0:T(8,128)(2,1)S(1)} %collective-permute-done.5.refs_5_), channel_id=1, source_target_pairs={{0,2},{2,0},{4,6},{6,4},{8,10},{10,8},{12,14},{14,12},{16,18},{18,... | collective-permute-start | bytes 294920 | tf_op jit(solution)/shard_map/ppermute | solution.py:241
  20.1 3.1 %collective-permute-start.8 = (bf16[48,1024]{1,0:T(8,128)(2,1)S(1)}, bf16[48,1024]{1,0:T(8,128)(2,1)S(1)}, u32[]{:S(2)}, u32[]{:S(2)}) collective-permute-start(bf16[48,1024]{1,0:T(8,128)(2,1)S(1)} %collective-permute-done.4.refs_4_), channel_id=1, source_target_pairs={{0,2},{2,0},{4,6},{6,4},{8,10},{10,8},{12,14},{14,12},{16,18},{18,... | collective-permute-start | bytes 294920 | tf_op jit(solution)/shard_map/ppermute | solution.py:241
  20.4 2.8 %collective-permute-start.7 = (bf16[48,1024]{1,0:T(8,128)(2,1)S(1)}, bf16[48,1024]{1,0:T(8,128)(2,1)S(1)}, u32[]{:S(2)}, u32[]{:S(2)}) collective-permute-start(bf16[48,1024]{1,0:T(8,128)(2,1)S(1)} %collective-permute-done.3.refs_3_), channel_id=1, source_target_pairs={{0,2},{2,0},{4,6},{6,4},{8,10},{10,8},{12,14},{14,12},{16,18},{18,... | collective-permute-start | bytes 294920 | tf_op jit(solution)/shard_map/ppermute | solution.py:241

commit v2 on v1

--- a/solution.py
+++ b/solution.py
@@ -13,11 +13,12 @@
 
 
 def project_kernel(*refs):
-    sources, (r_ref, l_ref, held), buffers, sems = refs[:7], refs[7:10], refs[10:17], refs[17]
-    copies = [pltpu.make_async_copy(src, dst, sems.at[k]) for k, (src, dst) in enumerate(zip(sources, buffers))]
+    sources, (r_ref, l_ref, final_ref, held), buffers, sems = refs[:8], refs[8:12], refs[12:19], refs[19]
+    targets = (*buffers, final_ref)
+    copies = [pltpu.make_async_copy(src, dst, sems.at[k]) for k, (src, dst) in enumerate(zip(sources, targets))]
     for copy in copies:
         copy.start()
-    for copy in copies:
+    for copy in copies[:-1]:
         copy.wait()
     x_ref, gain_ref, shift_ref, left_ref, left_shift_ref, right_ref, right_shift_ref = buffers
     seqs, here, channels = x_ref.shape
@@ -56,27 +57,21 @@
     ordered = jnp.dot(packed, order, preferred_element_type=F32).astype(BF16)
     for q in range(seqs // RUN):
         r_ref[:, q * span : (q + 1) * span] = ordered[q * here : (q + 1) * here, :]
+    copies[-1].wait()
 
 
 def spread_left(seqs, width, l_ref, pairs, t_ref):
     groups = LANES // width
     residues = l_ref.shape[0] // seqs * groups
     left = jnp.concatenate([l_ref[:, g * width : (g + 1) * width] for g in range(groups)], axis=0)
-    unroll = 4
-
-    def step(n, carry):
-        for u in range(unroll):
-            m = n * unroll + u
-            wide_out = jnp.dot(left, pairs[m], preferred_element_type=F32)
-            for i in range(residues):
-                for q in range(seqs // RUN):
-                    s = i * seqs + q * RUN
-                    block = jnp.concatenate([wide_out[s : s + RUN, :LANES], wide_out[s : s + RUN, LANES:]], axis=0)
-                    start = pl.multiple_of(q * RUN * width + m * 2 * RUN, 2 * RUN)
-                    t_ref[i // 2, pl.ds(start, 2 * RUN), (i % 2) * LANES : (i % 2 + 1) * LANES] = block.astype(BF16)
-        return carry
-
-    lax.fori_loop(0, width // 2 // unroll, step, 0)
+    for m in range(width // 2):
+        wide_out = jnp.dot(left, pairs[m], preferred_element_type=F32)
+        for i in range(residues):
+            for q in range(seqs // RUN):
+                s = i * seqs + q * RUN
+                block = jnp.concatenate([wide_out[s : s + RUN, :LANES], wide_out[s : s + RUN, LANES:]], axis=0)
+                start = q * RUN * width + m * 2 * RUN
+                t_ref[i // 2, start : start + 2 * RUN, (i % 2) * LANES : (i % 2 + 1) * LANES] = block.astype(BF16)
 
 
 def spread_first_kernel(seqs, width, l_ref, f_ref, t_ref, pairs, wide):
@@ -98,6 +93,10 @@
     same, other = jnp.where(inside, own, near), jnp.where(inside, near, far)
     pair_ref[:here, :] = jnp.where(col == 0, same, other)
     pair_ref[here:, :] = jnp.where(col == 0, other, same)
+
+
+def order_kernel(*refs):
+    pass
 
 
 def combine_kernel(seqs, masks, n_left, *refs):
@@ -109,7 +108,7 @@
         place = jnp.bitwise_xor(lax.rem(lax.axis_index("row"), len(masks)), mask) if len(masks) > 1 else 0
         right[pl.ds(pl.multiple_of(place * rows, rows), rows), :] = piece[...]
     shift = jnp.concatenate([shift_ref[...]] * 2, axis=1)
-    unroll = next(u for u in (6, 4, 3, 2, 1) if pairs % u == 0)
+    unroll = next(u for u in (12, 6, 4, 3, 2, 1) if pairs % u == 0)
 
     for h, left in enumerate(lefts):
         first = 2 * pairs * (jnp.bitwise_xor(lax.axis_index("col"), h) if n_left > 1 else 0)
@@ -144,21 +143,22 @@
     return pltpu.with_memory_space_constraint(value, pltpu.VMEM)
 
 
-def project(x, gain, shift, first, first_shift, second, second_shift):
+def project(x, gain, shift, first, first_shift, second, second_shift, final):
     seqs, here, channels = x.shape
     width = first.shape[1]
-    args = (x, gain[None], shift[None], first.T, first_shift[None], second.T, second_shift[None])
+    args = (x, gain[None], shift[None], first.T, first_shift[None], second.T, second_shift[None], final)
     args = [pltpu.with_memory_space_constraint(a, pltpu.HBM) for a in args]
     return pl.pallas_call(
         project_kernel,
         out_shape=(
             jax.ShapeDtypeStruct((here, seqs * width), BF16),
             jax.ShapeDtypeStruct((here * width // LANES * seqs, LANES), BF16),
+            pltpu.VMEM(final.shape, BF16),
         ),
         in_specs=[HBM] * len(args),
-        out_specs=(VMEM, VMEM),
+        out_specs=(VMEM, VMEM, VMEM),
         scratch_shapes=[pltpu.VMEM((2, seqs * here, LANES), F32)]
-        + [pltpu.VMEM(a.shape, a.dtype) for a in args]
+        + [pltpu.VMEM(a.shape, a.dtype) for a in args[:-1]]
         + [pltpu.SemaphoreType.DMA((len(args),))],
         compiler_params=params(),
         cost_estimate=pl.CostEstimate(flops=2 * x.size * 256, bytes_accessed=2 * x.size, transcendentals=0),
@@ -182,7 +182,7 @@
             compiler_params=params(),
             cost_estimate=cost,
             name="spread_first",
-        )(left, final)
+        )(left, keep(final))
     return pl.pallas_call(
         functools.partial(spread_second_kernel, seqs, width),
         out_shape=wide,
@@ -203,6 +203,19 @@
         compiler_params=params(),
         name="arrange",
     )(own, near, far, keep(after))
+
+
+def after(values, *earlier):
+    n = len(values)
+    return pl.pallas_call(
+        order_kernel,
+        out_shape=[jax.ShapeDtypeStruct(v.shape, v.dtype) for v in values],
+        in_specs=[pl.BlockSpec(memory_space=pl.ANY)] * (n + len(earlier)),
+        out_specs=[pl.BlockSpec(memory_space=pl.ANY)] * n,
+        input_output_aliases={k: k for k in range(n)},
+        compiler_params=params(),
+        name="after",
+    )(*values, *earlier)
 
 
 def combine(lefts, pieces, masks, final_shift, seqs):
@@ -266,16 +279,17 @@
     width = first.shape[1]
     if (lax.axis_size("row"), lax.axis_size("col"), here % 24) != (16, 2, 0):
         return plain(x, gain, shift, first, first_shift, second, second_shift, final, final_shift)
-    right, left = project(x, gain, shift, first, first_shift, second, second_shift)
+    right, left, final = project(x, gain, shift, first, first_shift, second, second_shift, final)
     both = ("row", "col")
-    far = lax.ppermute(right, both, linear(lambda r, c, i: None if i else (r ^ 8, 1 - c)))
+    far = lax.ppermute(right, both, linear(lambda r, c, i: (r ^ 1, c) if i else (r ^ 8, 1 - c)))
     beside = lax.ppermute(left, "col", [(0, 1), (1, 0)])
     near = lax.ppermute(right, both, linear(lambda r, c, i: (r ^ 8, c) if i else (r, 1 - c)))
     own, pairs = spread(left, final, seqs, width)
     pair = arrange(right, near, far, pairs)
-    pieces = [pair] + [flip(pair, bits) for bits in (2, 4, 6)]
+    gathered = [flip(pair, bits) for bits in (2, 4, 6)]
+    lefts = [own, spread(beside, final, seqs, width, pairs)]
+    pieces = [pair, *after(gathered, keep(lefts[1]))]
     pieces += [flip(piece, 1) for piece in pieces]
-    lefts = [own, spread(beside, final, seqs, width, pairs)]
     return combine(lefts, pieces, (0, 2, 4, 6, 1, 3, 5, 7), final_shift, seqs)
 
 

time: 30.2 us -> 26.3 us (0.87)
  the two profiles are of different devices: /device:TPU:0 before, /device:TPU:3 now
where the time goes in v2:
time: 26.3 us; the launch traced here: 26.2 us
  Pallas kernels  11.6 us (44%)
  starting transfers between devices  9.64 us (37%)
  waiting for transfers between devices  4.89 us (19%)
    pallas_call x1, Pallas kernels, combine(): pl.pallas_call(functools.partial(combine_kernel, seqs, masks, len(lefts))...  6.22 us
    ppermute x7, starting transfers between devices, flip(): return lax.ppermute(value, 'row', [(r, r ^ bits) for r in range(16)])  6.02 us
    ppermute x7, waiting for transfers between devices, flip(): return lax.ppermute(value, 'row', [(r, r ^ bits) for r in range(16)])  3.92 us
    ppermute x1, starting transfers between devices, per_device(): lax.ppermute(right, both, linear(lambda r, c, i: (r ^ 1, c) if i else (r...  2.35 us
    pallas_call x1, Pallas kernels, spread(): pl.pallas_call(functools.partial(spread_first_kernel, seqs, width), out_s...  1.88 us
    pallas_call x1, Pallas kernels, spread(): pl.pallas_call(functools.partial(spread_second_kernel, seqs, width), out_...  1.79 us
    pallas_call x1, Pallas kernels, project(): pl.pallas_call(project_kernel, out_shape=(jax.ShapeDtypeStruct((here, seq...  1.69 us
    ppermute x1, starting transfers between devices, per_device(): beside = lax.ppermute(left, 'col', [(0, 1), (1, 0)])  1.26 us
  transfers between devices with their start and end apart: 10, of which 6 were waited for; matrix products, arithmetic and copies ran while one was open for 0% of the time, Pallas kernels for 14%

profile of v2, /device:TPU:3, one launch (start us, length us, event | category | flops | bytes accessed | tf_op | source)
XLA Modules:
  0.0 26.2 jit_solution(12320209012266318136)
XLA Ops:
  0.0 1.7 %project.1 = (bf16[24,1024]{1,0:T(8,128)(2,1)S(1)}, bf16[192,128]{1,0:T(8,128)(2,1)S(1)}, bf16[1024,128]{1,0:T(8,128)(2,1)S(1)}) custom-call(bf16[32,24,256]{2,1,0:T(8,128)(2,1)} %refs_0_.1, f32[1,256]{1,0:T(1,128)} %bitcast.10, f32[1,256]{1,0:T(1,128)} %bitcast.11, bf16[32,256]{1,0:T(8,128)(2,1)} %bitcast.8, f32[1,32]{1,0:T(1,128)} %bitcast.12, ...), custom_call_target="tpu_custom_call" | custom-call | flops 100663296 | bytes 393216 | tf_op jit(solution)/shard_map/project/pallas_call | solution.py:151
  1.7 2.3 %collective-permute-start.2 = (bf16[24,1024]{1,0:T(8,128)(2,1)S(1)}, bf16[24,1024]{1,0:T(8,128)(2,1)S(1)}, u32[]{:S(2)}, u32[]{:S(2)}) collective-permute-start(bf16[24,1024]{1,0:T(8,128)(2,1)S(1)} %get-tuple-element.17.own_ref), channel_id=1, source_target_pairs={{0,2},{1,16},{2,0},{3,18},{4,6},{5,20},{6,4},{7,22},{8,10},{9,24},... | collective-permute-start | bytes 147464 | tf_op jit(solution)/shard_map/ppermute | solution.py:284
  4.0 0.0 collective-permute-start.1
  4.1 1.3 %collective-permute-start = (bf16[192,128]{1,0:T(8,128)(2,1)S(1)}, bf16[192,128]{1,0:T(8,128)(2,1)S(1)}, u32[]{:S(2)}, u32[]{:S(2)}) collective-permute-start(bf16[192,128]{1,0:T(8,128)(2,1)S(1)} %get-tuple-element.13.l_ref), channel_id=1, source_target_pairs={{0,1},{1,0},{2,3},{3,2},{4,5},{5,4},{6,7},{7,6},{8,9},{9,8},{10,11... | collective-permute-start | bytes 147464 | tf_op jit(solution)/shard_map/ppermute | solution.py:285
  5.3 1.9 %spread_first.1 = (bf16[12,1024,256]{2,1,0:T(8,128)(2,1)S(1)}, bf16[16,32,256]{2,1,0:T(8,128)(2,1)S(1)}) custom-call(bf16[192,128]{1,0:T(8,128)(2,1)S(1)} %get-tuple-element.13.l_ref, bf16[1024,128]{1,0:T(8,128)(2,1)S(1)} %get-tuple-element.14.f_ref), custom_call_target="tpu_custom_call" | custom-call | flops 1610612736 | bytes 49152 | tf_op jit(solution)/shard_map/spread_first/pallas_call | solution.py:176
  7.2 0.0 collective-permute-done.2.far_ref
  7.2 1.0 %collective-permute-done.1.near_ref = bf16[24,1024]{1,0:T(8,128)(2,1)S(1)} collective-permute-done((bf16[24,1024]{1,0:T(8,128)(2,1)S(1)}, bf16[24,1024]{1,0:T(8,128)(2,1)S(1)}, u32[]{:S(2)}, u32[]{:S(2)}) %collective-permute-start.1) | collective-permute-done | bytes 49184 | tf_op jit(solution)/shard_map/ppermute | solution.py:286
  8.2 0.0 copy-start
  8.2 2.0 %collective-permute-start.6 = (bf16[48,1024]{1,0:T(8,128)(2,1)S(1)}, bf16[48,1024]{1,0:T(8,128)(2,1)S(1)}, u32[]{:S(2)}, u32[]{:S(2)}) collective-permute-start(bf16[48,1024]{1,0:T(8,128)(2,1)S(1)} %arrange.1.refs_2_), channel_id=1, source_target_pairs={{0,2},{2,0},{4,6},{6,4},{8,10},{10,8},{12,14},{14,12},{16,18},{18,... | collective-permute-start | bytes 294920 | tf_op jit(solution)/shard_map/ppermute | solution.py:254
  10.2 2.1 %collective-permute-start.5 = (bf16[48,1024]{1,0:T(8,128)(2,1)S(1)}, bf16[48,1024]{1,0:T(8,128)(2,1)S(1)}, u32[]{:S(2)}, u32[]{:S(2)}) collective-permute-start(bf16[48,1024]{1,0:T(8,128)(2,1)S(1)} %arrange.1.refs_2_), channel_id=1, source_target_pairs={{0,12},{2,14},{4,8},{6,10},{8,4},{10,6},{12,0},{14,2},{16,28},{18,... | collective-permute-start | bytes 294920 | tf_op jit(solution)/shard_map/ppermute | solution.py:254
  12.4 0.3 %collective-permute-start.4 = (bf16[48,1024]{1,0:T(8,128)(2,1)S(1)}, bf16[48,1024]{1,0:T(8,128)(2,1)S(1)}, u32[]{:S(2)}, u32[]{:S(2)}) collective-permute-start(bf16[48,1024]{1,0:T(8,128)(2,1)S(1)} %arrange.1.refs_2_), channel_id=1, source_target_pairs={{0,8},{2,10},{4,12},{6,14},{8,0},{10,2},{12,4},{14,6},{16,24},{18,... | collective-permute-start | bytes 294920 | tf_op jit(solution)/shard_map/ppermute | solution.py:254
  12.7 0.2 collective-permute-start.3
  12.9 0.0 collective-permute-done.l_ref
  12.9 1.8 %spread_second.1.refs_3_.refs_1_ = bf16[12,1024,256]{2,1,0:T(8,128)(2,1)S(1)} custom-call(bf16[192,128]{1,0:T(8,128)(2,1)S(1)} %collective-permute-done.l_ref, bf16[16,32,256]{2,1,0:T(8,128)(2,1)S(1)} %get-tuple-element.16.pairs._), custom_call_target="tpu_custom_call" | custom-call | flops 1610612736 | bytes 49152 | tf_op jit(solution)/shard_map/spread_second/pallas_call | solution.py:186
  14.7 0.8 %collective-permute-done.5.refs_2_ = bf16[48,1024]{1,0:T(8,128)(2,1)S(1)} collective-permute-done((bf16[48,1024]{1,0:T(8,128)(2,1)S(1)}, bf16[48,1024]{1,0:T(8,128)(2,1)S(1)}, u32[]{:S(2)}, u32[]{:S(2)}) %collective-permute-start.5) | collective-permute-done | bytes 98336 | tf_op jit(solution)/shard_map/ppermute | solution.py:254
  15.5 2.2 %collective-permute-done.4.refs_1_ = bf16[48,1024]{1,0:T(8,128)(2,1)S(1)} collective-permute-done((bf16[48,1024]{1,0:T(8,128)(2,1)S(1)}, bf16[48,1024]{1,0:T(8,128)(2,1)S(1)}, u32[]{:S(2)}, u32[]{:S(2)}) %collective-permute-start.4) | collective-permute-done | bytes 98336 | tf_op jit(solution)/shard_map/ppermute | solution.py:254
  17.7 0.0 collective-permute-done.3.refs_0_
  17.7 0.9 %collective-permute-start.7 = (bf16[48,1024]{1,0:T(8,128)(2,1)S(1)}, bf16[48,1024]{1,0:T(8,128)(2,1)S(1)}, u32[]{:S(2)}, u32[]{:S(2)}) collective-permute-start(bf16[48,1024]{1,0:T(8,128)(2,1)S(1)} %get-tuple-element.18.refs_3_), channel_id=1, source_target_pairs={{0,2},{2,0},{4,6},{6,4},{8,10},{10,8},{12,14},{14,12},{16,18},{18,... | collective-permute-start | bytes 294920 | tf_op jit(solution)/shard_map/ppermute | solution.py:254
  18.5 0.1 collective-permute-start.8
  18.6 0.4 %collective-permute-start.9 = (bf16[48,1024]{1,0:T(8,128)(2,1)S(1)}, bf16[48,1024]{1,0:T(8,128)(2,1)S(1)}, u32[]{:S(2)}, u32[]{:S(2)}) collective-permute-start(bf16[48,1024]{1,0:T(8,128)(2,1)S(1)} %get-tuple-element.20.refs_5_), channel_id=1, source_target_pairs={{0,2},{2,0},{4,6},{6,4},{8,10},{10,8},{12,14},{14,12},{16,18},{18,... | collective-permute-start | bytes 294920 | tf_op jit(solution)/shard_map/ppermute | solution.py:254
  19.0 0.4 %collective-permute-done.7.refs_7_ = bf16[48,1024]{1,0:T(8,128)(2,1)S(1)} collective-permute-done((bf16[48,1024]{1,0:T(8,128)(2,1)S(1)}, bf16[48,1024]{1,0:T(8,128)(2,1)S(1)}, u32[]{:S(2)}, u32[]{:S(2)}) %collective-permute-start.7) | collective-permute-done | bytes 98336 | tf_op jit(solution)/shard_map/ppermute | solution.py:254
  19.5 0.4 %collective-permute-done.8.refs_8_ = bf16[48,1024]{1,0:T(8,128)(2,1)S(1)} collective-permute-done((bf16[48,1024]{1,0:T(8,128)(2,1)S(1)}, bf16[48,1024]{1,0:T(8,128)(2,1)S(1)}, u32[]{:S(2)}, u32[]{:S(2)}) %collective-permute-start.8) | collective-permute-done | bytes 98336 | tf_op jit(solution)/shard_map/ppermute | solution.py:254
  19.8 0.2 collective-permute-done.9.refs_9_
  20.0 6.2 %combine.1 = bf16[48,384,128]{2,1,0:T(8,128)(2,1)} custom-call(bf16[12,1024,256]{2,1,0:T(8,128)(2,1)S(1)} %get-tuple-element.15.refs_0_, bf16[12,1024,256]{2,1,0:T(8,128)(2,1)S(1)} %spread_second.1.refs_3_.refs_1_, bf16[48,1024]{1,0:T(8,128)(2,1)S(1)} %arrange.1.refs_2_, bf16[48,1024]{1,0:T(8,128)(2,1)S(1)} %get-tuple-element.18.refs_3_, ...), custom_call_target="tpu_custom_call" | custom-call | flops 4831838208 | bytes 4718592 | tf_op jit(solution)/shard_map/combine/pallas_call | solution.py:225
  (4 shorter events, 0.0 us)
Async XLA Ops:
  1.7 5.5 %collective-permute-start.2 = (bf16[24,1024]{1,0:T(8,128)(2,1)S(1)}, bf16[24,1024]{1,0:T(8,128)(2,1)S(1)}, u32[]{:S(2)}, u32[]{:S(2)}) collective-permute-start(bf16[24,1024]{1,0:T(8,128)(2,1)S(1)} %get-tuple-element.17.own_ref), channel_id=1, source_target_pairs={{0,2},{1,16},{2,0},{3,18},{4,6},{5,20},{6,4},{7,22},{8,10},{9,24},... | collective-permute-start | bytes 147464 | tf_op jit(solution)/shard_map/ppermute | solution.py:284
  4.0 4.1 %collective-permute-start.1 = (bf16[24,1024]{1,0:T(8,128)(2,1)S(1)}, bf16[24,1024]{1,0:T(8,128)(2,1)S(1)}, u32[]{:S(2)}, u32[]{:S(2)}) collective-permute-start(bf16[24,1024]{1,0:T(8,128)(2,1)S(1)} %get-tuple-element.17.own_ref), channel_id=1, source_target_pairs={{0,16},{1,0},{2,18},{3,2},{4,20},{5,4},{6,22},{7,6},{8,24},{9,8},{... | collective-permute-start | bytes 147464 | tf_op jit(solution)/shard_map/ppermute | solution.py:286
  4.1 8.8 %collective-permute-start = (bf16[192,128]{1,0:T(8,128)(2,1)S(1)}, bf16[192,128]{1,0:T(8,128)(2,1)S(1)}, u32[]{:S(2)}, u32[]{:S(2)}) collective-permute-start(bf16[192,128]{1,0:T(8,128)(2,1)S(1)} %get-tuple-element.13.l_ref), channel_id=1, source_target_pairs={{0,1},{1,0},{2,3},{3,2},{4,5},{5,4},{6,7},{7,6},{8,9},{9,8},{10,11... | collective-permute-start | bytes 147464 | tf_op jit(solution)/shard_map/ppermute | solution.py:285
  8.2 11.8 %copy-start = (f32[128]{0:T(128)S(1)}, f32[128]{0:T(128)}, u32[]{:S(2)}) copy-start(f32[128]{0:T(128)} %param.17) | copy-start | bytes 1540
  8.2 10.8 %collective-permute-start.6 = (bf16[48,1024]{1,0:T(8,128)(2,1)S(1)}, bf16[48,1024]{1,0:T(8,128)(2,1)S(1)}, u32[]{:S(2)}, u32[]{:S(2)}) collective-permute-start(bf16[48,1024]{1,0:T(8,128)(2,1)S(1)} %arrange.1.refs_2_), channel_id=1, source_target_pairs={{0,2},{2,0},{4,6},{6,4},{8,10},{10,8},{12,14},{14,12},{16,18},{18,... | collective-permute-start | bytes 294920 | tf_op jit(solution)/shard_map/ppermute | solution.py:254
  10.2 5.3 %collective-permute-start.5 = (bf16[48,1024]{1,0:T(8,128)(2,1)S(1)}, bf16[48,1024]{1,0:T(8,128)(2,1)S(1)}, u32[]{:S(2)}, u32[]{:S(2)}) collective-permute-start(bf16[48,1024]{1,0:T(8,128)(2,1)S(1)} %arrange.1.refs_2_), channel_id=1, source_target_pairs={{0,12},{2,14},{4,8},{6,10},{8,4},{10,6},{12,0},{14,2},{16,28},{18,... | collective-permute-start | bytes 294920 | tf_op jit(solution)/shard_map/ppermute | solution.py:254
  12.4 5.3 %collective-permute-start.4 = (bf16[48,1024]{1,0:T(8,128)(2,1)S(1)}, bf16[48,1024]{1,0:T(8,128)(2,1)S(1)}, u32[]{:S(2)}, u32[]{:S(2)}) collective-permute-start(bf16[48,1024]{1,0:T(8,128)(2,1)S(1)} %arrange.1.refs_2_), channel_id=1, source_target_pairs={{0,8},{2,10},{4,12},{6,14},{8,0},{10,2},{12,4},{14,6},{16,24},{18,... | collective-permute-start | bytes 294920 | tf_op jit(solution)/shard_map/ppermute | solution.py:254
  12.7 5.0 %collective-permute-start.3 = (bf16[48,1024]{1,0:T(8,128)(2,1)S(1)}, bf16[48,1024]{1,0:T(8,128)(2,1)S(1)}, u32[]{:S(2)}, u32[]{:S(2)}) collective-permute-start(bf16[48,1024]{1,0:T(8,128)(2,1)S(1)} %arrange.1.refs_2_), channel_id=1, source_target_pairs={{0,4},{2,6},{4,0},{6,2},{8,12},{10,14},{12,8},{14,10},{16,20},{18,... | collective-permute-start | bytes 294920 | tf_op jit(solution)/shard_map/ppermute | solution.py:254
  17.7 1.8 %collective-permute-start.7 = (bf16[48,1024]{1,0:T(8,128)(2,1)S(1)}, bf16[48,1024]{1,0:T(8,128)(2,1)S(1)}, u32[]{:S(2)}, u32[]{:S(2)}) collective-permute-start(bf16[48,1024]{1,0:T(8,128)(2,1)S(1)} %get-tuple-element.18.refs_3_), channel_id=1, source_target_pairs={{0,2},{2,0},{4,6},{6,4},{8,10},{10,8},{12,14},{14,12},{16,18},{18,... | collective-permute-start | bytes 294920 | tf_op jit(solution)/shard_map/ppermute | solution.py:254
  18.5 1.3 %collective-permute-start.8 = (bf16[48,1024]{1,0:T(8,128)(2,1)S(1)}, bf16[48,1024]{1,0:T(8,128)(2,1)S(1)}, u32[]{:S(2)}, u32[]{:S(2)}) collective-permute-start(bf16[48,1024]{1,0:T(8,128)(2,1)S(1)} %get-tuple-element.19.refs_4_), channel_id=1, source_target_pairs={{0,2},{2,0},{4,6},{6,4},{8,10},{10,8},{12,14},{14,12},{16,18},{18,... | collective-permute-start | bytes 294920 | tf_op jit(solution)/shard_map/ppermute | solution.py:254
  18.6 1.4 %collective-permute-start.9 = (bf16[48,1024]{1,0:T(8,128)(2,1)S(1)}, bf16[48,1024]{1,0:T(8,128)(2,1)S(1)}, u32[]{:S(2)}, u32[]{:S(2)}) collective-permute-start(bf16[48,1024]{1,0:T(8,128)(2,1)S(1)} %get-tuple-element.20.refs_5_), channel_id=1, source_target_pairs={{0,2},{2,0},{4,6},{6,4},{8,10},{10,8},{12,14},{14,12},{16,18},{18,... | collective-permute-start | bytes 294920 | tf_op jit(solution)/shard_map/ppermute | solution.py:254

commit v3 on v2

--- a/solution.py
+++ b/solution.py
@@ -99,16 +99,24 @@
     pass
 
 
-def combine_kernel(seqs, masks, n_left, *refs):
+def combine_kernel(seqs, masks, n_left, last, *refs):
     lefts, pieces = refs[:n_left], refs[n_left : n_left + len(masks)]
-    shift_ref, out_ref, right, stage, sem = refs[n_left + len(masks) :]
+    shift_ref, refs = refs[n_left + len(masks)], refs[n_left + len(masks) + 1 :]
+    stage, right = refs[-3], refs[-2]
     rows = pieces[0].shape[0]
     pairs = lefts[0].shape[0]
-    for mask, piece in zip(masks, pieces):
-        place = jnp.bitwise_xor(lax.rem(lax.axis_index("row"), len(masks)), mask) if len(masks) > 1 else 0
-        right[pl.ds(pl.multiple_of(place * rows, rows), rows), :] = piece[...]
+    count = stage.shape[2] // rows
+    spot = lax.rem(lax.axis_index("row"), count) if count > 1 else 0
+    run = 2 * rows if count > 1 else rows
+    for n, (mask, piece) in enumerate(zip(masks, pieces)):
+        start = (n // 2 * 2 + jnp.bitwise_and(jnp.bitwise_xor(spot, mask), 1)) * rows if count > 1 else 0
+        right[pl.ds(pl.multiple_of(start, rows), rows), :] = piece[...]
     shift = jnp.concatenate([shift_ref[...]] * 2, axis=1)
     unroll = next(u for u in (12, 6, 4, 3, 2, 1) if pairs % u == 0)
+    places = [
+        pl.multiple_of(jnp.bitwise_xor(spot, masks[n]) // 2 * run, run) if count > 1 else 0
+        for n in range(0, len(masks), 2)
+    ]
 
     for h, left in enumerate(lefts):
         first = 2 * pairs * (jnp.bitwise_xor(lax.axis_index("col"), h) if n_left > 1 else 0)
@@ -117,18 +125,19 @@
             for u in range(unroll):
                 p = n * unroll + u
                 update = jnp.dot(right[...], left[p], preferred_element_type=F32) * (1.0 / seqs) + shift
-                stage[h * pairs + p, 0] = update[:, :LANES].astype(BF16)
-                stage[h * pairs + p, 1] = update[:, LANES:].astype(BF16)
-                pltpu.make_async_copy(stage.at[h * pairs + p], out_ref.at[pl.ds(first + 2 * p, 2)], sem.at[h * pairs + p]).start()
+                for k, place in enumerate(places):
+                    block = update[k * run : (k + 1) * run].astype(BF16)
+                    stage[h * pairs + p, 0, pl.ds(place, run)] = block[:, :LANES]
+                    stage[h * pairs + p, 1, pl.ds(place, run)] = block[:, LANES:]
+                if last:
+                    out_ref, sem = refs[-4], refs[-1]
+                    pltpu.make_async_copy(stage.at[h * pairs + p], out_ref.at[pl.ds(first + 2 * p, 2)], sem).start()
             return carry
 
         lax.fori_loop(0, pairs // unroll, step, 0)
-
-    def wait(p, carry):
-        pltpu.make_async_copy(stage.at[p], out_ref.at[pl.ds(2 * p, 2)], sem.at[p]).wait()
-        return carry
-
-    lax.fori_loop(0, n_left * pairs, wait, 0)
+    if last:
+        out_ref, sem = refs[-4], refs[-1]
+        pltpu.make_async_copy(out_ref, out_ref, sem).wait()
 
 
 VMEM = pl.BlockSpec(memory_space=pltpu.VMEM)
@@ -218,26 +227,26 @@
     )(*values, *earlier)
 
 
-def combine(lefts, pieces, masks, final_shift, seqs):
+def combine(lefts, pieces, masks, final_shift, seqs, span, begun=None, last=True):
     pairs, depth, _ = lefts[0].shape
-    span = pieces[0].shape[0] * len(pieces)
+    rows = pieces[0].shape[0] * len(pieces)
     total = 2 * pairs * len(lefts)
-    return pl.pallas_call(
-        functools.partial(combine_kernel, seqs, masks, len(lefts)),
-        out_shape=jax.ShapeDtypeStruct((total, span, LANES), BF16),
-        in_specs=[VMEM] * (len(lefts) + len(pieces) + 1),
-        out_specs=HBM,
-        scratch_shapes=[
-            pltpu.VMEM((span, depth), BF16),
-            pltpu.VMEM((total // 2, 2, span, LANES), BF16),
-            pltpu.SemaphoreType.DMA((total // 2,)),
-        ],
+    stage = pltpu.VMEM((total // 2, 2, span, LANES), BF16)
+    args = [*[keep(left) for left in lefts], *pieces, final_shift[None]] + ([] if begun is None else [keep(begun)])
+    outs = ([jax.ShapeDtypeStruct((total, span, LANES), BF16)] if last else []) + [stage]
+    return pl.pallas_call(
+        functools.partial(combine_kernel, seqs, masks, len(lefts), last),
+        out_shape=outs,
+        in_specs=[VMEM] * len(args),
+        out_specs=[HBM, VMEM] if last else [VMEM],
+        input_output_aliases={} if begun is None else {len(args) - 1: len(outs) - 1},
+        scratch_shapes=[pltpu.VMEM((rows, depth), BF16), pltpu.SemaphoreType.DMA],
         compiler_params=params(),
         cost_estimate=pl.CostEstimate(
-            flops=2 * total * span * LANES * depth, bytes_accessed=total * span * LANES * 2, transcendentals=0
+            flops=2 * total * rows * LANES * depth, bytes_accessed=total * rows * LANES * 2, transcendentals=0
         ),
-        name="combine",
-    )(*[keep(left) for left in lefts], *pieces, final_shift[None])
+        name="combine_last" if last else "combine_some",
+    )(*args)[0]
 
 
 def linear(target):
@@ -271,7 +280,7 @@
     span = every.shape[0] // lax.axis_size("col")
     mine = lax.dynamic_slice_in_dim(every, lax.axis_index("col") * span, span, 0)
     spread_left, _ = spread(left, final, seqs, width)
-    return combine([spread_left], [mine], (0,), final_shift, seqs)
+    return combine([spread_left], [mine], (0,), final_shift, seqs, span)
 
 
 def per_device(x, gain, shift, first, first_shift, second, second_shift, final, final_shift):
@@ -286,11 +295,13 @@
     near = lax.ppermute(right, both, linear(lambda r, c, i: (r ^ 8, c) if i else (r, 1 - c)))
     own, pairs = spread(left, final, seqs, width)
     pair = arrange(right, near, far, pairs)
-    gathered = [flip(pair, bits) for bits in (2, 4, 6)]
+    first, second, third = [flip(pair, bits) for bits in (2, 4, 6)]
     lefts = [own, spread(beside, final, seqs, width, pairs)]
-    pieces = [pair, *after(gathered, keep(lefts[1]))]
-    pieces += [flip(piece, 1) for piece in pieces]
-    return combine(lefts, pieces, (0, 2, 4, 6, 1, 3, 5, 7), final_shift, seqs)
+    span = 16 * here
+    begun = combine(lefts, [pair, flip(pair, 1)], (0, 1), final_shift, seqs, span, last=False)
+    first, second, third = [after([piece], keep(begun))[0] for piece in (first, second, third)]
+    pieces = [first, flip(first, 1), second, flip(second, 1), third, flip(third, 1)]
+    return combine(lefts, pieces, (2, 3, 4, 5, 6, 7), final_shift, seqs, span, begun)
 
 
 def solution(mesh):

time: 26.3 us -> 24.7 us (0.939)
  waiting for transfers between devices: 4.89 us -> 2.08 us
  Pallas kernels: 11.6 us -> 12.3 us
  starting transfers between devices: 9.64 us -> 10.1 us
    ppermute x7, waiting for transfers between devices: 3.92 us -> 1.12 us  [flip(): return lax.ppermute(value, 'row', [(r, r ^ bits) for r in range(16)])]
    pallas_call x1 -> x2, Pallas kernels: 6.22 us -> 6.87 us  [combine(): pl.pallas_call(functools.partial(combine_kernel, seqs, masks, len(lefts),...]
    ppermute x7, starting transfers between devices: 6.02 us -> 6.5 us  [flip(): return lax.ppermute(value, 'row', [(r, r ^ bits) for r in range(16)])]
  transfers between devices with their start and end apart: 10 -> 10, of which waited for: 6 -> 5; matrix products, arithmetic and copies ran while one was open for 0% -> 0% of each run, Pallas kernels for 14% -> 24%
where the time goes in v3:
time: 24.7 us; the launch traced here: 24.5 us
  Pallas kernels  12.3 us (50%)
  starting transfers between devices  10.1 us (41%)
  waiting for transfers between devices  2.08 us (8%)
    pallas_call x2, Pallas kernels, combine(): pl.pallas_call(functools.partial(combine_kernel, seqs, masks, len(lefts),...  6.87 us
    ppermute x7, starting transfers between devices, flip(): return lax.ppermute(value, 'row', [(r, r ^ bits) for r in range(16)])  6.5 us
    ppermute x1, starting transfers between devices, per_device(): lax.ppermute(right, both, linear(lambda r, c, i: (r ^ 1, c) if i else (r...  2.35 us
    pallas_call x1, Pallas kernels, spread(): pl.pallas_call(functools.partial(spread_first_kernel, seqs, width), out_s...  1.88 us
    pallas_call x1, Pallas kernels, spread(): pl.pallas_call(functools.partial(spread_second_kernel, seqs, width), out_...  1.79 us
    pallas_call x1, Pallas kernels, project(): pl.pallas_call(project_kernel, out_shape=(jax.ShapeDtypeStruct((here, seq...  1.69 us
    ppermute x1, starting transfers between devices, per_device(): beside = lax.ppermute(left, 'col', [(0, 1), (1, 0)])  1.26 us
    ppermute x7, waiting for transfers between devices, flip(): return lax.ppermute(value, 'row', [(r, r ^ bits) for r in range(16)])  1.12 us
  transfers between devices with their start and end apart: 10, of which 5 were waited for; matrix products, arithmetic and copies ran while one was open for 0% of the time, Pallas kernels for 24%

profile of v3, /device:TPU:3, one launch (start us, length us, event | category | flops | bytes accessed | tf_op | source)
XLA Modules:
  0.0 24.5 jit_solution(7531793606516819084)
XLA Ops:
  0.0 1.7 %project.1 = (bf16[24,1024]{1,0:T(8,128)(2,1)S(1)}, bf16[192,128]{1,0:T(8,128)(2,1)S(1)}, bf16[1024,128]{1,0:T(8,128)(2,1)S(1)}) custom-call(bf16[32,24,256]{2,1,0:T(8,128)(2,1)} %refs_0_.1, f32[1,256]{1,0:T(1,128)} %bitcast.11, f32[1,256]{1,0:T(1,128)} %bitcast.12, bf16[32,256]{1,0:T(8,128)(2,1)} %bitcast.9, f32[1,32]{1,0:T(1,128)} %bitcast.13, ...), custom_call_target="tpu_custom_call" | custom-call | flops 100663296 | bytes 393216 | tf_op jit(solution)/shard_map/project/pallas_call | solution.py:160
  1.7 2.3 %collective-permute-start.2 = (bf16[24,1024]{1,0:T(8,128)(2,1)S(1)}, bf16[24,1024]{1,0:T(8,128)(2,1)S(1)}, u32[]{:S(2)}, u32[]{:S(2)}) collective-permute-start(bf16[24,1024]{1,0:T(8,128)(2,1)S(1)} %get-tuple-element.15.own_ref), channel_id=1, source_target_pairs={{0,2},{1,16},{2,0},{3,18},{4,6},{5,20},{6,4},{7,22},{8,10},{9,24},... | collective-permute-start | bytes 147464 | tf_op jit(solution)/shard_map/ppermute | solution.py:293
  4.1 1.3 %collective-permute-start = (bf16[192,128]{1,0:T(8,128)(2,1)S(1)}, bf16[192,128]{1,0:T(8,128)(2,1)S(1)}, u32[]{:S(2)}, u32[]{:S(2)}) collective-permute-start(bf16[192,128]{1,0:T(8,128)(2,1)S(1)} %get-tuple-element.11.l_ref), channel_id=1, source_target_pairs={{0,1},{1,0},{2,3},{3,2},{4,5},{5,4},{6,7},{7,6},{8,9},{9,8},{10,11... | collective-permute-start | bytes 147464 | tf_op jit(solution)/shard_map/ppermute | solution.py:294
  5.3 1.9 %spread_first.1 = (bf16[12,1024,256]{2,1,0:T(8,128)(2,1)S(1)}, bf16[16,32,256]{2,1,0:T(8,128)(2,1)S(1)}) custom-call(bf16[192,128]{1,0:T(8,128)(2,1)S(1)} %get-tuple-element.11.l_ref, bf16[1024,128]{1,0:T(8,128)(2,1)S(1)} %get-tuple-element.12.f_ref), custom_call_target="tpu_custom_call" | custom-call | flops 1610612736 | bytes 49152 | tf_op jit(solution)/shard_map/spread_first/pallas_call | solution.py:185
  7.2 0.0 copy-start
  7.2 0.0 collective-permute-done.2.far_ref
  7.2 1.0 %collective-permute-done.1.near_ref = bf16[24,1024]{1,0:T(8,128)(2,1)S(1)} collective-permute-done((bf16[24,1024]{1,0:T(8,128)(2,1)S(1)}, bf16[24,1024]{1,0:T(8,128)(2,1)S(1)}, u32[]{:S(2)}, u32[]{:S(2)}) %collective-permute-start.1) | collective-permute-done | bytes 49184 | tf_op jit(solution)/shard_map/ppermute | solution.py:295
  8.2 2.1 %collective-permute-start.8 = (bf16[48,1024]{1,0:T(8,128)(2,1)S(1)}, bf16[48,1024]{1,0:T(8,128)(2,1)S(1)}, u32[]{:S(2)}, u32[]{:S(2)}) collective-permute-start(bf16[48,1024]{1,0:T(8,128)(2,1)S(1)} %arrange.1.refs_2_), channel_id=1, source_target_pairs={{0,12},{2,14},{4,8},{6,10},{8,4},{10,6},{12,0},{14,2},{16,28},{18,... | collective-permute-start | bytes 294920 | tf_op jit(solution)/shard_map/ppermute | solution.py:263
  10.3 0.4 %collective-permute-start.6 = (bf16[48,1024]{1,0:T(8,128)(2,1)S(1)}, bf16[48,1024]{1,0:T(8,128)(2,1)S(1)}, u32[]{:S(2)}, u32[]{:S(2)}) collective-permute-start(bf16[48,1024]{1,0:T(8,128)(2,1)S(1)} %arrange.1.refs_2_), channel_id=1, source_target_pairs={{0,8},{2,10},{4,12},{6,14},{8,0},{10,2},{12,4},{14,6},{16,24},{18,... | collective-permute-start | bytes 294920 | tf_op jit(solution)/shard_map/ppermute | solution.py:263
  10.7 2.5 %collective-permute-start.4 = (bf16[48,1024]{1,0:T(8,128)(2,1)S(1)}, bf16[48,1024]{1,0:T(8,128)(2,1)S(1)}, u32[]{:S(2)}, u32[]{:S(2)}) collective-permute-start(bf16[48,1024]{1,0:T(8,128)(2,1)S(1)} %arrange.1.refs_2_), channel_id=1, source_target_pairs={{0,2},{2,0},{4,6},{6,4},{8,10},{10,8},{12,14},{14,12},{16,18},{18,... | collective-permute-start | bytes 294920 | tf_op jit(solution)/shard_map/ppermute | solution.py:263
  13.2 0.2 collective-permute-start.3
  13.4 0.0 collective-permute-done.l_ref
  13.4 1.8 %spread_second.1.refs_1_ = bf16[12,1024,256]{2,1,0:T(8,128)(2,1)S(1)} custom-call(bf16[192,128]{1,0:T(8,128)(2,1)S(1)} %collective-permute-done.l_ref, bf16[16,32,256]{2,1,0:T(8,128)(2,1)S(1)} %get-tuple-element.14.pairs._), custom_call_target="tpu_custom_call" | custom-call | flops 1610612736 | bytes 49152 | tf_op jit(solution)/shard_map/spread_second/pallas_call | solution.py:195
  15.2 0.0 collective-permute-done.4.refs_3_
  15.2 2.2 %combine_some.1.refs_1_.refs_9_ = bf16[24,2,384,128]{3,2,1,0:T(8,128)(2,1)S(1)} custom-call(bf16[12,1024,256]{2,1,0:T(8,128)(2,1)S(1)} %get-tuple-element.13.refs_0_, bf16[12,1024,256]{2,1,0:T(8,128)(2,1)S(1)} %spread_second.1.refs_1_, bf16[48,1024]{1,0:T(8,128)(2,1)S(1)} %arrange.1.refs_2_, bf16[48,1024]{1,0:T(8,128)(2,1)S(1)} %collective-permute-done.4.refs_3_, ...), custom_call_target="tpu_custom_call" | custom-call | flops 1207959552 | bytes 1179648 | tf_op jit(solution)/shard_map/combine_some/pallas_call | solution.py:237
  17.4 0.2 collective-permute-done.3.refs_0_
  17.6 0.8 %collective-permute-start.5 = (bf16[48,1024]{1,0:T(8,128)(2,1)S(1)}, bf16[48,1024]{1,0:T(8,128)(2,1)S(1)}, u32[]{:S(2)}, u32[]{:S(2)}) collective-permute-start(bf16[48,1024]{1,0:T(8,128)(2,1)S(1)} %after.3.refs_2_), channel_id=1, source_target_pairs={{0,2},{2,0},{4,6},{6,4},{8,10},{10,8},{12,14},{14,12},{16,18},{18,... | collective-permute-start | bytes 294920 | tf_op jit(solution)/shard_map/ppermute | solution.py:263
  18.4 0.1 collective-permute-start.7
  18.5 0.0 collective-permute-done.8.refs_0_
  18.5 0.4 %collective-permute-start.9 = (bf16[48,1024]{1,0:T(8,128)(2,1)S(1)}, bf16[48,1024]{1,0:T(8,128)(2,1)S(1)}, u32[]{:S(2)}, u32[]{:S(2)}) collective-permute-start(bf16[48,1024]{1,0:T(8,128)(2,1)S(1)} %after.5.refs_6_), channel_id=1, source_target_pairs={{0,2},{2,0},{4,6},{6,4},{8,10},{10,8},{12,14},{14,12},{16,18},{18,... | collective-permute-start | bytes 294920 | tf_op jit(solution)/shard_map/ppermute | solution.py:263
  18.9 0.4 %collective-permute-done.5.refs_3_ = bf16[48,1024]{1,0:T(8,128)(2,1)S(1)} collective-permute-done((bf16[48,1024]{1,0:T(8,128)(2,1)S(1)}, bf16[48,1024]{1,0:T(8,128)(2,1)S(1)}, u32[]{:S(2)}, u32[]{:S(2)}) %collective-permute-start.5) | collective-permute-done | bytes 98336 | tf_op jit(solution)/shard_map/ppermute | solution.py:263
  19.3 0.4 %collective-permute-done.7.refs_5_ = bf16[48,1024]{1,0:T(8,128)(2,1)S(1)} collective-permute-done((bf16[48,1024]{1,0:T(8,128)(2,1)S(1)}, bf16[48,1024]{1,0:T(8,128)(2,1)S(1)}, u32[]{:S(2)}, u32[]{:S(2)}) %collective-permute-start.7) | collective-permute-done | bytes 98336 | tf_op jit(solution)/shard_map/ppermute | solution.py:263
  19.7 0.2 collective-permute-done.9.refs_7_
  19.9 4.7 %combine_last.1 = (bf16[48,384,128]{2,1,0:T(8,128)(2,1)}, bf16[24,2,384,128]{3,2,1,0:T(8,128)(2,1)S(1)}) custom-call(bf16[12,1024,256]{2,1,0:T(8,128)(2,1)S(1)} %get-tuple-element.13.refs_0_, bf16[12,1024,256]{2,1,0:T(8,128)(2,1)S(1)} %spread_second.1.refs_1_, bf16[48,1024]{1,0:T(8,128)(2,1)S(1)} %after.3.refs_2_, ...), custom_call_target="tpu_custom_call", output_to_operand_aliasing={{1}: (9, {})} | custom-call | flops 3623878656 | bytes 3538944 | tf_op jit(solution)/shard_map/combine_last/pallas_call | solution.py:237
  (7 shorter events, 0.0 us)
Async XLA Ops:
  1.7 5.5 %collective-permute-start.2 = (bf16[24,1024]{1,0:T(8,128)(2,1)S(1)}, bf16[24,1024]{1,0:T(8,128)(2,1)S(1)}, u32[]{:S(2)}, u32[]{:S(2)}) collective-permute-start(bf16[24,1024]{1,0:T(8,128)(2,1)S(1)} %get-tuple-element.15.own_ref), channel_id=1, source_target_pairs={{0,2},{1,16},{2,0},{3,18},{4,6},{5,20},{6,4},{7,22},{8,10},{9,24},... | collective-permute-start | bytes 147464 | tf_op jit(solution)/shard_map/ppermute | solution.py:293
  4.0 4.1 %collective-permute-start.1 = (bf16[24,1024]{1,0:T(8,128)(2,1)S(1)}, bf16[24,1024]{1,0:T(8,128)(2,1)S(1)}, u32[]{:S(2)}, u32[]{:S(2)}) collective-permute-start(bf16[24,1024]{1,0:T(8,128)(2,1)S(1)} %get-tuple-element.15.own_ref), channel_id=1, source_target_pairs={{0,16},{1,0},{2,18},{3,2},{4,20},{5,4},{6,22},{7,6},{8,24},{9,8},{... | collective-permute-start | bytes 147464 | tf_op jit(solution)/shard_map/ppermute | solution.py:295
  4.1 9.4 %collective-permute-start = (bf16[192,128]{1,0:T(8,128)(2,1)S(1)}, bf16[192,128]{1,0:T(8,128)(2,1)S(1)}, u32[]{:S(2)}, u32[]{:S(2)}) collective-permute-start(bf16[192,128]{1,0:T(8,128)(2,1)S(1)} %get-tuple-element.11.l_ref), channel_id=1, source_target_pairs={{0,1},{1,0},{2,3},{3,2},{4,5},{5,4},{6,7},{7,6},{8,9},{9,8},{10,11... | collective-permute-start | bytes 147464 | tf_op jit(solution)/shard_map/ppermute | solution.py:294
  7.2 8.0 %copy-start = (f32[128]{0:T(128)S(1)}, f32[128]{0:T(128)}, u32[]{:S(2)}) copy-start(f32[128]{0:T(128)} %param.17) | copy-start | bytes 1540
  8.2 10.3 %collective-permute-start.8 = (bf16[48,1024]{1,0:T(8,128)(2,1)S(1)}, bf16[48,1024]{1,0:T(8,128)(2,1)S(1)}, u32[]{:S(2)}, u32[]{:S(2)}) collective-permute-start(bf16[48,1024]{1,0:T(8,128)(2,1)S(1)} %arrange.1.refs_2_), channel_id=1, source_target_pairs={{0,12},{2,14},{4,8},{6,10},{8,4},{10,6},{12,0},{14,2},{16,28},{18,... | collective-permute-start | bytes 294920 | tf_op jit(solution)/shard_map/ppermute | solution.py:263
  10.3 8.1 %collective-permute-start.6 = (bf16[48,1024]{1,0:T(8,128)(2,1)S(1)}, bf16[48,1024]{1,0:T(8,128)(2,1)S(1)}, u32[]{:S(2)}, u32[]{:S(2)}) collective-permute-start(bf16[48,1024]{1,0:T(8,128)(2,1)S(1)} %arrange.1.refs_2_), channel_id=1, source_target_pairs={{0,8},{2,10},{4,12},{6,14},{8,0},{10,2},{12,4},{14,6},{16,24},{18,... | collective-permute-start | bytes 294920 | tf_op jit(solution)/shard_map/ppermute | solution.py:263
  10.7 4.5 %collective-permute-start.4 = (bf16[48,1024]{1,0:T(8,128)(2,1)S(1)}, bf16[48,1024]{1,0:T(8,128)(2,1)S(1)}, u32[]{:S(2)}, u32[]{:S(2)}) collective-permute-start(bf16[48,1024]{1,0:T(8,128)(2,1)S(1)} %arrange.1.refs_2_), channel_id=1, source_target_pairs={{0,2},{2,0},{4,6},{6,4},{8,10},{10,8},{12,14},{14,12},{16,18},{18,... | collective-permute-start | bytes 294920 | tf_op jit(solution)/shard_map/ppermute | solution.py:263
  13.2 4.4 %collective-permute-start.3 = (bf16[48,1024]{1,0:T(8,128)(2,1)S(1)}, bf16[48,1024]{1,0:T(8,128)(2,1)S(1)}, u32[]{:S(2)}, u32[]{:S(2)}) collective-permute-start(bf16[48,1024]{1,0:T(8,128)(2,1)S(1)} %arrange.1.refs_2_), channel_id=1, source_target_pairs={{0,4},{2,6},{4,0},{6,2},{8,12},{10,14},{12,8},{14,10},{16,20},{18,... | collective-permute-start | bytes 294920 | tf_op jit(solution)/shard_map/ppermute | solution.py:263
  17.6 1.7 %collective-permute-start.5 = (bf16[48,1024]{1,0:T(8,128)(2,1)S(1)}, bf16[48,1024]{1,0:T(8,128)(2,1)S(1)}, u32[]{:S(2)}, u32[]{:S(2)}) collective-permute-start(bf16[48,1024]{1,0:T(8,128)(2,1)S(1)} %after.3.refs_2_), channel_id=1, source_target_pairs={{0,2},{2,0},{4,6},{6,4},{8,10},{10,8},{12,14},{14,12},{16,18},{18,... | collective-permute-start | bytes 294920 | tf_op jit(solution)/shard_map/ppermute | solution.py:263
  18.4 1.3 %collective-permute-start.7 = (bf16[48,1024]{1,0:T(8,128)(2,1)S(1)}, bf16[48,1024]{1,0:T(8,128)(2,1)S(1)}, u32[]{:S(2)}, u32[]{:S(2)}) collective-permute-start(bf16[48,1024]{1,0:T(8,128)(2,1)S(1)} %after.4.refs_4_), channel_id=1, source_target_pairs={{0,2},{2,0},{4,6},{6,4},{8,10},{10,8},{12,14},{14,12},{16,18},{18,... | collective-permute-start | bytes 294920 | tf_op jit(solution)/shard_map/ppermute | solution.py:263
  18.5 1.4 %collective-permute-start.9 = (bf16[48,1024]{1,0:T(8,128)(2,1)S(1)}, bf16[48,1024]{1,0:T(8,128)(2,1)S(1)}, u32[]{:S(2)}, u32[]{:S(2)}) collective-permute-start(bf16[48,1024]{1,0:T(8,128)(2,1)S(1)} %after.5.refs_6_), channel_id=1, source_target_pairs={{0,2},{2,0},{4,6},{6,4},{8,10},{10,8},{12,14},{14,12},{16,18},{18,... | collective-permute-start | bytes 294920 | tf_op jit(solution)/shard_map/ppermute | solution.py:263

commit v4 on v3

--- a/solution.py
+++ b/solution.py
@@ -99,9 +99,10 @@
     pass
 
 
-def combine_kernel(seqs, masks, n_left, last, *refs):
+def combine_kernel(seqs, masks, n_left, offset, last, skip, *refs):
+    refs = refs[skip:]
+    shift_ref, *refs = refs
     lefts, pieces = refs[:n_left], refs[n_left : n_left + len(masks)]
-    shift_ref, refs = refs[n_left + len(masks)], refs[n_left + len(masks) + 1 :]
     stage, right = refs[-3], refs[-2]
     rows = pieces[0].shape[0]
     pairs = lefts[0].shape[0]
@@ -127,8 +128,8 @@
                 update = jnp.dot(right[...], left[p], preferred_element_type=F32) * (1.0 / seqs) + shift
                 for k, place in enumerate(places):
                     block = update[k * run : (k + 1) * run].astype(BF16)
-                    stage[h * pairs + p, 0, pl.ds(place, run)] = block[:, :LANES]
-                    stage[h * pairs + p, 1, pl.ds(place, run)] = block[:, LANES:]
+                    stage[offset + h * pairs + p, 0, pl.ds(place, run)] = block[:, :LANES]
+                    stage[offset + h * pairs + p, 1, pl.ds(place, run)] = block[:, LANES:]
                 if last:
                     out_ref, sem = refs[-4], refs[-1]
                     pltpu.make_async_copy(stage.at[h * pairs + p], out_ref.at[pl.ds(first + 2 * p, 2)], sem).start()
@@ -227,23 +228,25 @@
     )(*values, *earlier)
 
 
-def combine(lefts, pieces, masks, final_shift, seqs, span, begun=None, last=True):
+def combine(lefts, pieces, masks, final_shift, seqs, span, begun=None, offset=0, total=None, follow=()):
+    last = total is None
     pairs, depth, _ = lefts[0].shape
     rows = pieces[0].shape[0] * len(pieces)
-    total = 2 * pairs * len(lefts)
+    total = total or 2 * pairs * len(lefts)
     stage = pltpu.VMEM((total // 2, 2, span, LANES), BF16)
-    args = [*[keep(left) for left in lefts], *pieces, final_shift[None]] + ([] if begun is None else [keep(begun)])
+    first = ([] if begun is None else [keep(begun)]) + [*follow]
+    args = [*first, final_shift[None], *[keep(left) for left in lefts], *pieces]
     outs = ([jax.ShapeDtypeStruct((total, span, LANES), BF16)] if last else []) + [stage]
     return pl.pallas_call(
-        functools.partial(combine_kernel, seqs, masks, len(lefts), last),
+        functools.partial(combine_kernel, seqs, masks, len(lefts), offset, last, len(first)),
         out_shape=outs,
         in_specs=[VMEM] * len(args),
         out_specs=[HBM, VMEM] if last else [VMEM],
-        input_output_aliases={} if begun is None else {len(args) - 1: len(outs) - 1},
+        input_output_aliases={} if begun is None else {0: len(outs) - 1},
         scratch_shapes=[pltpu.VMEM((rows, depth), BF16), pltpu.SemaphoreType.DMA],
         compiler_params=params(),
         cost_estimate=pl.CostEstimate(
-            flops=2 * total * rows * LANES * depth, bytes_accessed=total * rows * LANES * 2, transcendentals=0
+            flops=4 * pairs * len(lefts) * rows * LANES * depth, bytes_accessed=0, transcendentals=0
         ),
         name="combine_last" if last else "combine_some",
     )(*args)[0]
@@ -291,15 +294,17 @@
     right, left, final = project(x, gain, shift, first, first_shift, second, second_shift, final)
     both = ("row", "col")
     far = lax.ppermute(right, both, linear(lambda r, c, i: (r ^ 1, c) if i else (r ^ 8, 1 - c)))
-    beside = lax.ppermute(left, "col", [(0, 1), (1, 0)])
     near = lax.ppermute(right, both, linear(lambda r, c, i: (r ^ 8, c) if i else (r, 1 - c)))
     own, pairs = spread(left, final, seqs, width)
+    beside = lax.ppermute(after([left], keep(pairs))[0], "col", [(0, 1), (1, 0)])
     pair = arrange(right, near, far, pairs)
     first, second, third = [flip(pair, bits) for bits in (2, 4, 6)]
     lefts = [own, spread(beside, final, seqs, width, pairs)]
     span = 16 * here
-    begun = combine(lefts, [pair, flip(pair, 1)], (0, 1), final_shift, seqs, span, last=False)
-    first, second, third = [after([piece], keep(begun))[0] for piece in (first, second, third)]
+    some, masks, total = [pair, flip(pair, 1)], (0, 1), 2 * here
+    begun = combine(lefts[:1], some, masks, final_shift, seqs, span, None, 0, total)
+    first, second, third = after([first, second, third], keep(begun), keep(lefts[1]))
+    begun = combine(lefts[1:], some, masks, final_shift, seqs, span, begun, here // 2, total, [first])
     pieces = [first, flip(first, 1), second, flip(second, 1), third, flip(third, 1)]
     return combine(lefts, pieces, (2, 3, 4, 5, 6, 7), final_shift, seqs, span, begun)
 

time: 24.7 us -> 24.4 us (0.988)
  waiting for transfers between devices: 2.08 us -> 0.91 us
  starting transfers between devices: 10.1 us -> 10.7 us
    ppermute x7, waiting for transfers between devices: 1.12 us -> 0.02 us  [flip(): return lax.ppermute(value, 'row', [(r, r ^ bits) for r in range(16)])]
    ppermute x7, starting transfers between devices: 6.5 us -> 7.06 us  [flip(): return lax.ppermute(value, 'row', [(r, r ^ bits) for r in range(16)])]
    pallas_call x2 -> x3, Pallas kernels: 6.87 us -> 7.04 us  [combine(): pl.pallas_call(functools.partial(combine_kernel, seqs, masks, len(lefts),...]
  transfers between devices with their start and end apart: 10 -> 10, of which waited for: 5 -> 1; matrix products, arithmetic and copies ran while one was open for 0% -> 0% of each run, Pallas kernels for 24% -> 25%
where the time goes in v4:
time: 24.4 us; the launch traced here: 24.2 us
  Pallas kernels  12.4 us (51%)
  starting transfers between devices  10.7 us (44%)
  waiting for transfers between devices  0.91 us (4%)
    ppermute x7, starting transfers between devices, flip(): return lax.ppermute(value, 'row', [(r, r ^ bits) for r in range(16)])  7.06 us
    pallas_call x3, Pallas kernels, combine(): pl.pallas_call(functools.partial(combine_kernel, seqs, masks, len(lefts),...  7.04 us
    ppermute x1, starting transfers between devices, per_device(): lax.ppermute(right, both, linear(lambda r, c, i: (r ^ 1, c) if i else (r...  2.35 us
    pallas_call x1, Pallas kernels, spread(): pl.pallas_call(functools.partial(spread_first_kernel, seqs, width), out_s...  1.88 us
    pallas_call x1, Pallas kernels, spread(): pl.pallas_call(functools.partial(spread_second_kernel, seqs, width), out_...  1.79 us
    pallas_call x1, Pallas kernels, project(): pl.pallas_call(project_kernel, out_shape=(jax.ShapeDtypeStruct((here, seq...  1.69 us
    ppermute x1, starting transfers between devices, per_device(): lax.ppermute(after([left], keep(pairs))[0], 'col', [(0, 1), (1, 0)])  1.33 us
    ppermute x1, waiting for transfers between devices, per_device(): lax.ppermute(right, both, linear(lambda r, c, i: (r ^ 8, c) if i else (r,...  0.89 us
  transfers between devices with their start and end apart: 10, of which 1 were waited for; matrix products, arithmetic and copies ran while one was open for 0% of the time, Pallas kernels for 25%

profile of v4, /device:TPU:3, one launch (start us, length us, event | category | flops | bytes accessed | tf_op | source)
XLA Modules:
  0.0 24.2 jit_solution(13436016367613232959)
XLA Ops:
  0.0 1.7 %project.1 = (bf16[24,1024]{1,0:T(8,128)(2,1)S(1)}, bf16[192,128]{1,0:T(8,128)(2,1)S(1)}, bf16[1024,128]{1,0:T(8,128)(2,1)S(1)}) custom-call(bf16[32,24,256]{2,1,0:T(8,128)(2,1)} %refs_0_.1, f32[1,256]{1,0:T(1,128)} %bitcast.12, f32[1,256]{1,0:T(1,128)} %bitcast.13, bf16[32,256]{1,0:T(8,128)(2,1)} %bitcast.10, f32[1,32]{1,0:T(1,128)} %bitcast.14, ...), custom_call_target="tpu_custom_call" | custom-call | flops 100663296 | bytes 393216 | tf_op jit(solution)/shard_map/project/pallas_call | solution.py:161
  1.7 2.3 %collective-permute-start.1 = (bf16[24,1024]{1,0:T(8,128)(2,1)S(1)}, bf16[24,1024]{1,0:T(8,128)(2,1)S(1)}, u32[]{:S(2)}, u32[]{:S(2)}) collective-permute-start(bf16[24,1024]{1,0:T(8,128)(2,1)S(1)} %get-tuple-element.17.own_ref), channel_id=1, source_target_pairs={{0,2},{1,16},{2,0},{3,18},{4,6},{5,20},{6,4},{7,22},{8,10},{9,24},... | collective-permute-start | bytes 147464 | tf_op jit(solution)/shard_map/ppermute | solution.py:296
  4.0 0.0 collective-permute-start
  4.1 1.9 %spread_first.1 = (bf16[12,1024,256]{2,1,0:T(8,128)(2,1)S(1)}, bf16[16,32,256]{2,1,0:T(8,128)(2,1)S(1)}) custom-call(bf16[192,128]{1,0:T(8,128)(2,1)S(1)} %get-tuple-element.14.l_ref.refs_0_, bf16[1024,128]{1,0:T(8,128)(2,1)S(1)} %get-tuple-element.15.f_ref), custom_call_target="tpu_custom_call" | custom-call | flops 1610612736 | bytes 49152 | tf_op jit(solution)/shard_map/spread_first/pallas_call | solution.py:186
  5.9 0.0 copy-start
  6.0 1.3 %collective-permute-start.6 = (bf16[192,128]{1,0:T(8,128)(2,1)S(1)}, bf16[192,128]{1,0:T(8,128)(2,1)S(1)}, u32[]{:S(2)}, u32[]{:S(2)}) collective-permute-start(bf16[192,128]{1,0:T(8,128)(2,1)S(1)} %after.2), channel_id=1, source_target_pairs={{0,1},{1,0},{2,3},{3,2},{4,5},{5,4},{6,7},{7,6},{8,9},{9,8},{10,11... | collective-permute-start | bytes 147464 | tf_op jit(solution)/shard_map/ppermute | solution.py:299
  7.3 0.0 collective-permute-done.1.far_ref
  7.3 0.9 %collective-permute-done.near_ref = bf16[24,1024]{1,0:T(8,128)(2,1)S(1)} collective-permute-done((bf16[24,1024]{1,0:T(8,128)(2,1)S(1)}, bf16[24,1024]{1,0:T(8,128)(2,1)S(1)}, u32[]{:S(2)}, u32[]{:S(2)}) %collective-permute-start) | collective-permute-done | bytes 49184 | tf_op jit(solution)/shard_map/ppermute | solution.py:297
  8.2 2.1 %collective-permute-start.5 = (bf16[48,1024]{1,0:T(8,128)(2,1)S(1)}, bf16[48,1024]{1,0:T(8,128)(2,1)S(1)}, u32[]{:S(2)}, u32[]{:S(2)}) collective-permute-start(bf16[48,1024]{1,0:T(8,128)(2,1)S(1)} %arrange.1.refs_2_.refs_4_), channel_id=1, source_target_pairs={{0,12},{2,14},{4,8},{6,10},{8,4},{10,6},{12,0},{14,2},{16,28},{18,... | collective-permute-start | bytes 294920 | tf_op jit(solution)/shard_map/ppermute | solution.py:266
  10.3 0.4 %collective-permute-start.4 = (bf16[48,1024]{1,0:T(8,128)(2,1)S(1)}, bf16[48,1024]{1,0:T(8,128)(2,1)S(1)}, u32[]{:S(2)}, u32[]{:S(2)}) collective-permute-start(bf16[48,1024]{1,0:T(8,128)(2,1)S(1)} %arrange.1.refs_2_.refs_4_), channel_id=1, source_target_pairs={{0,8},{2,10},{4,12},{6,14},{8,0},{10,2},{12,4},{14,6},{16,24},{18,... | collective-permute-start | bytes 294920 | tf_op jit(solution)/shard_map/ppermute | solution.py:266
  10.7 0.2 collective-permute-start.3
  10.9 2.8 %collective-permute-start.2 = (bf16[48,1024]{1,0:T(8,128)(2,1)S(1)}, bf16[48,1024]{1,0:T(8,128)(2,1)S(1)}, u32[]{:S(2)}, u32[]{:S(2)}) collective-permute-start(bf16[48,1024]{1,0:T(8,128)(2,1)S(1)} %arrange.1.refs_2_.refs_4_), channel_id=1, source_target_pairs={{0,2},{2,0},{4,6},{6,4},{8,10},{10,8},{12,14},{14,12},{16,18},{18,... | collective-permute-start | bytes 294920 | tf_op jit(solution)/shard_map/ppermute | solution.py:266
  13.7 1.8 %spread_second.1.refs_4_.refs_3_ = bf16[12,1024,256]{2,1,0:T(8,128)(2,1)S(1)} custom-call(bf16[192,128]{1,0:T(8,128)(2,1)S(1)} %collective-permute-done.6.l_ref, bf16[16,32,256]{2,1,0:T(8,128)(2,1)S(1)} %get-tuple-element.18._.refs_1_.pairs), custom_call_target="tpu_custom_call" | custom-call | flops 1610612736 | bytes 49152 | tf_op jit(solution)/shard_map/spread_second/pallas_call | solution.py:196
  15.5 0.0 collective-permute-done.2.refs_3_.refs_5_
  15.5 1.2 %combine_some.2.refs_3_.refs_0_ = bf16[24,2,384,128]{3,2,1,0:T(8,128)(2,1)S(1)} custom-call(f32[1,128]{1,0:T(1,128)S(1)} %bitcast.7, bf16[12,1024,256]{2,1,0:T(8,128)(2,1)S(1)} %get-tuple-element.16.refs_1_.refs_2_, bf16[48,1024]{1,0:T(8,128)(2,1)S(1)} %arrange.1.refs_2_.refs_4_, bf16[48,1024]{1,0:T(8,128)(2,1)S(1)} %collective-permute-done.2.refs_3_.refs_5_), custom_call_target="tpu_custom_call" | custom-call | flops 603979776 | tf_op jit(solution)/shard_map/combine_some/pallas_call | solution.py:240
  16.7 0.0 collective-permute-done.4.refs_1_
  16.7 0.0 collective-permute-done.3.refs_0_
  16.7 1.1 %collective-permute-start.8 = (bf16[48,1024]{1,0:T(8,128)(2,1)S(1)}, bf16[48,1024]{1,0:T(8,128)(2,1)S(1)}, u32[]{:S(2)}, u32[]{:S(2)}) collective-permute-start(bf16[48,1024]{1,0:T(8,128)(2,1)S(1)} %get-tuple-element.20.refs_6_), channel_id=1, source_target_pairs={{0,2},{2,0},{4,6},{6,4},{8,10},{10,8},{12,14},{14,12},{16,18},{18,... | collective-permute-start | bytes 294920 | tf_op jit(solution)/shard_map/ppermute | solution.py:266
  17.8 0.0 collective-permute-start.9
  17.8 0.5 %collective-permute-start.7 = (bf16[48,1024]{1,0:T(8,128)(2,1)S(1)}, bf16[48,1024]{1,0:T(8,128)(2,1)S(1)}, u32[]{:S(2)}, u32[]{:S(2)}) collective-permute-start(bf16[48,1024]{1,0:T(8,128)(2,1)S(1)} %get-tuple-element.19.refs_1_.refs_4_), channel_id=1, source_target_pairs={{0,2},{2,0},{4,6},{6,4},{8,10},{10,8},{12,14},{14,12},{16,18},{18,... | collective-permute-start | bytes 294920 | tf_op jit(solution)/shard_map/ppermute | solution.py:266
  18.3 1.2 %combine_some.3.refs_0_ = bf16[24,2,384,128]{3,2,1,0:T(8,128)(2,1)S(1)} custom-call(bf16[24,2,384,128]{3,2,1,0:T(8,128)(2,1)S(1)} %combine_some.2.refs_3_.refs_0_, bf16[48,1024]{1,0:T(8,128)(2,1)S(1)} %get-tuple-element.19.refs_1_.refs_4_, f32[1,128]{1,0:T(1,128)S(1)} %bitcast.8, ...), custom_call_target="tpu_custom_call", output_to_operand_aliasing={{}: (0, {})} | custom-call | flops 603979776 | tf_op jit(solution)/shard_map/combine_some/pallas_call | solution.py:240
  19.5 0.0 collective-permute-done.9.refs_9_
  19.5 0.0 collective-permute-done.7.refs_5_
  19.5 4.7 %combine_last.1 = (bf16[48,384,128]{2,1,0:T(8,128)(2,1)}, bf16[24,2,384,128]{3,2,1,0:T(8,128)(2,1)S(1)}) custom-call(bf16[24,2,384,128]{3,2,1,0:T(8,128)(2,1)S(1)} %combine_some.3.refs_0_, f32[1,128]{1,0:T(1,128)S(1)} %bitcast.9, bf16[12,1024,256]{2,1,0:T(8,128)(2,1)S(1)} %get-tuple-element.16.refs_1_.refs_2_, ...), custom_call_target="tpu_custom_call", output_to_operand_aliasing={{1}: (0, {})} | custom-call | flops 3623878656 | tf_op jit(solution)/shard_map/combine_last/pallas_call | solution.py:240
  (7 shorter events, 0.0 us)
Async XLA Ops:
  1.7 5.6 %collective-permute-start.1 = (bf16[24,1024]{1,0:T(8,128)(2,1)S(1)}, bf16[24,1024]{1,0:T(8,128)(2,1)S(1)}, u32[]{:S(2)}, u32[]{:S(2)}) collective-permute-start(bf16[24,1024]{1,0:T(8,128)(2,1)S(1)} %get-tuple-element.17.own_ref), channel_id=1, source_target_pairs={{0,2},{1,16},{2,0},{3,18},{4,6},{5,20},{6,4},{7,22},{8,10},{9,24},... | collective-permute-start | bytes 147464 | tf_op jit(solution)/shard_map/ppermute | solution.py:296
  4.0 4.1 %collective-permute-start = (bf16[24,1024]{1,0:T(8,128)(2,1)S(1)}, bf16[24,1024]{1,0:T(8,128)(2,1)S(1)}, u32[]{:S(2)}, u32[]{:S(2)}) collective-permute-start(bf16[24,1024]{1,0:T(8,128)(2,1)S(1)} %get-tuple-element.17.own_ref), channel_id=1, source_target_pairs={{0,16},{1,0},{2,18},{3,2},{4,20},{5,4},{6,22},{7,6},{8,24},{9,8},{... | collective-permute-start | bytes 147464 | tf_op jit(solution)/shard_map/ppermute | solution.py:297
  5.9 9.6 %copy-start = (f32[128]{0:T(128)S(1)}, f32[128]{0:T(128)}, u32[]{:S(2)}) copy-start(f32[128]{0:T(128)} %param.17) | copy-start | bytes 1540
  6.0 7.7 %collective-permute-start.6 = (bf16[192,128]{1,0:T(8,128)(2,1)S(1)}, bf16[192,128]{1,0:T(8,128)(2,1)S(1)}, u32[]{:S(2)}, u32[]{:S(2)}) collective-permute-start(bf16[192,128]{1,0:T(8,128)(2,1)S(1)} %after.2), channel_id=1, source_target_pairs={{0,1},{1,0},{2,3},{3,2},{4,5},{5,4},{6,7},{7,6},{8,9},{9,8},{10,11... | collective-permute-start | bytes 147464 | tf_op jit(solution)/shard_map/ppermute | solution.py:299
  8.2 8.5 %collective-permute-start.5 = (bf16[48,1024]{1,0:T(8,128)(2,1)S(1)}, bf16[48,1024]{1,0:T(8,128)(2,1)S(1)}, u32[]{:S(2)}, u32[]{:S(2)}) collective-permute-start(bf16[48,1024]{1,0:T(8,128)(2,1)S(1)} %arrange.1.refs_2_.refs_4_), channel_id=1, source_target_pairs={{0,12},{2,14},{4,8},{6,10},{8,4},{10,6},{12,0},{14,2},{16,28},{18,... | collective-permute-start | bytes 294920 | tf_op jit(solution)/shard_map/ppermute | solution.py:266
  10.3 6.4 %collective-permute-start.4 = (bf16[48,1024]{1,0:T(8,128)(2,1)S(1)}, bf16[48,1024]{1,0:T(8,128)(2,1)S(1)}, u32[]{:S(2)}, u32[]{:S(2)}) collective-permute-start(bf16[48,1024]{1,0:T(8,128)(2,1)S(1)} %arrange.1.refs_2_.refs_4_), channel_id=1, source_target_pairs={{0,8},{2,10},{4,12},{6,14},{8,0},{10,2},{12,4},{14,6},{16,24},{18,... | collective-permute-start | bytes 294920 | tf_op jit(solution)/shard_map/ppermute | solution.py:266
  10.7 6.0 %collective-permute-start.3 = (bf16[48,1024]{1,0:T(8,128)(2,1)S(1)}, bf16[48,1024]{1,0:T(8,128)(2,1)S(1)}, u32[]{:S(2)}, u32[]{:S(2)}) collective-permute-start(bf16[48,1024]{1,0:T(8,128)(2,1)S(1)} %arrange.1.refs_2_.refs_4_), channel_id=1, source_target_pairs={{0,4},{2,6},{4,0},{6,2},{8,12},{10,14},{12,8},{14,10},{16,20},{18,... | collective-permute-start | bytes 294920 | tf_op jit(solution)/shard_map/ppermute | solution.py:266
  10.9 4.6 %collective-permute-start.2 = (bf16[48,1024]{1,0:T(8,128)(2,1)S(1)}, bf16[48,1024]{1,0:T(8,128)(2,1)S(1)}, u32[]{:S(2)}, u32[]{:S(2)}) collective-permute-start(bf16[48,1024]{1,0:T(8,128)(2,1)S(1)} %arrange.1.refs_2_.refs_4_), channel_id=1, source_target_pairs={{0,2},{2,0},{4,6},{6,4},{8,10},{10,8},{12,14},{14,12},{16,18},{18,... | collective-permute-start | bytes 294920 | tf_op jit(solution)/shard_map/ppermute | solution.py:266
  16.7 2.8 %collective-permute-start.8 = (bf16[48,1024]{1,0:T(8,128)(2,1)S(1)}, bf16[48,1024]{1,0:T(8,128)(2,1)S(1)}, u32[]{:S(2)}, u32[]{:S(2)}) collective-permute-start(bf16[48,1024]{1,0:T(8,128)(2,1)S(1)} %get-tuple-element.20.refs_6_), channel_id=1, source_target_pairs={{0,2},{2,0},{4,6},{6,4},{8,10},{10,8},{12,14},{14,12},{16,18},{18,... | collective-permute-start | bytes 294920 | tf_op jit(solution)/shard_map/ppermute | solution.py:266
  17.8 1.7 %collective-permute-start.9 = (bf16[48,1024]{1,0:T(8,128)(2,1)S(1)}, bf16[48,1024]{1,0:T(8,128)(2,1)S(1)}, u32[]{:S(2)}, u32[]{:S(2)}) collective-permute-start(bf16[48,1024]{1,0:T(8,128)(2,1)S(1)} %get-tuple-element.21.refs_8_), channel_id=1, source_target_pairs={{0,2},{2,0},{4,6},{6,4},{8,10},{10,8},{12,14},{14,12},{16,18},{18,... | collective-permute-start | bytes 294920 | tf_op jit(solution)/shard_map/ppermute | solution.py:266
  17.8 1.7 %collective-permute-start.7 = (bf16[48,1024]{1,0:T(8,128)(2,1)S(1)}, bf16[48,1024]{1,0:T(8,128)(2,1)S(1)}, u32[]{:S(2)}, u32[]{:S(2)}) collective-permute-start(bf16[48,1024]{1,0:T(8,128)(2,1)S(1)} %get-tuple-element.19.refs_1_.refs_4_), channel_id=1, source_target_pairs={{0,2},{2,0},{4,6},{6,4},{8,10},{10,8},{12,14},{14,12},{16,18},{18,... | collective-permute-start | bytes 294920 | tf_op jit(solution)/shard_map/ppermute | solution.py:266

commit v5 on v4

--- a/solution.py
+++ b/solution.py
@@ -99,37 +99,31 @@
     pass
 
 
-def combine_kernel(seqs, masks, n_left, offset, last, skip, *refs):
-    refs = refs[skip:]
-    shift_ref, *refs = refs
-    lefts, pieces = refs[:n_left], refs[n_left : n_left + len(masks)]
-    stage, right = refs[-3], refs[-2]
+def combine_kernel(seqs, masks, counts, offset, last, begun, *refs):
+    refs = refs[begun:]
+    lefts, pieces = refs[1 : 1 + len(counts)], refs[1 + len(counts) : 1 + len(counts) + len(masks)]
+    shift_ref, stage, right = refs[0], refs[-3], refs[-2]
     rows = pieces[0].shape[0]
     pairs = lefts[0].shape[0]
-    count = stage.shape[2] // rows
-    spot = lax.rem(lax.axis_index("row"), count) if count > 1 else 0
-    run = 2 * rows if count > 1 else rows
-    for n, (mask, piece) in enumerate(zip(masks, pieces)):
-        start = (n // 2 * 2 + jnp.bitwise_and(jnp.bitwise_xor(spot, mask), 1)) * rows if count > 1 else 0
-        right[pl.ds(pl.multiple_of(start, rows), rows), :] = piece[...]
+    spots = stage.shape[2] // rows
+    spot = lax.rem(lax.axis_index("row"), spots) if spots > 1 else 0
+    places = [pl.multiple_of(jnp.bitwise_xor(spot, mask) * rows, rows) if spots > 1 else 0 for mask in masks]
+    for n, piece in enumerate(pieces):
+        right[n * rows : (n + 1) * rows, :] = piece[...]
     shift = jnp.concatenate([shift_ref[...]] * 2, axis=1)
     unroll = next(u for u in (12, 6, 4, 3, 2, 1) if pairs % u == 0)
-    places = [
-        pl.multiple_of(jnp.bitwise_xor(spot, masks[n]) // 2 * run, run) if count > 1 else 0
-        for n in range(0, len(masks), 2)
-    ]
-
-    for h, left in enumerate(lefts):
-        first = 2 * pairs * (jnp.bitwise_xor(lax.axis_index("col"), h) if n_left > 1 else 0)
-
-        def step(n, carry, left=left, first=first, h=h):
+
+    for h, (left, count) in enumerate(zip(lefts, counts)):
+        first = 2 * pairs * (jnp.bitwise_xor(lax.axis_index("col"), h) if len(lefts) > 1 else 0)
+
+        def step(n, carry, left=left, first=first, count=count, h=h):
             for u in range(unroll):
                 p = n * unroll + u
-                update = jnp.dot(right[...], left[p], preferred_element_type=F32) * (1.0 / seqs) + shift
-                for k, place in enumerate(places):
-                    block = update[k * run : (k + 1) * run].astype(BF16)
-                    stage[offset + h * pairs + p, 0, pl.ds(place, run)] = block[:, :LANES]
-                    stage[offset + h * pairs + p, 1, pl.ds(place, run)] = block[:, LANES:]
+                update = jnp.dot(right[: count * rows, :], left[p], preferred_element_type=F32) * (1.0 / seqs) + shift
+                for k, place in enumerate(places[:count]):
+                    block = update[k * rows : (k + 1) * rows].astype(BF16)
+                    stage[offset + h * pairs + p, 0, pl.ds(place, rows)] = block[:, :LANES]
+                    stage[offset + h * pairs + p, 1, pl.ds(place, rows)] = block[:, LANES:]
                 if last:
                     out_ref, sem = refs[-4], refs[-1]
                     pltpu.make_async_copy(stage.at[h * pairs + p], out_ref.at[pl.ds(first + 2 * p, 2)], sem).start()
@@ -192,7 +186,7 @@
             compiler_params=params(),
             cost_estimate=cost,
             name="spread_first",
-        )(left, keep(final))
+        )(left, final)
     return pl.pallas_call(
         functools.partial(spread_second_kernel, seqs, width),
         out_shape=wide,
@@ -228,25 +222,25 @@
     )(*values, *earlier)
 
 
-def combine(lefts, pieces, masks, final_shift, seqs, span, begun=None, offset=0, total=None, follow=()):
+def combine(lefts, pieces, masks, counts, final_shift, seqs, span, begun=None, offset=0, total=None):
     last = total is None
     pairs, depth, _ = lefts[0].shape
-    rows = pieces[0].shape[0] * len(pieces)
+    rows = pieces[0].shape[0]
     total = total or 2 * pairs * len(lefts)
     stage = pltpu.VMEM((total // 2, 2, span, LANES), BF16)
-    first = ([] if begun is None else [keep(begun)]) + [*follow]
-    args = [*first, final_shift[None], *[keep(left) for left in lefts], *pieces]
+    args = [] if begun is None else [keep(begun)]
+    args += [final_shift[None], *[keep(left) for left in lefts], *pieces]
     outs = ([jax.ShapeDtypeStruct((total, span, LANES), BF16)] if last else []) + [stage]
     return pl.pallas_call(
-        functools.partial(combine_kernel, seqs, masks, len(lefts), offset, last, len(first)),
+        functools.partial(combine_kernel, seqs, masks, counts, offset, last, 0 if begun is None else 1),
         out_shape=outs,
         in_specs=[VMEM] * len(args),
         out_specs=[HBM, VMEM] if last else [VMEM],
         input_output_aliases={} if begun is None else {0: len(outs) - 1},
-        scratch_shapes=[pltpu.VMEM((rows, depth), BF16), pltpu.SemaphoreType.DMA],
+        scratch_shapes=[pltpu.VMEM((rows * len(pieces), depth), BF16), pltpu.SemaphoreType.DMA],
         compiler_params=params(),
         cost_estimate=pl.CostEstimate(
-            flops=4 * pairs * len(lefts) * rows * LANES * depth, bytes_accessed=0, transcendentals=0
+            flops=4 * pairs * sum(counts) * rows * LANES * depth, bytes_accessed=0, transcendentals=0
         ),
         name="combine_last" if last else "combine_some",
     )(*args)[0]
@@ -274,7 +268,7 @@
     variance = jnp.mean(centered * centered, axis=-1, keepdims=True)
     normed = (centered * lax.rsqrt(variance + 1e-05) * gain + shift).astype(BF16)
     left = (jnp.einsum("src,ck->rsk", normed, first, preferred_element_type=F32) + first_shift).astype(BF16)
-    right = (jnp.einsum("src,ck->rks", normed, second, preferred_element_type=F32) + second_shift).astype(BF16)
+    right = (jnp.einsum("src,ck->rks", normed, second, preferred_element_type=F32) + second_shift[:, None]).astype(BF16)
     right = right.reshape(here, width, seqs // RUN, RUN).transpose(0, 2, 1, 3).reshape(here, seqs * width)
     left = lax.all_gather(left.reshape(here, seqs * width), "col", axis=0, tiled=True)
     groups = LANES // width
@@ -283,7 +277,7 @@
     span = every.shape[0] // lax.axis_size("col")
     mine = lax.dynamic_slice_in_dim(every, lax.axis_index("col") * span, span, 0)
     spread_left, _ = spread(left, final, seqs, width)
-    return combine([spread_left], [mine], (0,), final_shift, seqs, span)
+    return combine([spread_left], [mine], (0,), (1,), final_shift, seqs, span)
 
 
 def per_device(x, gain, shift, first, first_shift, second, second_shift, final, final_shift):
@@ -295,18 +289,19 @@
     both = ("row", "col")
     far = lax.ppermute(right, both, linear(lambda r, c, i: (r ^ 1, c) if i else (r ^ 8, 1 - c)))
     near = lax.ppermute(right, both, linear(lambda r, c, i: (r ^ 8, c) if i else (r, 1 - c)))
-    own, pairs = spread(left, final, seqs, width)
+    own, pairs = spread(left, keep(final), seqs, width)
     beside = lax.ppermute(after([left], keep(pairs))[0], "col", [(0, 1), (1, 0)])
     pair = arrange(right, near, far, pairs)
     first, second, third = [flip(pair, bits) for bits in (2, 4, 6)]
     lefts = [own, spread(beside, final, seqs, width, pairs)]
     span = 16 * here
     some, masks, total = [pair, flip(pair, 1)], (0, 1), 2 * here
-    begun = combine(lefts[:1], some, masks, final_shift, seqs, span, None, 0, total)
-    first, second, third = after([first, second, third], keep(begun), keep(lefts[1]))
-    begun = combine(lefts[1:], some, masks, final_shift, seqs, span, begun, here // 2, total, [first])
-    pieces = [first, flip(first, 1), second, flip(second, 1), third, flip(third, 1)]
-    return combine(lefts, pieces, (2, 3, 4, 5, 6, 7), final_shift, seqs, span, begun)
+    begun = combine(lefts[:1], some, masks, (2,), final_shift, seqs, span, None, 0, total)
+    begun = combine(lefts[1:], some, masks, (2,), final_shift, seqs, span, begun, here // 2, total)
+    pieces = after([first, second, third], keep(begun))
+    begun = combine(lefts[:1], pieces, (2, 4, 6), (3,), final_shift, seqs, span, begun, 0, total)
+    pieces = [flip(piece, 1) for piece in pieces] + [*pieces]
+    return combine(lefts, pieces, (3, 5, 7, 2, 4, 6), (3, 6), final_shift, seqs, span, begun)
 
 
 def solution(mesh):

time: 24.4 us -> 23.6 us (0.967)
  starting transfers between devices: 10.7 us -> 9.81 us
    ppermute x7, starting transfers between devices: 7.06 us -> 6.13 us  [flip(): return lax.ppermute(value, 'row', [(r, r ^ bits) for r in range(16)])]
    pallas_call x3 -> x4, Pallas kernels: 7.04 us -> 7.17 us  [combine(): pl.pallas_call(functools.partial(combine_kernel, seqs, masks, counts, off...]
  transfers between devices with their start and end apart: 10 -> 10, of which waited for: 1 -> 2; matrix products, arithmetic and copies ran while one was open for 0% -> 0% of each run, Pallas kernels for 25% -> 30%
where the time goes in v5:
time: 23.6 us; the launch traced here: 23.5 us
  Pallas kernels  12.6 us (53%)
  starting transfers between devices  9.81 us (42%)
  waiting for transfers between devices  0.98 us (4%)
    pallas_call x4, Pallas kernels, combine(): pl.pallas_call(functools.partial(combine_kernel, seqs, masks, counts, off...  7.17 us
    ppermute x7, starting transfers between devices, flip(): return lax.ppermute(value, 'row', [(r, r ^ bits) for r in range(16)])  6.13 us
    ppermute x1, starting transfers between devices, per_device(): lax.ppermute(right, both, linear(lambda r, c, i: (r ^ 1, c) if i else (r...  2.35 us
    pallas_call x1, Pallas kernels, spread(): pl.pallas_call(functools.partial(spread_first_kernel, seqs, width), out_s...  1.88 us
    pallas_call x1, Pallas kernels, spread(): pl.pallas_call(functools.partial(spread_second_kernel, seqs, width), out_...  1.79 us
    pallas_call x1, Pallas kernels, project(): pl.pallas_call(project_kernel, out_shape=(jax.ShapeDtypeStruct((here, seq...  1.69 us
    ppermute x1, starting transfers between devices, per_device(): lax.ppermute(after([left], keep(pairs))[0], 'col', [(0, 1), (1, 0)])  1.33 us
    ppermute x1, waiting for transfers between devices, per_device(): lax.ppermute(right, both, linear(lambda r, c, i: (r ^ 8, c) if i else (r,...  0.89 us
  transfers between devices with their start and end apart: 10, of which 2 were waited for; matrix products, arithmetic and copies ran while one was open for 0% of the time, Pallas kernels for 30%

profile of v5, /device:TPU:3, one launch (start us, length us, event | category | flops | bytes accessed | tf_op | source)
XLA Modules:
  0.0 23.5 jit_solution(8602899299353638329)
XLA Ops:
  0.0 1.7 %project.1 = (bf16[24,1024]{1,0:T(8,128)(2,1)S(1)}, bf16[192,128]{1,0:T(8,128)(2,1)S(1)}, bf16[1024,128]{1,0:T(8,128)(2,1)S(1)}) custom-call(bf16[32,24,256]{2,1,0:T(8,128)(2,1)} %refs_0_.1, f32[1,256]{1,0:T(1,128)} %bitcast.13, f32[1,256]{1,0:T(1,128)} %bitcast.14, bf16[32,256]{1,0:T(8,128)(2,1)} %bitcast.11, f32[1,32]{1,0:T(1,128)} %bitcast.15, ...), custom_call_target="tpu_custom_call" | custom-call | flops 100663296 | bytes 393216 | tf_op jit(solution)/shard_map/project/pallas_call | solution.py:155
  1.7 2.3 %collective-permute-start.1 = (bf16[24,1024]{1,0:T(8,128)(2,1)S(1)}, bf16[24,1024]{1,0:T(8,128)(2,1)S(1)}, u32[]{:S(2)}, u32[]{:S(2)}) collective-permute-start(bf16[24,1024]{1,0:T(8,128)(2,1)S(1)} %get-tuple-element.17.own_ref), channel_id=1, source_target_pairs={{0,2},{1,16},{2,0},{3,18},{4,6},{5,20},{6,4},{7,22},{8,10},{9,24},... | collective-permute-start | bytes 147464 | tf_op jit(solution)/shard_map/ppermute | solution.py:290
  4.0 0.0 collective-permute-start
  4.1 1.9 %spread_first.1 = (bf16[12,1024,256]{2,1,0:T(8,128)(2,1)S(1)}, bf16[16,32,256]{2,1,0:T(8,128)(2,1)S(1)}) custom-call(bf16[192,128]{1,0:T(8,128)(2,1)S(1)} %get-tuple-element.14.l_ref.refs_0_, bf16[1024,128]{1,0:T(8,128)(2,1)S(1)} %get-tuple-element.15.f_ref), custom_call_target="tpu_custom_call" | custom-call | flops 1610612736 | bytes 49152 | tf_op jit(solution)/shard_map/spread_first/pallas_call | solution.py:180
  5.9 0.0 copy-start
  6.0 1.3 %collective-permute-start.3 = (bf16[192,128]{1,0:T(8,128)(2,1)S(1)}, bf16[192,128]{1,0:T(8,128)(2,1)S(1)}, u32[]{:S(2)}, u32[]{:S(2)}) collective-permute-start(bf16[192,128]{1,0:T(8,128)(2,1)S(1)} %after.2), channel_id=1, source_target_pairs={{0,1},{1,0},{2,3},{3,2},{4,5},{5,4},{6,7},{7,6},{8,9},{9,8},{10,11... | collective-permute-start | bytes 147464 | tf_op jit(solution)/shard_map/ppermute | solution.py:293
  7.3 0.0 collective-permute-done.1.far_ref
  7.3 0.9 %collective-permute-done.near_ref = bf16[24,1024]{1,0:T(8,128)(2,1)S(1)} collective-permute-done((bf16[24,1024]{1,0:T(8,128)(2,1)S(1)}, bf16[24,1024]{1,0:T(8,128)(2,1)S(1)}, u32[]{:S(2)}, u32[]{:S(2)}) %collective-permute-start) | collective-permute-done | bytes 49184 | tf_op jit(solution)/shard_map/ppermute | solution.py:291
  8.2 2.1 %collective-permute-start.6 = (bf16[48,1024]{1,0:T(8,128)(2,1)S(1)}, bf16[48,1024]{1,0:T(8,128)(2,1)S(1)}, u32[]{:S(2)}, u32[]{:S(2)}) collective-permute-start(bf16[48,1024]{1,0:T(8,128)(2,1)S(1)} %arrange.1.refs_2_.refs_3_), channel_id=1, source_target_pairs={{0,12},{2,14},{4,8},{6,10},{8,4},{10,6},{12,0},{14,2},{16,28},{18,... | collective-permute-start | bytes 294920 | tf_op jit(solution)/shard_map/ppermute | solution.py:260
  10.3 0.4 %collective-permute-start.5 = (bf16[48,1024]{1,0:T(8,128)(2,1)S(1)}, bf16[48,1024]{1,0:T(8,128)(2,1)S(1)}, u32[]{:S(2)}, u32[]{:S(2)}) collective-permute-start(bf16[48,1024]{1,0:T(8,128)(2,1)S(1)} %arrange.1.refs_2_.refs_3_), channel_id=1, source_target_pairs={{0,8},{2,10},{4,12},{6,14},{8,0},{10,2},{12,4},{14,6},{16,24},{18,... | collective-permute-start | bytes 294920 | tf_op jit(solution)/shard_map/ppermute | solution.py:260
  10.7 0.2 collective-permute-start.4
  10.9 2.8 %collective-permute-start.2 = (bf16[48,1024]{1,0:T(8,128)(2,1)S(1)}, bf16[48,1024]{1,0:T(8,128)(2,1)S(1)}, u32[]{:S(2)}, u32[]{:S(2)}) collective-permute-start(bf16[48,1024]{1,0:T(8,128)(2,1)S(1)} %arrange.1.refs_2_.refs_3_), channel_id=1, source_target_pairs={{0,2},{2,0},{4,6},{6,4},{8,10},{10,8},{12,14},{14,12},{16,18},{18,... | collective-permute-start | bytes 294920 | tf_op jit(solution)/shard_map/ppermute | solution.py:260
  13.7 1.8 %spread_second.1.refs_2_.refs_3_ = bf16[12,1024,256]{2,1,0:T(8,128)(2,1)S(1)} custom-call(bf16[192,128]{1,0:T(8,128)(2,1)S(1)} %collective-permute-done.3.l_ref, bf16[16,32,256]{2,1,0:T(8,128)(2,1)S(1)} %get-tuple-element.18._.refs_1_.pairs), custom_call_target="tpu_custom_call" | custom-call | flops 1610612736 | bytes 49152 | tf_op jit(solution)/shard_map/spread_second/pallas_call | solution.py:190
  15.5 0.0 collective-permute-done.2.refs_3_.refs_4_
  15.5 1.2 %combine_some.3.refs_0_ = bf16[24,2,384,128]{3,2,1,0:T(8,128)(2,1)S(1)} custom-call(f32[1,128]{1,0:T(1,128)S(1)} %bitcast.7, bf16[12,1024,256]{2,1,0:T(8,128)(2,1)S(1)} %get-tuple-element.16.refs_1_.refs_2_, bf16[48,1024]{1,0:T(8,128)(2,1)S(1)} %arrange.1.refs_2_.refs_3_, bf16[48,1024]{1,0:T(8,128)(2,1)S(1)} %collective-permute-done.2.refs_3_.refs_4_), custom_call_target="tpu_custom_call" | custom-call | flops 603979776 | tf_op jit(solution)/shard_map/combine_some/pallas_call | solution.py:234
  16.7 1.2 %combine_some.4.refs_3_.refs_0_ = bf16[24,2,384,128]{3,2,1,0:T(8,128)(2,1)S(1)} custom-call(bf16[24,2,384,128]{3,2,1,0:T(8,128)(2,1)S(1)} %combine_some.3.refs_0_, f32[1,128]{1,0:T(1,128)S(1)} %bitcast.8, bf16[12,1024,256]{2,1,0:T(8,128)(2,1)S(1)} %spread_second.1.refs_2_.refs_3_, ...), custom_call_target="tpu_custom_call", output_to_operand_aliasing={{}: (0, {})} | custom-call | flops 603979776 | tf_op jit(solution)/shard_map/combine_some/pallas_call | solution.py:234
  17.8 0.0 collective-permute-done.6.refs_2_
  17.8 0.0 collective-permute-done.5.refs_1_
  17.9 0.1 collective-permute-start.7
  18.0 0.5 %collective-permute-start.8 = (bf16[48,1024]{1,0:T(8,128)(2,1)S(1)}, bf16[48,1024]{1,0:T(8,128)(2,1)S(1)}, u32[]{:S(2)}, u32[]{:S(2)}) collective-permute-start(bf16[48,1024]{1,0:T(8,128)(2,1)S(1)} %get-tuple-element.20.refs_4_.refs_8_), channel_id=1, source_target_pairs={{0,2},{2,0},{4,6},{6,4},{8,10},{10,8},{12,14},{14,12},{16,18},{18,... | collective-permute-start | bytes 294920 | tf_op jit(solution)/shard_map/ppermute | solution.py:260
  18.5 0.1 collective-permute-start.9
  18.5 1.1 %combine_some.5.refs_0_ = bf16[24,2,384,128]{3,2,1,0:T(8,128)(2,1)S(1)} custom-call(bf16[24,2,384,128]{3,2,1,0:T(8,128)(2,1)S(1)} %combine_some.4.refs_3_.refs_0_, f32[1,128]{1,0:T(1,128)S(1)} %bitcast.9, bf16[12,1024,256]{2,1,0:T(8,128)(2,1)S(1)} %get-tuple-element.16.refs_1_.refs_2_, ...), custom_call_target="tpu_custom_call", output_to_operand_aliasing={{}: (0, {})} | custom-call | flops 905969664 | tf_op jit(solution)/shard_map/combine_some/pallas_call | solution.py:234
  19.7 0.1 collective-permute-done.9.refs_6_
  19.8 3.7 %combine_last.1 = (bf16[48,384,128]{2,1,0:T(8,128)(2,1)}, bf16[24,2,384,128]{3,2,1,0:T(8,128)(2,1)S(1)}) custom-call(bf16[24,2,384,128]{3,2,1,0:T(8,128)(2,1)S(1)} %combine_some.5.refs_0_, f32[1,128]{1,0:T(1,128)S(1)} %bitcast.10, bf16[12,1024,256]{2,1,0:T(8,128)(2,1)S(1)} %get-tuple-element.16.refs_1_.refs_2_, ...), custom_call_target="tpu_custom_call", output_to_operand_aliasing={{1}: (0, {})} | custom-call | flops 2717908992 | tf_op jit(solution)/shard_map/combine_last/pallas_call | solution.py:234
  (8 shorter events, 0.0 us)
Async XLA Ops:
  1.7 5.6 %collective-permute-start.1 = (bf16[24,1024]{1,0:T(8,128)(2,1)S(1)}, bf16[24,1024]{1,0:T(8,128)(2,1)S(1)}, u32[]{:S(2)}, u32[]{:S(2)}) collective-permute-start(bf16[24,1024]{1,0:T(8,128)(2,1)S(1)} %get-tuple-element.17.own_ref), channel_id=1, source_target_pairs={{0,2},{1,16},{2,0},{3,18},{4,6},{5,20},{6,4},{7,22},{8,10},{9,24},... | collective-permute-start | bytes 147464 | tf_op jit(solution)/shard_map/ppermute | solution.py:290
  4.0 4.1 %collective-permute-start = (bf16[24,1024]{1,0:T(8,128)(2,1)S(1)}, bf16[24,1024]{1,0:T(8,128)(2,1)S(1)}, u32[]{:S(2)}, u32[]{:S(2)}) collective-permute-start(bf16[24,1024]{1,0:T(8,128)(2,1)S(1)} %get-tuple-element.17.own_ref), channel_id=1, source_target_pairs={{0,16},{1,0},{2,18},{3,2},{4,20},{5,4},{6,22},{7,6},{8,24},{9,8},{... | collective-permute-start | bytes 147464 | tf_op jit(solution)/shard_map/ppermute | solution.py:291
  5.9 9.6 %copy-start = (f32[128]{0:T(128)S(1)}, f32[128]{0:T(128)}, u32[]{:S(2)}) copy-start(f32[128]{0:T(128)} %param.17) | copy-start | bytes 1540
  6.0 7.7 %collective-permute-start.3 = (bf16[192,128]{1,0:T(8,128)(2,1)S(1)}, bf16[192,128]{1,0:T(8,128)(2,1)S(1)}, u32[]{:S(2)}, u32[]{:S(2)}) collective-permute-start(bf16[192,128]{1,0:T(8,128)(2,1)S(1)} %after.2), channel_id=1, source_target_pairs={{0,1},{1,0},{2,3},{3,2},{4,5},{5,4},{6,7},{7,6},{8,9},{9,8},{10,11... | collective-permute-start | bytes 147464 | tf_op jit(solution)/shard_map/ppermute | solution.py:293
  8.2 9.6 %collective-permute-start.6 = (bf16[48,1024]{1,0:T(8,128)(2,1)S(1)}, bf16[48,1024]{1,0:T(8,128)(2,1)S(1)}, u32[]{:S(2)}, u32[]{:S(2)}) collective-permute-start(bf16[48,1024]{1,0:T(8,128)(2,1)S(1)} %arrange.1.refs_2_.refs_3_), channel_id=1, source_target_pairs={{0,12},{2,14},{4,8},{6,10},{8,4},{10,6},{12,0},{14,2},{16,28},{18,... | collective-permute-start | bytes 294920 | tf_op jit(solution)/shard_map/ppermute | solution.py:260
  10.3 7.6 %collective-permute-start.5 = (bf16[48,1024]{1,0:T(8,128)(2,1)S(1)}, bf16[48,1024]{1,0:T(8,128)(2,1)S(1)}, u32[]{:S(2)}, u32[]{:S(2)}) collective-permute-start(bf16[48,1024]{1,0:T(8,128)(2,1)S(1)} %arrange.1.refs_2_.refs_3_), channel_id=1, source_target_pairs={{0,8},{2,10},{4,12},{6,14},{8,0},{10,2},{12,4},{14,6},{16,24},{18,... | collective-permute-start | bytes 294920 | tf_op jit(solution)/shard_map/ppermute | solution.py:260
  10.7 7.2 %collective-permute-start.4 = (bf16[48,1024]{1,0:T(8,128)(2,1)S(1)}, bf16[48,1024]{1,0:T(8,128)(2,1)S(1)}, u32[]{:S(2)}, u32[]{:S(2)}) collective-permute-start(bf16[48,1024]{1,0:T(8,128)(2,1)S(1)} %arrange.1.refs_2_.refs_3_), channel_id=1, source_target_pairs={{0,4},{2,6},{4,0},{6,2},{8,12},{10,14},{12,8},{14,10},{16,20},{18,... | collective-permute-start | bytes 294920 | tf_op jit(solution)/shard_map/ppermute | solution.py:260
  10.9 4.6 %collective-permute-start.2 = (bf16[48,1024]{1,0:T(8,128)(2,1)S(1)}, bf16[48,1024]{1,0:T(8,128)(2,1)S(1)}, u32[]{:S(2)}, u32[]{:S(2)}) collective-permute-start(bf16[48,1024]{1,0:T(8,128)(2,1)S(1)} %arrange.1.refs_2_.refs_3_), channel_id=1, source_target_pairs={{0,2},{2,0},{4,6},{6,4},{8,10},{10,8},{12,14},{14,12},{16,18},{18,... | collective-permute-start | bytes 294920 | tf_op jit(solution)/shard_map/ppermute | solution.py:260
  17.9 1.8 %collective-permute-start.7 = (bf16[48,1024]{1,0:T(8,128)(2,1)S(1)}, bf16[48,1024]{1,0:T(8,128)(2,1)S(1)}, u32[]{:S(2)}, u32[]{:S(2)}) collective-permute-start(bf16[48,1024]{1,0:T(8,128)(2,1)S(1)} %get-tuple-element.19.refs_3_.refs_7_), channel_id=1, source_target_pairs={{0,2},{2,0},{4,6},{6,4},{8,10},{10,8},{12,14},{14,12},{16,18},{18,... | collective-permute-start | bytes 294920 | tf_op jit(solution)/shard_map/ppermute | solution.py:260
  18.0 1.7 %collective-permute-start.8 = (bf16[48,1024]{1,0:T(8,128)(2,1)S(1)}, bf16[48,1024]{1,0:T(8,128)(2,1)S(1)}, u32[]{:S(2)}, u32[]{:S(2)}) collective-permute-start(bf16[48,1024]{1,0:T(8,128)(2,1)S(1)} %get-tuple-element.20.refs_4_.refs_8_), channel_id=1, source_target_pairs={{0,2},{2,0},{4,6},{6,4},{8,10},{10,8},{12,14},{14,12},{16,18},{18,... | collective-permute-start | bytes 294920 | tf_op jit(solution)/shard_map/ppermute | solution.py:260
  18.5 1.3 %collective-permute-start.9 = (bf16[48,1024]{1,0:T(8,128)(2,1)S(1)}, bf16[48,1024]{1,0:T(8,128)(2,1)S(1)}, u32[]{:S(2)}, u32[]{:S(2)}) collective-permute-start(bf16[48,1024]{1,0:T(8,128)(2,1)S(1)} %get-tuple-element.21.refs_5_.refs_9_), channel_id=1, source_target_pairs={{0,2},{2,0},{4,6},{6,4},{8,10},{10,8},{12,14},{14,12},{16,18},{18,... | collective-permute-start | bytes 294920 | tf_op jit(solution)/shard_map/ppermute | solution.py:260

commit v6 on v5

--- a/solution.py
+++ b/solution.py
@@ -99,17 +99,27 @@
     pass
 
 
-def combine_kernel(seqs, masks, counts, offset, last, begun, *refs):
+def join_kernel(count, *refs):
+    rows = refs[0].shape[0]
+    for n in range(count):
+        refs[-1][n * rows : (n + 1) * rows, :] = refs[n][...]
+
+
+def combine_kernel(seqs, rows, n_pieces, masks, counts, offset, last, begun, *refs):
     refs = refs[begun:]
-    lefts, pieces = refs[1 : 1 + len(counts)], refs[1 + len(counts) : 1 + len(counts) + len(masks)]
+    lefts, pieces = refs[1 : 1 + len(counts)], refs[1 + len(counts) : 1 + len(counts) + n_pieces]
     shift_ref, stage, right = refs[0], refs[-3], refs[-2]
-    rows = pieces[0].shape[0]
     pairs = lefts[0].shape[0]
     spots = stage.shape[2] // rows
     spot = lax.rem(lax.axis_index("row"), spots) if spots > 1 else 0
     places = [pl.multiple_of(jnp.bitwise_xor(spot, mask) * rows, rows) if spots > 1 else 0 for mask in masks]
-    for n, piece in enumerate(pieces):
-        right[n * rows : (n + 1) * rows, :] = piece[...]
+    if n_pieces == 1:
+        right = pieces[0]
+    else:
+        start = 0
+        for piece in pieces:
+            right[start : start + piece.shape[0], :] = piece[...]
+            start += piece.shape[0]
     shift = jnp.concatenate([shift_ref[...]] * 2, axis=1)
     unroll = next(u for u in (12, 6, 4, 3, 2, 1) if pairs % u == 0)
 
@@ -222,22 +232,34 @@
     )(*values, *earlier)
 
 
+def join(values, *earlier):
+    rows, depth = values[0].shape
+    return pl.pallas_call(
+        functools.partial(join_kernel, len(values)),
+        out_shape=jax.ShapeDtypeStruct((len(values) * rows, depth), BF16),
+        in_specs=[VMEM] * (len(values) + len(earlier)),
+        out_specs=VMEM,
+        compiler_params=params(),
+        name="join",
+    )(*values, *[keep(e) for e in earlier])
+
+
 def combine(lefts, pieces, masks, counts, final_shift, seqs, span, begun=None, offset=0, total=None):
     last = total is None
     pairs, depth, _ = lefts[0].shape
-    rows = pieces[0].shape[0]
+    rows = sum(piece.shape[0] for piece in pieces) // len(masks)
     total = total or 2 * pairs * len(lefts)
     stage = pltpu.VMEM((total // 2, 2, span, LANES), BF16)
     args = [] if begun is None else [keep(begun)]
     args += [final_shift[None], *[keep(left) for left in lefts], *pieces]
     outs = ([jax.ShapeDtypeStruct((total, span, LANES), BF16)] if last else []) + [stage]
     return pl.pallas_call(
-        functools.partial(combine_kernel, seqs, masks, counts, offset, last, 0 if begun is None else 1),
+        functools.partial(combine_kernel, seqs, rows, len(pieces), masks, counts, offset, last, 0 if begun is None else 1),
         out_shape=outs,
         in_specs=[VMEM] * len(args),
         out_specs=[HBM, VMEM] if last else [VMEM],
         input_output_aliases={} if begun is None else {0: len(outs) - 1},
-        scratch_shapes=[pltpu.VMEM((rows * len(pieces), depth), BF16), pltpu.SemaphoreType.DMA],
+        scratch_shapes=[pltpu.VMEM((rows * len(masks), depth), BF16), pltpu.SemaphoreType.DMA],
         compiler_params=params(),
         cost_estimate=pl.CostEstimate(
             flops=4 * pairs * sum(counts) * rows * LANES * depth, bytes_accessed=0, transcendentals=0
@@ -298,10 +320,9 @@
     some, masks, total = [pair, flip(pair, 1)], (0, 1), 2 * here
     begun = combine(lefts[:1], some, masks, (2,), final_shift, seqs, span, None, 0, total)
     begun = combine(lefts[1:], some, masks, (2,), final_shift, seqs, span, begun, here // 2, total)
-    pieces = after([first, second, third], keep(begun))
-    begun = combine(lefts[:1], pieces, (2, 4, 6), (3,), final_shift, seqs, span, begun, 0, total)
-    pieces = [flip(piece, 1) for piece in pieces] + [*pieces]
-    return combine(lefts, pieces, (3, 5, 7, 2, 4, 6), (3, 6), final_shift, seqs, span, begun)
+    three = join([first, second, third], begun)
+    begun = combine(lefts[:1], [three], (2, 4, 6), (3,), final_shift, seqs, span, begun, 0, total)
+    return combine(lefts, [flip(three, 1), three], (3, 5, 7, 2, 4, 6), (3, 6), final_shift, seqs, span, begun)
 
 
 def solution(mesh):

time: 23.6 us -> 23.4 us (level)
  starting transfers between devices: 9.81 us -> 9.24 us
  waiting for transfers between devices: 0.98 us -> 1.32 us
    ppermute x7 -> x5, starting transfers between devices: 6.13 us -> 5.56 us  [flip(): return lax.ppermute(value, 'row', [(r, r ^ bits) for r in range(16)])]
    ppermute x7 -> x5, waiting for transfers between devices: 0.08 us -> 0.42 us  [flip(): return lax.ppermute(value, 'row', [(r, r ^ bits) for r in range(16)])]
    pallas_call x4 -> x5, Pallas kernels: 7.17 us -> 7.23 us  [the longest x4 7.21 us: combine(): pl.pallas_call(functools.partial(combine_kernel, seqs, rows, len(pieces),...]
  transfers between devices with their start and end apart: 10 -> 8, of which waited for: 2 -> 2; matrix products, arithmetic and copies ran while one was open for 0% -> 0% of each run, Pallas kernels for 30% -> 31%
where the time goes in v6:
time: 23.4 us; the launch traced here: 23.3 us
  Pallas kernels  12.6 us (54%)
  starting transfers between devices  9.24 us (39%)
  waiting for transfers between devices  1.32 us (6%)
    pallas_call x4, Pallas kernels, combine(): pl.pallas_call(functools.partial(combine_kernel, seqs, rows, len(pieces),...  7.21 us
    ppermute x5, starting transfers between devices, flip(): return lax.ppermute(value, 'row', [(r, r ^ bits) for r in range(16)])  5.56 us
    ppermute x1, starting transfers between devices, per_device(): lax.ppermute(right, both, linear(lambda r, c, i: (r ^ 1, c) if i else (r...  2.35 us
    pallas_call x1, Pallas kernels, spread(): pl.pallas_call(functools.partial(spread_first_kernel, seqs, width), out_s...  1.88 us
    pallas_call x1, Pallas kernels, spread(): pl.pallas_call(functools.partial(spread_second_kernel, seqs, width), out_...  1.79 us
    pallas_call x1, Pallas kernels, project(): pl.pallas_call(project_kernel, out_shape=(jax.ShapeDtypeStruct((here, seq...  1.69 us
    ppermute x1, starting transfers between devices, per_device(): lax.ppermute(after([left], keep(pairs))[0], 'col', [(0, 1), (1, 0)])  1.33 us
    ppermute x1, waiting for transfers between devices, per_device(): lax.ppermute(right, both, linear(lambda r, c, i: (r ^ 8, c) if i else (r,...  0.89 us
  transfers between devices with their start and end apart: 8, of which 2 were waited for; matrix products, arithmetic and copies ran while one was open for 0% of the time, Pallas kernels for 31%

profile of v6, /device:TPU:3, one launch (start us, length us, event | category | flops | bytes accessed | tf_op | source)
XLA Modules:
  0.0 23.3 jit_solution(13748989451797563459)
XLA Ops:
  0.0 1.7 %project.1 = (bf16[24,1024]{1,0:T(8,128)(2,1)S(1)}, bf16[192,128]{1,0:T(8,128)(2,1)S(1)}, bf16[1024,128]{1,0:T(8,128)(2,1)S(1)}) custom-call(bf16[32,24,256]{2,1,0:T(8,128)(2,1)} %refs_0_.1, f32[1,256]{1,0:T(1,128)} %bitcast.13, f32[1,256]{1,0:T(1,128)} %bitcast.14, bf16[32,256]{1,0:T(8,128)(2,1)} %bitcast.11, f32[1,32]{1,0:T(1,128)} %bitcast.15, ...), custom_call_target="tpu_custom_call" | custom-call | flops 100663296 | bytes 393216 | tf_op jit(solution)/shard_map/project/pallas_call | solution.py:165
  1.7 2.3 %collective-permute-start.1 = (bf16[24,1024]{1,0:T(8,128)(2,1)S(1)}, bf16[24,1024]{1,0:T(8,128)(2,1)S(1)}, u32[]{:S(2)}, u32[]{:S(2)}) collective-permute-start(bf16[24,1024]{1,0:T(8,128)(2,1)S(1)} %get-tuple-element.14.own_ref), channel_id=1, source_target_pairs={{0,2},{1,16},{2,0},{3,18},{4,6},{5,20},{6,4},{7,22},{8,10},{9,24},... | collective-permute-start | bytes 147464 | tf_op jit(solution)/shard_map/ppermute | solution.py:312
  4.0 0.0 collective-permute-start
  4.1 1.9 %spread_first.1 = (bf16[12,1024,256]{2,1,0:T(8,128)(2,1)S(1)}, bf16[16,32,256]{2,1,0:T(8,128)(2,1)S(1)}) custom-call(bf16[192,128]{1,0:T(8,128)(2,1)S(1)} %get-tuple-element.11.l_ref.refs_0_, bf16[1024,128]{1,0:T(8,128)(2,1)S(1)} %get-tuple-element.12.f_ref), custom_call_target="tpu_custom_call" | custom-call | flops 1610612736 | bytes 49152 | tf_op jit(solution)/shard_map/spread_first/pallas_call | solution.py:190
  5.9 0.0 copy-start
  6.0 1.3 %collective-permute-start.3 = (bf16[192,128]{1,0:T(8,128)(2,1)S(1)}, bf16[192,128]{1,0:T(8,128)(2,1)S(1)}, u32[]{:S(2)}, u32[]{:S(2)}) collective-permute-start(bf16[192,128]{1,0:T(8,128)(2,1)S(1)} %after.1), channel_id=1, source_target_pairs={{0,1},{1,0},{2,3},{3,2},{4,5},{5,4},{6,7},{7,6},{8,9},{9,8},{10,11... | collective-permute-start | bytes 147464 | tf_op jit(solution)/shard_map/ppermute | solution.py:315
  7.3 0.0 collective-permute-done.1.far_ref
  7.3 0.9 %collective-permute-done.near_ref = bf16[24,1024]{1,0:T(8,128)(2,1)S(1)} collective-permute-done((bf16[24,1024]{1,0:T(8,128)(2,1)S(1)}, bf16[24,1024]{1,0:T(8,128)(2,1)S(1)}, u32[]{:S(2)}, u32[]{:S(2)}) %collective-permute-start) | collective-permute-done | bytes 49184 | tf_op jit(solution)/shard_map/ppermute | solution.py:313
  8.2 2.1 %collective-permute-start.6 = (bf16[48,1024]{1,0:T(8,128)(2,1)S(1)}, bf16[48,1024]{1,0:T(8,128)(2,1)S(1)}, u32[]{:S(2)}, u32[]{:S(2)}) collective-permute-start(bf16[48,1024]{1,0:T(8,128)(2,1)S(1)} %arrange.1.refs_2_.refs_3_), channel_id=1, source_target_pairs={{0,12},{2,14},{4,8},{6,10},{8,4},{10,6},{12,0},{14,2},{16,28},{18,... | collective-permute-start | bytes 294920 | tf_op jit(solution)/shard_map/ppermute | solution.py:282
  10.3 0.4 %collective-permute-start.5 = (bf16[48,1024]{1,0:T(8,128)(2,1)S(1)}, bf16[48,1024]{1,0:T(8,128)(2,1)S(1)}, u32[]{:S(2)}, u32[]{:S(2)}) collective-permute-start(bf16[48,1024]{1,0:T(8,128)(2,1)S(1)} %arrange.1.refs_2_.refs_3_), channel_id=1, source_target_pairs={{0,8},{2,10},{4,12},{6,14},{8,0},{10,2},{12,4},{14,6},{16,24},{18,... | collective-permute-start | bytes 294920 | tf_op jit(solution)/shard_map/ppermute | solution.py:282
  10.7 0.2 collective-permute-start.4
  10.9 2.8 %collective-permute-start.2 = (bf16[48,1024]{1,0:T(8,128)(2,1)S(1)}, bf16[48,1024]{1,0:T(8,128)(2,1)S(1)}, u32[]{:S(2)}, u32[]{:S(2)}) collective-permute-start(bf16[48,1024]{1,0:T(8,128)(2,1)S(1)} %arrange.1.refs_2_.refs_3_), channel_id=1, source_target_pairs={{0,2},{2,0},{4,6},{6,4},{8,10},{10,8},{12,14},{14,12},{16,18},{18,... | collective-permute-start | bytes 294920 | tf_op jit(solution)/shard_map/ppermute | solution.py:282
  13.7 0.0 collective-permute-done.3.l_ref
  13.7 1.8 %spread_second.1.refs_2_.refs_3_ = bf16[12,1024,256]{2,1,0:T(8,128)(2,1)S(1)} custom-call(bf16[192,128]{1,0:T(8,128)(2,1)S(1)} %collective-permute-done.3.l_ref, bf16[16,32,256]{2,1,0:T(8,128)(2,1)S(1)} %get-tuple-element.15._.refs_1_.pairs), custom_call_target="tpu_custom_call" | custom-call | flops 1610612736 | bytes 49152 | tf_op jit(solution)/shard_map/spread_second/pallas_call | solution.py:200
  15.5 0.0 collective-permute-done.2.refs_3_.refs_4_
  15.5 1.2 %combine_some.3.refs_0_ = bf16[24,2,384,128]{3,2,1,0:T(8,128)(2,1)S(1)} custom-call(f32[1,128]{1,0:T(1,128)S(1)} %bitcast.7, bf16[12,1024,256]{2,1,0:T(8,128)(2,1)S(1)} %get-tuple-element.13.refs_1_.refs_2_, bf16[48,1024]{1,0:T(8,128)(2,1)S(1)} %arrange.1.refs_2_.refs_3_, bf16[48,1024]{1,0:T(8,128)(2,1)S(1)} %collective-permute-done.2.refs_3_.refs_4_), custom_call_target="tpu_custom_call" | custom-call | flops 603979776 | tf_op jit(solution)/shard_map/combine_some/pallas_call | solution.py:256
  16.7 1.2 %combine_some.4.refs_3_.refs_0_ = bf16[24,2,384,128]{3,2,1,0:T(8,128)(2,1)S(1)} custom-call(bf16[24,2,384,128]{3,2,1,0:T(8,128)(2,1)S(1)} %combine_some.3.refs_0_, f32[1,128]{1,0:T(1,128)S(1)} %bitcast.8, bf16[12,1024,256]{2,1,0:T(8,128)(2,1)S(1)} %spread_second.1.refs_2_.refs_3_, ...), custom_call_target="tpu_custom_call", output_to_operand_aliasing={{}: (0, {})} | custom-call | flops 603979776 | tf_op jit(solution)/shard_map/combine_some/pallas_call | solution.py:256
  17.8 0.0 collective-permute-done.6.refs_2_
  17.9 0.0 collective-permute-done.5.refs_1_
  17.9 0.0 collective-permute-done.4.refs_0_
  17.9 0.1 collective-permute-start.7
  18.0 1.1 %combine_some.5.refs_0_ = bf16[24,2,384,128]{3,2,1,0:T(8,128)(2,1)S(1)} custom-call(bf16[24,2,384,128]{3,2,1,0:T(8,128)(2,1)S(1)} %combine_some.4.refs_3_.refs_0_, f32[1,128]{1,0:T(1,128)S(1)} %bitcast.9, bf16[12,1024,256]{2,1,0:T(8,128)(2,1)S(1)} %get-tuple-element.13.refs_1_.refs_2_, ...), custom_call_target="tpu_custom_call", output_to_operand_aliasing={{}: (0, {})} | custom-call | flops 905969664 | tf_op jit(solution)/shard_map/combine_some/pallas_call | solution.py:256
  19.1 0.4 %collective-permute-done.7.refs_4_ = bf16[144,1024]{1,0:T(8,128)(2,1)S(1)} collective-permute-done((bf16[144,1024]{1,0:T(8,128)(2,1)S(1)}, bf16[144,1024]{1,0:T(8,128)(2,1)S(1)}, u32[]{:S(2)}, u32[]{:S(2)}) %collective-permute-start.7) | collective-permute-done | bytes 294944 | tf_op jit(solution)/shard_map/ppermute | solution.py:282
  19.6 3.7 %combine_last.1 = (bf16[48,384,128]{2,1,0:T(8,128)(2,1)}, bf16[24,2,384,128]{3,2,1,0:T(8,128)(2,1)S(1)}) custom-call(bf16[24,2,384,128]{3,2,1,0:T(8,128)(2,1)S(1)} %combine_some.5.refs_0_, f32[1,128]{1,0:T(1,128)S(1)} %bitcast.10, bf16[12,1024,256]{2,1,0:T(8,128)(2,1)S(1)} %get-tuple-element.13.refs_1_.refs_2_, ...), custom_call_target="tpu_custom_call", output_to_operand_aliasing={{1}: (0, {})} | custom-call | flops 2717908992 | tf_op jit(solution)/shard_map/combine_last/pallas_call | solution.py:256
  (4 shorter events, 0.0 us)
Async XLA Ops:
  1.7 5.6 %collective-permute-start.1 = (bf16[24,1024]{1,0:T(8,128)(2,1)S(1)}, bf16[24,1024]{1,0:T(8,128)(2,1)S(1)}, u32[]{:S(2)}, u32[]{:S(2)}) collective-permute-start(bf16[24,1024]{1,0:T(8,128)(2,1)S(1)} %get-tuple-element.14.own_ref), channel_id=1, source_target_pairs={{0,2},{1,16},{2,0},{3,18},{4,6},{5,20},{6,4},{7,22},{8,10},{9,24},... | collective-permute-start | bytes 147464 | tf_op jit(solution)/shard_map/ppermute | solution.py:312
  4.0 4.1 %collective-permute-start = (bf16[24,1024]{1,0:T(8,128)(2,1)S(1)}, bf16[24,1024]{1,0:T(8,128)(2,1)S(1)}, u32[]{:S(2)}, u32[]{:S(2)}) collective-permute-start(bf16[24,1024]{1,0:T(8,128)(2,1)S(1)} %get-tuple-element.14.own_ref), channel_id=1, source_target_pairs={{0,16},{1,0},{2,18},{3,2},{4,20},{5,4},{6,22},{7,6},{8,24},{9,8},{... | collective-permute-start | bytes 147464 | tf_op jit(solution)/shard_map/ppermute | solution.py:313
  5.9 9.6 %copy-start = (f32[128]{0:T(128)S(1)}, f32[128]{0:T(128)}, u32[]{:S(2)}) copy-start(f32[128]{0:T(128)} %param.17) | copy-start | bytes 1540
  6.0 7.7 %collective-permute-start.3 = (bf16[192,128]{1,0:T(8,128)(2,1)S(1)}, bf16[192,128]{1,0:T(8,128)(2,1)S(1)}, u32[]{:S(2)}, u32[]{:S(2)}) collective-permute-start(bf16[192,128]{1,0:T(8,128)(2,1)S(1)} %after.1), channel_id=1, source_target_pairs={{0,1},{1,0},{2,3},{3,2},{4,5},{5,4},{6,7},{7,6},{8,9},{9,8},{10,11... | collective-permute-start | bytes 147464 | tf_op jit(solution)/shard_map/ppermute | solution.py:315
  8.2 9.6 %collective-permute-start.6 = (bf16[48,1024]{1,0:T(8,128)(2,1)S(1)}, bf16[48,1024]{1,0:T(8,128)(2,1)S(1)}, u32[]{:S(2)}, u32[]{:S(2)}) collective-permute-start(bf16[48,1024]{1,0:T(8,128)(2,1)S(1)} %arrange.1.refs_2_.refs_3_), channel_id=1, source_target_pairs={{0,12},{2,14},{4,8},{6,10},{8,4},{10,6},{12,0},{14,2},{16,28},{18,... | collective-permute-start | bytes 294920 | tf_op jit(solution)/shard_map/ppermute | solution.py:282
  10.3 7.6 %collective-permute-start.5 = (bf16[48,1024]{1,0:T(8,128)(2,1)S(1)}, bf16[48,1024]{1,0:T(8,128)(2,1)S(1)}, u32[]{:S(2)}, u32[]{:S(2)}) collective-permute-start(bf16[48,1024]{1,0:T(8,128)(2,1)S(1)} %arrange.1.refs_2_.refs_3_), channel_id=1, source_target_pairs={{0,8},{2,10},{4,12},{6,14},{8,0},{10,2},{12,4},{14,6},{16,24},{18,... | collective-permute-start | bytes 294920 | tf_op jit(solution)/shard_map/ppermute | solution.py:282
  10.7 7.2 %collective-permute-start.4 = (bf16[48,1024]{1,0:T(8,128)(2,1)S(1)}, bf16[48,1024]{1,0:T(8,128)(2,1)S(1)}, u32[]{:S(2)}, u32[]{:S(2)}) collective-permute-start(bf16[48,1024]{1,0:T(8,128)(2,1)S(1)} %arrange.1.refs_2_.refs_3_), channel_id=1, source_target_pairs={{0,4},{2,6},{4,0},{6,2},{8,12},{10,14},{12,8},{14,10},{16,20},{18,... | collective-permute-start | bytes 294920 | tf_op jit(solution)/shard_map/ppermute | solution.py:282
  10.9 4.6 %collective-permute-start.2 = (bf16[48,1024]{1,0:T(8,128)(2,1)S(1)}, bf16[48,1024]{1,0:T(8,128)(2,1)S(1)}, u32[]{:S(2)}, u32[]{:S(2)}) collective-permute-start(bf16[48,1024]{1,0:T(8,128)(2,1)S(1)} %arrange.1.refs_2_.refs_3_), channel_id=1, source_target_pairs={{0,2},{2,0},{4,6},{6,4},{8,10},{10,8},{12,14},{14,12},{16,18},{18,... | collective-permute-start | bytes 294920 | tf_op jit(solution)/shard_map/ppermute | solution.py:282
  17.9 1.6 %collective-permute-start.7 = (bf16[144,1024]{1,0:T(8,128)(2,1)S(1)}, bf16[144,1024]{1,0:T(8,128)(2,1)S(1)}, u32[]{:S(2)}, u32[]{:S(2)}) collective-permute-start(bf16[144,1024]{1,0:T(8,128)(2,1)S(1)} %join.1.refs_3_.refs_5_), channel_id=1, source_target_pairs={{0,2},{2,0},{4,6},{6,4},{8,10},{10,8},{12,14},{14,12},{16,18},{18,... | collective-permute-start | bytes 884744 | tf_op jit(solution)/shard_map/ppermute | solution.py:282

commit v7 on v6

--- a/solution.py
+++ b/solution.py
@@ -318,8 +318,7 @@
     lefts = [own, spread(beside, final, seqs, width, pairs)]
     span = 16 * here
     some, masks, total = [pair, flip(pair, 1)], (0, 1), 2 * here
-    begun = combine(lefts[:1], some, masks, (2,), final_shift, seqs, span, None, 0, total)
-    begun = combine(lefts[1:], some, masks, (2,), final_shift, seqs, span, begun, here // 2, total)
+    begun = combine(lefts, some, masks, (2, 2), final_shift, seqs, span, None, 0, total)
     three = join([first, second, third], begun)
     begun = combine(lefts[:1], [three], (2, 4, 6), (3,), final_shift, seqs, span, begun, 0, total)
     return combine(lefts, [flip(three, 1), three], (3, 5, 7, 2, 4, 6), (3, 6), final_shift, seqs, span, begun)

time: 23.4 us -> 23.3 us (level)
    pallas_call x4 -> x3, Pallas kernels: 7.21 us -> 7 us  [combine(): pl.pallas_call(functools.partial(combine_kernel, seqs, rows, len(pieces),...]
  transfers between devices with their start and end apart: 8 -> 8, of which waited for: 2 -> 2; matrix products, arithmetic and copies ran while one was open for 0% -> 0% of each run, Pallas kernels for 31% -> 30%
where the time goes in v7:
time: 23.3 us; the launch traced here: 23.1 us
  Pallas kernels  12.4 us (53%)
  starting transfers between devices  9.32 us (40%)
  waiting for transfers between devices  1.27 us (5%)
    pallas_call x3, Pallas kernels, combine(): pl.pallas_call(functools.partial(combine_kernel, seqs, rows, len(pieces),...  7 us
    ppermute x5, starting transfers between devices, flip(): return lax.ppermute(value, 'row', [(r, r ^ bits) for r in range(16)])  5.65 us
    ppermute x1, starting transfers between devices, per_device(): lax.ppermute(right, both, linear(lambda r, c, i: (r ^ 1, c) if i else (r...  2.35 us
    pallas_call x1, Pallas kernels, spread(): pl.pallas_call(functools.partial(spread_first_kernel, seqs, width), out_s...  1.88 us
    pallas_call x1, Pallas kernels, spread(): pl.pallas_call(functools.partial(spread_second_kernel, seqs, width), out_...  1.79 us
    pallas_call x1, Pallas kernels, project(): pl.pallas_call(project_kernel, out_shape=(jax.ShapeDtypeStruct((here, seq...  1.69 us
    ppermute x1, starting transfers between devices, per_device(): lax.ppermute(after([left], keep(pairs))[0], 'col', [(0, 1), (1, 0)])  1.33 us
    ppermute x1, waiting for transfers between devices, per_device(): lax.ppermute(right, both, linear(lambda r, c, i: (r ^ 8, c) if i else (r,...  0.89 us
  transfers between devices with their start and end apart: 8, of which 2 were waited for; matrix products, arithmetic and copies ran while one was open for 0% of the time, Pallas kernels for 30%

profile of v7, /device:TPU:3, one launch (start us, length us, event | category | flops | bytes accessed | tf_op | source)
XLA Modules:
  0.0 23.1 jit_solution(11714036159887675904)
XLA Ops:
  0.0 1.7 %project.1 = (bf16[24,1024]{1,0:T(8,128)(2,1)S(1)}, bf16[192,128]{1,0:T(8,128)(2,1)S(1)}, bf16[1024,128]{1,0:T(8,128)(2,1)S(1)}) custom-call(bf16[32,24,256]{2,1,0:T(8,128)(2,1)} %refs_0_.1, f32[1,256]{1,0:T(1,128)} %bitcast.12, f32[1,256]{1,0:T(1,128)} %bitcast.13, bf16[32,256]{1,0:T(8,128)(2,1)} %bitcast.10, f32[1,32]{1,0:T(1,128)} %bitcast.14, ...), custom_call_target="tpu_custom_call" | custom-call | flops 100663296 | bytes 393216 | tf_op jit(solution)/shard_map/project/pallas_call | solution.py:165
  1.7 2.3 %collective-permute-start.2 = (bf16[24,1024]{1,0:T(8,128)(2,1)S(1)}, bf16[24,1024]{1,0:T(8,128)(2,1)S(1)}, u32[]{:S(2)}, u32[]{:S(2)}) collective-permute-start(bf16[24,1024]{1,0:T(8,128)(2,1)S(1)} %get-tuple-element.15.own_ref), channel_id=1, source_target_pairs={{0,2},{1,16},{2,0},{3,18},{4,6},{5,20},{6,4},{7,22},{8,10},{9,24},... | collective-permute-start | bytes 147464 | tf_op jit(solution)/shard_map/ppermute | solution.py:312
  4.0 0.0 collective-permute-start.1
  4.1 1.9 %spread_first.1 = (bf16[12,1024,256]{2,1,0:T(8,128)(2,1)S(1)}, bf16[16,32,256]{2,1,0:T(8,128)(2,1)S(1)}) custom-call(bf16[192,128]{1,0:T(8,128)(2,1)S(1)} %get-tuple-element.11.l_ref.refs_0_, bf16[1024,128]{1,0:T(8,128)(2,1)S(1)} %get-tuple-element.12.f_ref), custom_call_target="tpu_custom_call" | custom-call | flops 1610612736 | bytes 49152 | tf_op jit(solution)/shard_map/spread_first/pallas_call | solution.py:190
  5.9 0.0 copy-start
  6.0 1.3 %collective-permute-start = (bf16[192,128]{1,0:T(8,128)(2,1)S(1)}, bf16[192,128]{1,0:T(8,128)(2,1)S(1)}, u32[]{:S(2)}, u32[]{:S(2)}) collective-permute-start(bf16[192,128]{1,0:T(8,128)(2,1)S(1)} %after.1), channel_id=1, source_target_pairs={{0,1},{1,0},{2,3},{3,2},{4,5},{5,4},{6,7},{7,6},{8,9},{9,8},{10,11... | collective-permute-start | bytes 147464 | tf_op jit(solution)/shard_map/ppermute | solution.py:315
  7.3 0.0 collective-permute-done.2.far_ref
  7.3 0.9 %collective-permute-done.1.near_ref = bf16[24,1024]{1,0:T(8,128)(2,1)S(1)} collective-permute-done((bf16[24,1024]{1,0:T(8,128)(2,1)S(1)}, bf16[24,1024]{1,0:T(8,128)(2,1)S(1)}, u32[]{:S(2)}, u32[]{:S(2)}) %collective-permute-start.1) | collective-permute-done | bytes 49184 | tf_op jit(solution)/shard_map/ppermute | solution.py:313
  8.2 2.1 %collective-permute-start.6 = (bf16[48,1024]{1,0:T(8,128)(2,1)S(1)}, bf16[48,1024]{1,0:T(8,128)(2,1)S(1)}, u32[]{:S(2)}, u32[]{:S(2)}) collective-permute-start(bf16[48,1024]{1,0:T(8,128)(2,1)S(1)} %arrange.1.refs_3_), channel_id=1, source_target_pairs={{0,12},{2,14},{4,8},{6,10},{8,4},{10,6},{12,0},{14,2},{16,28},{18,... | collective-permute-start | bytes 294920 | tf_op jit(solution)/shard_map/ppermute | solution.py:282
  10.3 0.4 %collective-permute-start.5 = (bf16[48,1024]{1,0:T(8,128)(2,1)S(1)}, bf16[48,1024]{1,0:T(8,128)(2,1)S(1)}, u32[]{:S(2)}, u32[]{:S(2)}) collective-permute-start(bf16[48,1024]{1,0:T(8,128)(2,1)S(1)} %arrange.1.refs_3_), channel_id=1, source_target_pairs={{0,8},{2,10},{4,12},{6,14},{8,0},{10,2},{12,4},{14,6},{16,24},{18,... | collective-permute-start | bytes 294920 | tf_op jit(solution)/shard_map/ppermute | solution.py:282
  10.7 0.2 collective-permute-start.4
  10.9 2.8 %collective-permute-start.3 = (bf16[48,1024]{1,0:T(8,128)(2,1)S(1)}, bf16[48,1024]{1,0:T(8,128)(2,1)S(1)}, u32[]{:S(2)}, u32[]{:S(2)}) collective-permute-start(bf16[48,1024]{1,0:T(8,128)(2,1)S(1)} %arrange.1.refs_3_), channel_id=1, source_target_pairs={{0,2},{2,0},{4,6},{6,4},{8,10},{10,8},{12,14},{14,12},{16,18},{18,... | collective-permute-start | bytes 294920 | tf_op jit(solution)/shard_map/ppermute | solution.py:282
  13.7 0.0 collective-permute-done.l_ref
  13.7 1.8 %spread_second.1.refs_2_.refs_3_ = bf16[12,1024,256]{2,1,0:T(8,128)(2,1)S(1)} custom-call(bf16[192,128]{1,0:T(8,128)(2,1)S(1)} %collective-permute-done.l_ref, bf16[16,32,256]{2,1,0:T(8,128)(2,1)S(1)} %get-tuple-element.14.refs_1_.pairs._), custom_call_target="tpu_custom_call" | custom-call | flops 1610612736 | bytes 49152 | tf_op jit(solution)/shard_map/spread_second/pallas_call | solution.py:200
  15.5 0.0 collective-permute-done.3.refs_4_
  15.5 0.0 copy-done
  15.5 2.2 %combine_some.2.refs_3_.refs_0_ = bf16[24,2,384,128]{3,2,1,0:T(8,128)(2,1)S(1)} custom-call(f32[1,128]{1,0:T(1,128)S(1)} %bitcast.7, bf16[12,1024,256]{2,1,0:T(8,128)(2,1)S(1)} %get-tuple-element.13.refs_1_.refs_2_, bf16[12,1024,256]{2,1,0:T(8,128)(2,1)S(1)} %spread_second.1.refs_2_.refs_3_, bf16[48,1024]{1,0:T(8,128)(2,1)S(1)} %arrange.1.refs_3_, ...), custom_call_target="tpu_custom_call" | custom-call | flops 1207959552 | tf_op jit(solution)/shard_map/combine_some/pallas_call | solution.py:256
  17.7 0.0 collective-permute-done.6.refs_2_
  17.7 0.0 collective-permute-done.5.refs_1_
  17.7 0.0 collective-permute-done.4.refs_0_
  17.7 0.2 collective-permute-start.7
  17.9 1.1 %combine_some.3.refs_0_ = bf16[24,2,384,128]{3,2,1,0:T(8,128)(2,1)S(1)} custom-call(bf16[24,2,384,128]{3,2,1,0:T(8,128)(2,1)S(1)} %combine_some.2.refs_3_.refs_0_, f32[1,128]{1,0:T(1,128)S(1)} %bitcast.8, bf16[12,1024,256]{2,1,0:T(8,128)(2,1)S(1)} %get-tuple-element.13.refs_1_.refs_2_, ...), custom_call_target="tpu_custom_call", output_to_operand_aliasing={{}: (0, {})} | custom-call | flops 905969664 | tf_op jit(solution)/shard_map/combine_some/pallas_call | solution.py:256
  19.0 0.4 %collective-permute-done.7.refs_4_ = bf16[144,1024]{1,0:T(8,128)(2,1)S(1)} collective-permute-done((bf16[144,1024]{1,0:T(8,128)(2,1)S(1)}, bf16[144,1024]{1,0:T(8,128)(2,1)S(1)}, u32[]{:S(2)}, u32[]{:S(2)}) %collective-permute-start.7) | collective-permute-done | bytes 294944 | tf_op jit(solution)/shard_map/ppermute | solution.py:282
  19.4 3.7 %combine_last.1 = (bf16[48,384,128]{2,1,0:T(8,128)(2,1)}, bf16[24,2,384,128]{3,2,1,0:T(8,128)(2,1)S(1)}) custom-call(bf16[24,2,384,128]{3,2,1,0:T(8,128)(2,1)S(1)} %combine_some.3.refs_0_, f32[1,128]{1,0:T(1,128)S(1)} %bitcast.9, bf16[12,1024,256]{2,1,0:T(8,128)(2,1)S(1)} %get-tuple-element.13.refs_1_.refs_2_, ...), custom_call_target="tpu_custom_call", output_to_operand_aliasing={{1}: (0, {})} | custom-call | flops 2717908992 | tf_op jit(solution)/shard_map/combine_last/pallas_call | solution.py:256
  (3 shorter events, 0.0 us)
Async XLA Ops:
  1.7 5.6 %collective-permute-start.2 = (bf16[24,1024]{1,0:T(8,128)(2,1)S(1)}, bf16[24,1024]{1,0:T(8,128)(2,1)S(1)}, u32[]{:S(2)}, u32[]{:S(2)}) collective-permute-start(bf16[24,1024]{1,0:T(8,128)(2,1)S(1)} %get-tuple-element.15.own_ref), channel_id=1, source_target_pairs={{0,2},{1,16},{2,0},{3,18},{4,6},{5,20},{6,4},{7,22},{8,10},{9,24},... | collective-permute-start | bytes 147464 | tf_op jit(solution)/shard_map/ppermute | solution.py:312
  4.0 4.1 %collective-permute-start.1 = (bf16[24,1024]{1,0:T(8,128)(2,1)S(1)}, bf16[24,1024]{1,0:T(8,128)(2,1)S(1)}, u32[]{:S(2)}, u32[]{:S(2)}) collective-permute-start(bf16[24,1024]{1,0:T(8,128)(2,1)S(1)} %get-tuple-element.15.own_ref), channel_id=1, source_target_pairs={{0,16},{1,0},{2,18},{3,2},{4,20},{5,4},{6,22},{7,6},{8,24},{9,8},{... | collective-permute-start | bytes 147464 | tf_op jit(solution)/shard_map/ppermute | solution.py:313
  5.9 9.6 %copy-start = (f32[128]{0:T(128)S(1)}, f32[128]{0:T(128)}, u32[]{:S(2)}) copy-start(f32[128]{0:T(128)} %param.17) | copy-start | bytes 1540
  6.0 7.7 %collective-permute-start = (bf16[192,128]{1,0:T(8,128)(2,1)S(1)}, bf16[192,128]{1,0:T(8,128)(2,1)S(1)}, u32[]{:S(2)}, u32[]{:S(2)}) collective-permute-start(bf16[192,128]{1,0:T(8,128)(2,1)S(1)} %after.1), channel_id=1, source_target_pairs={{0,1},{1,0},{2,3},{3,2},{4,5},{5,4},{6,7},{7,6},{8,9},{9,8},{10,11... | collective-permute-start | bytes 147464 | tf_op jit(solution)/shard_map/ppermute | solution.py:315
  8.2 9.5 %collective-permute-start.6 = (bf16[48,1024]{1,0:T(8,128)(2,1)S(1)}, bf16[48,1024]{1,0:T(8,128)(2,1)S(1)}, u32[]{:S(2)}, u32[]{:S(2)}) collective-permute-start(bf16[48,1024]{1,0:T(8,128)(2,1)S(1)} %arrange.1.refs_3_), channel_id=1, source_target_pairs={{0,12},{2,14},{4,8},{6,10},{8,4},{10,6},{12,0},{14,2},{16,28},{18,... | collective-permute-start | bytes 294920 | tf_op jit(solution)/shard_map/ppermute | solution.py:282
  10.3 7.4 %collective-permute-start.5 = (bf16[48,1024]{1,0:T(8,128)(2,1)S(1)}, bf16[48,1024]{1,0:T(8,128)(2,1)S(1)}, u32[]{:S(2)}, u32[]{:S(2)}) collective-permute-start(bf16[48,1024]{1,0:T(8,128)(2,1)S(1)} %arrange.1.refs_3_), channel_id=1, source_target_pairs={{0,8},{2,10},{4,12},{6,14},{8,0},{10,2},{12,4},{14,6},{16,24},{18,... | collective-permute-start | bytes 294920 | tf_op jit(solution)/shard_map/ppermute | solution.py:282
  10.7 7.0 %collective-permute-start.4 = (bf16[48,1024]{1,0:T(8,128)(2,1)S(1)}, bf16[48,1024]{1,0:T(8,128)(2,1)S(1)}, u32[]{:S(2)}, u32[]{:S(2)}) collective-permute-start(bf16[48,1024]{1,0:T(8,128)(2,1)S(1)} %arrange.1.refs_3_), channel_id=1, source_target_pairs={{0,4},{2,6},{4,0},{6,2},{8,12},{10,14},{12,8},{14,10},{16,20},{18,... | collective-permute-start | bytes 294920 | tf_op jit(solution)/shard_map/ppermute | solution.py:282
  10.9 4.6 %collective-permute-start.3 = (bf16[48,1024]{1,0:T(8,128)(2,1)S(1)}, bf16[48,1024]{1,0:T(8,128)(2,1)S(1)}, u32[]{:S(2)}, u32[]{:S(2)}) collective-permute-start(bf16[48,1024]{1,0:T(8,128)(2,1)S(1)} %arrange.1.refs_3_), channel_id=1, source_target_pairs={{0,2},{2,0},{4,6},{6,4},{8,10},{10,8},{12,14},{14,12},{16,18},{18,... | collective-permute-start | bytes 294920 | tf_op jit(solution)/shard_map/ppermute | solution.py:282
  17.7 1.6 %collective-permute-start.7 = (bf16[144,1024]{1,0:T(8,128)(2,1)S(1)}, bf16[144,1024]{1,0:T(8,128)(2,1)S(1)}, u32[]{:S(2)}, u32[]{:S(2)}) collective-permute-start(bf16[144,1024]{1,0:T(8,128)(2,1)S(1)} %join.1.refs_3_.refs_5_), channel_id=1, source_target_pairs={{0,2},{2,0},{4,6},{6,4},{8,10},{10,8},{12,14},{14,12},{16,18},{18,... | collective-permute-start | bytes 884744 | tf_op jit(solution)/shard_map/ppermute | solution.py:282

commit v8 on v7

--- a/solution.py
+++ b/solution.py
@@ -126,10 +126,12 @@
     for h, (left, count) in enumerate(zip(lefts, counts)):
         first = 2 * pairs * (jnp.bitwise_xor(lax.axis_index("col"), h) if len(lefts) > 1 else 0)
 
-        def step(n, carry, left=left, first=first, count=count, h=h):
+        source = pieces[0] if count * rows == pieces[0].shape[0] else right
+
+        def step(n, carry, left=left, first=first, count=count, h=h, source=source):
             for u in range(unroll):
                 p = n * unroll + u
-                update = jnp.dot(right[: count * rows, :], left[p], preferred_element_type=F32) * (1.0 / seqs) + shift
+                update = jnp.dot(source[: count * rows, :], left[p], preferred_element_type=F32) * (1.0 / seqs) + shift
                 for k, place in enumerate(places[:count]):
                     block = update[k * rows : (k + 1) * rows].astype(BF16)
                     stage[offset + h * pairs + p, 0, pl.ds(place, rows)] = block[:, :LANES]

time: 23.3 us -> 23.2 us (level)
  no operation moved by 1% of the time
where the time goes in v8:
time: 23.2 us; the launch traced here: 23.1 us
  Pallas kernels  12.4 us (53%)
  starting transfers between devices  9.32 us (40%)
  waiting for transfers between devices  1.27 us (5%)
    pallas_call x3, Pallas kernels, combine(): pl.pallas_call(functools.partial(combine_kernel, seqs, rows, len(pieces),...  6.96 us
    ppermute x5, starting transfers between devices, flip(): return lax.ppermute(value, 'row', [(r, r ^ bits) for r in range(16)])  5.65 us
    ppermute x1, starting transfers between devices, per_device(): lax.ppermute(right, both, linear(lambda r, c, i: (r ^ 1, c) if i else (r...  2.35 us
    pallas_call x1, Pallas kernels, spread(): pl.pallas_call(functools.partial(spread_first_kernel, seqs, width), out_s...  1.88 us
    pallas_call x1, Pallas kernels, spread(): pl.pallas_call(functools.partial(spread_second_kernel, seqs, width), out_...  1.79 us
    pallas_call x1, Pallas kernels, project(): pl.pallas_call(project_kernel, out_shape=(jax.ShapeDtypeStruct((here, seq...  1.69 us
    ppermute x1, starting transfers between devices, per_device(): lax.ppermute(after([left], keep(pairs))[0], 'col', [(0, 1), (1, 0)])  1.33 us
    ppermute x1, waiting for transfers between devices, per_device(): lax.ppermute(right, both, linear(lambda r, c, i: (r ^ 8, c) if i else (r,...  0.89 us
  transfers between devices with their start and end apart: 8, of which 2 were waited for; matrix products, arithmetic and copies ran while one was open for 0% of the time, Pallas kernels for 30%

profile of v8, /device:TPU:3, one launch (start us, length us, event | category | flops | bytes accessed | tf_op | source)
XLA Modules:
  0.0 23.1 jit_solution(8845181720324896298)
XLA Ops:
  0.0 1.7 %project.1 = (bf16[24,1024]{1,0:T(8,128)(2,1)S(1)}, bf16[192,128]{1,0:T(8,128)(2,1)S(1)}, bf16[1024,128]{1,0:T(8,128)(2,1)S(1)}) custom-call(bf16[32,24,256]{2,1,0:T(8,128)(2,1)} %refs_0_.1, f32[1,256]{1,0:T(1,128)} %bitcast.12, f32[1,256]{1,0:T(1,128)} %bitcast.13, bf16[32,256]{1,0:T(8,128)(2,1)} %bitcast.10, f32[1,32]{1,0:T(1,128)} %bitcast.14, ...), custom_call_target="tpu_custom_call" | custom-call | flops 100663296 | bytes 393216 | tf_op jit(solution)/shard_map/project/pallas_call | solution.py:167
  1.7 2.3 %collective-permute-start.2 = (bf16[24,1024]{1,0:T(8,128)(2,1)S(1)}, bf16[24,1024]{1,0:T(8,128)(2,1)S(1)}, u32[]{:S(2)}, u32[]{:S(2)}) collective-permute-start(bf16[24,1024]{1,0:T(8,128)(2,1)S(1)} %get-tuple-element.15.own_ref), channel_id=1, source_target_pairs={{0,2},{1,16},{2,0},{3,18},{4,6},{5,20},{6,4},{7,22},{8,10},{9,24},... | collective-permute-start | bytes 147464 | tf_op jit(solution)/shard_map/ppermute | solution.py:314
  4.0 0.0 collective-permute-start.1
  4.1 1.9 %spread_first.1 = (bf16[12,1024,256]{2,1,0:T(8,128)(2,1)S(1)}, bf16[16,32,256]{2,1,0:T(8,128)(2,1)S(1)}) custom-call(bf16[192,128]{1,0:T(8,128)(2,1)S(1)} %get-tuple-element.11.l_ref.refs_0_, bf16[1024,128]{1,0:T(8,128)(2,1)S(1)} %get-tuple-element.12.f_ref), custom_call_target="tpu_custom_call" | custom-call | flops 1610612736 | bytes 49152 | tf_op jit(solution)/shard_map/spread_first/pallas_call | solution.py:192
  5.9 0.0 copy-start
  6.0 1.3 %collective-permute-start = (bf16[192,128]{1,0:T(8,128)(2,1)S(1)}, bf16[192,128]{1,0:T(8,128)(2,1)S(1)}, u32[]{:S(2)}, u32[]{:S(2)}) collective-permute-start(bf16[192,128]{1,0:T(8,128)(2,1)S(1)} %after.1), channel_id=1, source_target_pairs={{0,1},{1,0},{2,3},{3,2},{4,5},{5,4},{6,7},{7,6},{8,9},{9,8},{10,11... | collective-permute-start | bytes 147464 | tf_op jit(solution)/shard_map/ppermute | solution.py:317
  7.3 0.0 collective-permute-done.2.far_ref
  7.3 0.9 %collective-permute-done.1.near_ref = bf16[24,1024]{1,0:T(8,128)(2,1)S(1)} collective-permute-done((bf16[24,1024]{1,0:T(8,128)(2,1)S(1)}, bf16[24,1024]{1,0:T(8,128)(2,1)S(1)}, u32[]{:S(2)}, u32[]{:S(2)}) %collective-permute-start.1) | collective-permute-done | bytes 49184 | tf_op jit(solution)/shard_map/ppermute | solution.py:315
  8.2 2.1 %collective-permute-start.6 = (bf16[48,1024]{1,0:T(8,128)(2,1)S(1)}, bf16[48,1024]{1,0:T(8,128)(2,1)S(1)}, u32[]{:S(2)}, u32[]{:S(2)}) collective-permute-start(bf16[48,1024]{1,0:T(8,128)(2,1)S(1)} %arrange.1.refs_3_), channel_id=1, source_target_pairs={{0,12},{2,14},{4,8},{6,10},{8,4},{10,6},{12,0},{14,2},{16,28},{18,... | collective-permute-start | bytes 294920 | tf_op jit(solution)/shard_map/ppermute | solution.py:284
  10.3 0.4 %collective-permute-start.5 = (bf16[48,1024]{1,0:T(8,128)(2,1)S(1)}, bf16[48,1024]{1,0:T(8,128)(2,1)S(1)}, u32[]{:S(2)}, u32[]{:S(2)}) collective-permute-start(bf16[48,1024]{1,0:T(8,128)(2,1)S(1)} %arrange.1.refs_3_), channel_id=1, source_target_pairs={{0,8},{2,10},{4,12},{6,14},{8,0},{10,2},{12,4},{14,6},{16,24},{18,... | collective-permute-start | bytes 294920 | tf_op jit(solution)/shard_map/ppermute | solution.py:284
  10.7 0.2 collective-permute-start.4
  10.9 2.8 %collective-permute-start.3 = (bf16[48,1024]{1,0:T(8,128)(2,1)S(1)}, bf16[48,1024]{1,0:T(8,128)(2,1)S(1)}, u32[]{:S(2)}, u32[]{:S(2)}) collective-permute-start(bf16[48,1024]{1,0:T(8,128)(2,1)S(1)} %arrange.1.refs_3_), channel_id=1, source_target_pairs={{0,2},{2,0},{4,6},{6,4},{8,10},{10,8},{12,14},{14,12},{16,18},{18,... | collective-permute-start | bytes 294920 | tf_op jit(solution)/shard_map/ppermute | solution.py:284
  13.7 0.0 collective-permute-done.l_ref
  13.7 1.8 %spread_second.1.refs_2_.refs_3_ = bf16[12,1024,256]{2,1,0:T(8,128)(2,1)S(1)} custom-call(bf16[192,128]{1,0:T(8,128)(2,1)S(1)} %collective-permute-done.l_ref, bf16[16,32,256]{2,1,0:T(8,128)(2,1)S(1)} %get-tuple-element.14.refs_1_.pairs._), custom_call_target="tpu_custom_call" | custom-call | flops 1610612736 | bytes 49152 | tf_op jit(solution)/shard_map/spread_second/pallas_call | solution.py:202
  15.5 0.0 collective-permute-done.3.refs_4_
  15.5 0.0 copy-done
  15.5 2.2 %combine_some.2.refs_3_.refs_0_ = bf16[24,2,384,128]{3,2,1,0:T(8,128)(2,1)S(1)} custom-call(f32[1,128]{1,0:T(1,128)S(1)} %bitcast.7, bf16[12,1024,256]{2,1,0:T(8,128)(2,1)S(1)} %get-tuple-element.13.refs_1_.refs_2_, bf16[12,1024,256]{2,1,0:T(8,128)(2,1)S(1)} %spread_second.1.refs_2_.refs_3_, bf16[48,1024]{1,0:T(8,128)(2,1)S(1)} %arrange.1.refs_3_, ...), custom_call_target="tpu_custom_call" | custom-call | flops 1207959552 | tf_op jit(solution)/shard_map/combine_some/pallas_call | solution.py:258
  17.7 0.0 collective-permute-done.6.refs_2_
  17.7 0.0 collective-permute-done.5.refs_1_
  17.7 0.0 collective-permute-done.4.refs_0_
  17.7 0.2 collective-permute-start.7
  17.9 1.1 %combine_some.3.refs_0_ = bf16[24,2,384,128]{3,2,1,0:T(8,128)(2,1)S(1)} custom-call(bf16[24,2,384,128]{3,2,1,0:T(8,128)(2,1)S(1)} %combine_some.2.refs_3_.refs_0_, f32[1,128]{1,0:T(1,128)S(1)} %bitcast.8, bf16[12,1024,256]{2,1,0:T(8,128)(2,1)S(1)} %get-tuple-element.13.refs_1_.refs_2_, ...), custom_call_target="tpu_custom_call", output_to_operand_aliasing={{}: (0, {})} | custom-call | flops 905969664 | tf_op jit(solution)/shard_map/combine_some/pallas_call | solution.py:258
  19.0 0.4 %collective-permute-done.7.refs_4_ = bf16[144,1024]{1,0:T(8,128)(2,1)S(1)} collective-permute-done((bf16[144,1024]{1,0:T(8,128)(2,1)S(1)}, bf16[144,1024]{1,0:T(8,128)(2,1)S(1)}, u32[]{:S(2)}, u32[]{:S(2)}) %collective-permute-start.7) | collective-permute-done | bytes 294944 | tf_op jit(solution)/shard_map/ppermute | solution.py:284
  19.4 3.7 %combine_last.1 = (bf16[48,384,128]{2,1,0:T(8,128)(2,1)}, bf16[24,2,384,128]{3,2,1,0:T(8,128)(2,1)S(1)}) custom-call(bf16[24,2,384,128]{3,2,1,0:T(8,128)(2,1)S(1)} %combine_some.3.refs_0_, f32[1,128]{1,0:T(1,128)S(1)} %bitcast.9, bf16[12,1024,256]{2,1,0:T(8,128)(2,1)S(1)} %get-tuple-element.13.refs_1_.refs_2_, ...), custom_call_target="tpu_custom_call", output_to_operand_aliasing={{1}: (0, {})} | custom-call | flops 2717908992 | tf_op jit(solution)/shard_map/combine_last/pallas_call | solution.py:258
  (3 shorter events, 0.0 us)
Async XLA Ops:
  1.7 5.6 %collective-permute-start.2 = (bf16[24,1024]{1,0:T(8,128)(2,1)S(1)}, bf16[24,1024]{1,0:T(8,128)(2,1)S(1)}, u32[]{:S(2)}, u32[]{:S(2)}) collective-permute-start(bf16[24,1024]{1,0:T(8,128)(2,1)S(1)} %get-tuple-element.15.own_ref), channel_id=1, source_target_pairs={{0,2},{1,16},{2,0},{3,18},{4,6},{5,20},{6,4},{7,22},{8,10},{9,24},... | collective-permute-start | bytes 147464 | tf_op jit(solution)/shard_map/ppermute | solution.py:314
  4.0 4.1 %collective-permute-start.1 = (bf16[24,1024]{1,0:T(8,128)(2,1)S(1)}, bf16[24,1024]{1,0:T(8,128)(2,1)S(1)}, u32[]{:S(2)}, u32[]{:S(2)}) collective-permute-start(bf16[24,1024]{1,0:T(8,128)(2,1)S(1)} %get-tuple-element.15.own_ref), channel_id=1, source_target_pairs={{0,16},{1,0},{2,18},{3,2},{4,20},{5,4},{6,22},{7,6},{8,24},{9,8},{... | collective-permute-start | bytes 147464 | tf_op jit(solution)/shard_map/ppermute | solution.py:315
  5.9 9.6 %copy-start = (f32[128]{0:T(128)S(1)}, f32[128]{0:T(128)}, u32[]{:S(2)}) copy-start(f32[128]{0:T(128)} %param.17) | copy-start | bytes 1540
  6.0 7.7 %collective-permute-start = (bf16[192,128]{1,0:T(8,128)(2,1)S(1)}, bf16[192,128]{1,0:T(8,128)(2,1)S(1)}, u32[]{:S(2)}, u32[]{:S(2)}) collective-permute-start(bf16[192,128]{1,0:T(8,128)(2,1)S(1)} %after.1), channel_id=1, source_target_pairs={{0,1},{1,0},{2,3},{3,2},{4,5},{5,4},{6,7},{7,6},{8,9},{9,8},{10,11... | collective-permute-start | bytes 147464 | tf_op jit(solution)/shard_map/ppermute | solution.py:317
  8.2 9.5 %collective-permute-start.6 = (bf16[48,1024]{1,0:T(8,128)(2,1)S(1)}, bf16[48,1024]{1,0:T(8,128)(2,1)S(1)}, u32[]{:S(2)}, u32[]{:S(2)}) collective-permute-start(bf16[48,1024]{1,0:T(8,128)(2,1)S(1)} %arrange.1.refs_3_), channel_id=1, source_target_pairs={{0,12},{2,14},{4,8},{6,10},{8,4},{10,6},{12,0},{14,2},{16,28},{18,... | collective-permute-start | bytes 294920 | tf_op jit(solution)/shard_map/ppermute | solution.py:284
  10.3 7.4 %collective-permute-start.5 = (bf16[48,1024]{1,0:T(8,128)(2,1)S(1)}, bf16[48,1024]{1,0:T(8,128)(2,1)S(1)}, u32[]{:S(2)}, u32[]{:S(2)}) collective-permute-start(bf16[48,1024]{1,0:T(8,128)(2,1)S(1)} %arrange.1.refs_3_), channel_id=1, source_target_pairs={{0,8},{2,10},{4,12},{6,14},{8,0},{10,2},{12,4},{14,6},{16,24},{18,... | collective-permute-start | bytes 294920 | tf_op jit(solution)/shard_map/ppermute | solution.py:284
  10.7 7.0 %collective-permute-start.4 = (bf16[48,1024]{1,0:T(8,128)(2,1)S(1)}, bf16[48,1024]{1,0:T(8,128)(2,1)S(1)}, u32[]{:S(2)}, u32[]{:S(2)}) collective-permute-start(bf16[48,1024]{1,0:T(8,128)(2,1)S(1)} %arrange.1.refs_3_), channel_id=1, source_target_pairs={{0,4},{2,6},{4,0},{6,2},{8,12},{10,14},{12,8},{14,10},{16,20},{18,... | collective-permute-start | bytes 294920 | tf_op jit(solution)/shard_map/ppermute | solution.py:284
  10.9 4.6 %collective-permute-start.3 = (bf16[48,1024]{1,0:T(8,128)(2,1)S(1)}, bf16[48,1024]{1,0:T(8,128)(2,1)S(1)}, u32[]{:S(2)}, u32[]{:S(2)}) collective-permute-start(bf16[48,1024]{1,0:T(8,128)(2,1)S(1)} %arrange.1.refs_3_), channel_id=1, source_target_pairs={{0,2},{2,0},{4,6},{6,4},{8,10},{10,8},{12,14},{14,12},{16,18},{18,... | collective-permute-start | bytes 294920 | tf_op jit(solution)/shard_map/ppermute | solution.py:284
  17.7 1.6 %collective-permute-start.7 = (bf16[144,1024]{1,0:T(8,128)(2,1)S(1)}, bf16[144,1024]{1,0:T(8,128)(2,1)S(1)}, u32[]{:S(2)}, u32[]{:S(2)}) collective-permute-start(bf16[144,1024]{1,0:T(8,128)(2,1)S(1)} %join.1.refs_3_.refs_5_), channel_id=1, source_target_pairs={{0,2},{2,0},{4,6},{6,4},{8,10},{10,8},{12,14},{14,12},{16,18},{18,... | collective-permute-start | bytes 884744 | tf_op jit(solution)/shard_map/ppermute | solution.py:284
